TPU v7x, 128 devices: a whole 4x4x4 slice. The times are simulated.
128 devices in a mesh: win: 32 (over x, y, z_lo), seq: 4 (over z_hi, core).
Axes of the slice: x: 4, y: 4, z: 4 (z_hi: 2, z_lo: 2; z = z_hi * 2 + z_lo), core: 2. Of those that a mesh axis runs over, the one named last changes fastest.
Arguments:
- tokens: bfloat16 [2, 32, 448, 768], P(None, 'win', 'seq'), may hold values from -6 to 6
- encoder_states: bfloat16 [2, 32, 1500, 768], P(None, 'win', 'seq'), may hold values from -6 to 6
- segments: int32 [2, 32, 448], P(None, 'win'), may hold values from 0 to 3, as said below
- frame_clips: int32 [2, 32, 1500], P(None, 'win'), may hold values from 0 to 3, as said below
- out_grad: bfloat16 [2, 32, 448, 768], P(None, 'win', 'seq'), may hold values from -6 to 6
- self_gain: bfloat16 [768], P(('win', 'seq')), may hold values from 0.5 to 1.5
- self_shift: bfloat16 [768], P(('win', 'seq')), may hold values from -3 to 3
- self_query: bfloat16 [768, 768], P(('win', 'seq')), may hold values from -0.21875 to 0.21875
- self_query_bias: bfloat16 [768], P(('win', 'seq')), may hold values from -3 to 3
- self_key: bfloat16 [768, 768], P(('win', 'seq')), may hold values from -0.21875 to 0.21875
- self_value: bfloat16 [768, 768], P(('win', 'seq')), may hold values from -0.21875 to 0.21875
- self_value_bias: bfloat16 [768], P(('win', 'seq')), may hold values from -3 to 3
- self_output: bfloat16 [768, 768], P(('win', 'seq')), may hold values from -1.25 to 1.25
- self_output_bias: bfloat16 [768], P(('win', 'seq')), may hold values from -3 to 3
- cross_gain: bfloat16 [768], P(('win', 'seq')), may hold values from 0.5 to 1.5
- cross_shift: bfloat16 [768], P(('win', 'seq')), may hold values from -3 to 3
- cross_query: bfloat16 [768, 768], P(('win', 'seq')), may hold values from -0.21875 to 0.21875
- cross_query_bias: bfloat16 [768], P(('win', 'seq')), may hold values from -3 to 3
- cross_key: bfloat16 [768, 768], P(('win', 'seq')), may hold values from -0.21875 to 0.21875
- cross_value: bfloat16 [768, 768], P(('win', 'seq')), may hold values from -0.21875 to 0.21875
- cross_value_bias: bfloat16 [768], P(('win', 'seq')), may hold values from -3 to 3
- cross_output: bfloat16 [768, 768], P(('win', 'seq')), may hold values from -1.25 to 1.25
- cross_output_bias: bfloat16 [768], P(('win', 'seq')), may hold values from -3 to 3
- final_gain: bfloat16 [768], P(('win', 'seq')), may hold values from 0.5 to 1.5
- final_shift: bfloat16 [768], P(('win', 'seq')), may hold values from -3 to 3
- hidden_in: bfloat16 [768, 3072], P(('win', 'seq')), may hold values from -0.21875 to 0.21875
- hidden_in_bias: bfloat16 [3072], P(('win', 'seq')), may hold values from -3 to 3
- hidden_out: bfloat16 [3072, 768], P(('win', 'seq')), may hold values from -0.109375 to 0.109375
- hidden_out_bias: bfloat16 [768], P(('win', 'seq')), may hold values from -3 to 3
Outputs:
- block_output: bfloat16 [2, 32, 448, 768], P(None, 'win', 'seq')
- input_grad: float32 [2, 32, 448, 768], P(None, 'win', 'seq')
- encoder_grad: float32 [2, 32, 1500, 768], P(None, 'win', 'seq')
- grad_self_gain: float32 [768], P(('win', 'seq'))
- grad_self_shift: float32 [768], P(('win', 'seq'))
- grad_self_query: float32 [768, 768], P(('win', 'seq'))
- grad_self_query_bias: float32 [768], P(('win', 'seq'))
- grad_self_key: float32 [768, 768], P(('win', 'seq'))
- grad_self_value: float32 [768, 768], P(('win', 'seq'))
- grad_self_value_bias: float32 [768], P(('win', 'seq'))
- grad_self_output: float32 [768, 768], P(('win', 'seq'))
- grad_self_output_bias: float32 [768], P(('win', 'seq'))
- grad_cross_gain: float32 [768], P(('win', 'seq'))
- grad_cross_shift: float32 [768], P(('win', 'seq'))
- grad_cross_query: float32 [768, 768], P(('win', 'seq'))
- grad_cross_query_bias: float32 [768], P(('win', 'seq'))
- grad_cross_key: float32 [768, 768], P(('win', 'seq'))
- grad_cross_value: float32 [768, 768], P(('win', 'seq'))
- grad_cross_value_bias: float32 [768], P(('win', 'seq'))
- grad_cross_output: float32 [768, 768], P(('win', 'seq'))
- grad_cross_output_bias: float32 [768], P(('win', 'seq'))
- grad_final_gain: float32 [768], P(('win', 'seq'))
- grad_final_shift: float32 [768], P(('win', 'seq'))
- grad_hidden_in: float32 [768, 3072], P(('win', 'seq'))
- grad_hidden_in_bias: float32 [3072], P(('win', 'seq'))
- grad_hidden_out: float32 [3072, 768], P(('win', 'seq'))
- grad_hidden_out_bias: float32 [768], P(('win', 'seq'))
Inputs may be any that keep to these rules, and one draw needn't show every extreme that they name: `segments`: for each window, the clip numbers of its 448 tokens never fall along the window, and each of the 4 clips has at least one token. `frame_clips`: for each window, the clip numbers of its 1500 frames never fall, use the same numbering as that window's segments, and each of the 4 clips has at least one frame.
All inputs are finite; a program needn't handle non-finite values.
Results may differ from a plain program's by a relative error of at most 0.025.
Values may be sent and summed in bfloat16 or wider, within the bound.
A program may use at most 256 MiB of HBM per device.

v0:
```python
from functools import partial

import jax
import jax.numpy as jnp
from jax import lax
from jax.sharding import PartitionSpec as P

HEADS = 12
HEAD_DIM = 64


EPS = 1e-05
SCALE = 0.125
BLOCKED = -1e30
HIGH = lax.Precision.HIGHEST


def layer_norm(values, gain, shift):
    mean = jnp.mean(values, -1, keepdims=True)
    centered = values - mean
    spread = jnp.mean(centered * centered, -1, keepdims=True)
    return centered * lax.rsqrt(spread + EPS) * gain + shift


def exact_gelu(values):
    return jax.nn.gelu(values, approximate=False)


def project(left, weight):
    return jnp.einsum("wcd,df->wcf", left, weight, preferred_element_type=jnp.float32)


def project_back(grad, weight):
    return jnp.einsum("wcf,df->wcd", grad, weight, preferred_element_type=jnp.float32)


def weight_grad(left, grad):
    return jnp.einsum("wcd,wcf->df", left, grad, preferred_element_type=jnp.float32)


def project_back_wide(grad, weight):
    return jnp.einsum(
        "wcf,df->wcd",
        grad,
        weight.astype(jnp.float32),
        precision=HIGH,
        preferred_element_type=jnp.float32,
    )


def weight_grad_wide(left, grad):
    return jnp.einsum(
        "wcd,wcf->df",
        left.astype(jnp.float32),
        grad,
        precision=HIGH,
        preferred_element_type=jnp.float32,
    )


def bias_grad(grad):
    return jnp.sum(grad.astype(jnp.float32), (0, 1))


def split_heads(values):
    return values.reshape(values.shape[0], values.shape[1], HEADS, HEAD_DIM)


def scores_of(queries, keys_all, allowed):
    raw = (
        jnp.einsum(
            "wqhe,wkhe->whqk",
            split_heads(queries),
            split_heads(keys_all),
            preferred_element_type=jnp.float32,
        )
        * SCALE
    )
    return jnp.where(allowed[:, None], raw, BLOCKED)


def attend_forward(queries, keys_all, values_all, allowed):
    scores = scores_of(queries, keys_all, allowed)
    top = jnp.max(scores, -1, keepdims=True)
    shifted = jnp.exp(scores - top)
    total = jnp.sum(shifted, -1, keepdims=True)
    probs = (shifted / total).astype(jnp.bfloat16)
    mixed = jnp.einsum(
        "whqk,wkhe->wqhe", probs, split_heads(values_all), preferred_element_type=jnp.float32
    )
    return (mixed.reshape(queries.shape).astype(jnp.bfloat16), top + jnp.log(total))


def attend_backward(queries, keys_all, values_all, allowed, log_total, grad_mixed):
    probs = jnp.exp(scores_of(queries, keys_all, allowed) - log_total)
    grad_heads = split_heads(grad_mixed)
    grad_probs = jnp.einsum(
        "wqhe,wkhe->whqk", grad_heads, split_heads(values_all), preferred_element_type=jnp.float32
    )
    grad_scores = probs * (grad_probs - jnp.sum(probs * grad_probs, -1, keepdims=True))
    grad_scores = grad_scores.astype(jnp.bfloat16)
    grad_queries = (
        jnp.einsum(
            "whqk,wkhe->wqhe",
            grad_scores,
            split_heads(keys_all),
            preferred_element_type=jnp.float32,
        )
        * SCALE
    )
    grad_keys = (
        jnp.einsum(
            "whqk,wqhe->wkhe", grad_scores, split_heads(queries), preferred_element_type=jnp.float32
        )
        * SCALE
    )
    grad_values = jnp.einsum(
        "whqk,wqhe->wkhe",
        probs.astype(jnp.bfloat16),
        grad_heads,
        preferred_element_type=jnp.float32,
    )
    return (
        grad_queries.reshape(queries.shape).astype(jnp.bfloat16),
        grad_keys.reshape(keys_all.shape),
        grad_values.reshape(values_all.shape),
    )


def summed_cross_back(key_terms, value_terms, encoder, cross_key, cross_value):
    grad_keys, grad_values = (
        lax.psum_scatter(
            key_terms.astype(jnp.bfloat16), "seq", scatter_dimension=1, tiled=True
        ).astype(jnp.float32),
        lax.psum_scatter(
            value_terms.astype(jnp.bfloat16), "seq", scatter_dimension=1, tiled=True
        ).astype(jnp.float32),
    )
    grad_encoder = project_back_wide(grad_keys, cross_key) + project_back_wide(
        grad_values, cross_value
    )
    return (
        weight_grad_wide(encoder, grad_keys),
        weight_grad_wide(encoder, grad_values),
        jnp.sum(grad_values, (0, 1)),
        grad_encoder,
    )


def layer_pass(weights, inputs, encoder, segment_ids, clip_ids, out_grad, place):
    (
        self_gain,
        self_shift,
        self_query,
        self_query_bias,
        self_key,
        self_value,
        self_value_bias,
        self_output,
        self_output_bias,
        cross_gain,
        cross_shift,
        cross_query,
        cross_query_bias,
        cross_key,
        cross_value,
        cross_value_bias,
        cross_output,
        cross_output_bias,
        final_gain,
        final_shift,
        hidden_in,
        hidden_in_bias,
        hidden_out,
        hidden_out_bias,
    ) = weights
    as_float = partial(jnp.asarray, dtype=jnp.float32)
    span = inputs.shape[1]
    length = segment_ids.shape[1]
    own_ids = lax.dynamic_slice_in_dim(segment_ids, place * span, span, 1)
    query_places = place * span + jnp.arange(span, dtype=jnp.int32)
    key_places = jnp.arange(length, dtype=jnp.int32)
    self_allowed = (own_ids[:, :, None] == segment_ids[:, None, :]) & (
        key_places[None, None, :] <= query_places[None, :, None]
    )
    cross_allowed = own_ids[:, :, None] == clip_ids[:, None, :]
    inputs_wide = inputs.astype(jnp.float32)
    first_norm, first_back = jax.vjp(
        layer_norm, inputs_wide, as_float(self_gain), as_float(self_shift)
    )
    first_norm = first_norm.astype(jnp.bfloat16)
    queries = (project(first_norm, self_query) + as_float(self_query_bias)).astype(jnp.bfloat16)
    keys_own = project(first_norm, self_key).astype(jnp.bfloat16)
    values_own = (project(first_norm, self_value) + as_float(self_value_bias)).astype(jnp.bfloat16)
    keys_self, values_self = (
        lax.all_gather(keys_own, "seq", axis=1, tiled=True),
        lax.all_gather(values_own, "seq", axis=1, tiled=True),
    )
    self_mixed, self_total = attend_forward(queries, keys_self, values_self, self_allowed)
    after_self = inputs_wide + project(self_mixed, self_output) + as_float(self_output_bias)
    second_norm, second_back = jax.vjp(
        layer_norm, after_self, as_float(cross_gain), as_float(cross_shift)
    )
    second_norm = second_norm.astype(jnp.bfloat16)
    cross_queries = (project(second_norm, cross_query) + as_float(cross_query_bias)).astype(
        jnp.bfloat16
    )
    keys_local = project(encoder, cross_key).astype(jnp.bfloat16)
    values_local = (project(encoder, cross_value) + as_float(cross_value_bias)).astype(jnp.bfloat16)
    cross_keys, cross_values = (
        lax.all_gather(keys_local, "seq", axis=1, tiled=True),
        lax.all_gather(values_local, "seq", axis=1, tiled=True),
    )
    cross_mixed, cross_total = attend_forward(
        cross_queries, cross_keys, cross_values, cross_allowed
    )
    after_cross = after_self + project(cross_mixed, cross_output) + as_float(cross_output_bias)
    third_norm, third_back = jax.vjp(
        layer_norm, after_cross, as_float(final_gain), as_float(final_shift)
    )
    third_norm = third_norm.astype(jnp.bfloat16)
    hidden_pre = project(third_norm, hidden_in) + as_float(hidden_in_bias)
    hidden_act, gelu_back = jax.vjp(exact_gelu, hidden_pre)
    hidden_act = hidden_act.astype(jnp.bfloat16)
    result = after_cross + project(hidden_act, hidden_out) + as_float(hidden_out_bias)
    grad_result = out_grad.astype(jnp.float32)
    grad_hidden_out = weight_grad(hidden_act, out_grad)
    grad_hidden_out_bias = bias_grad(out_grad)
    grad_hidden_act = project_back(out_grad, hidden_out)
    grad_hidden_pre = gelu_back(grad_hidden_act)[0].astype(jnp.bfloat16)
    grad_hidden_in = weight_grad(third_norm, grad_hidden_pre)
    grad_hidden_in_bias = bias_grad(grad_hidden_pre)
    back_third, grad_final_gain, grad_final_shift = third_back(
        project_back(grad_hidden_pre, hidden_in)
    )
    grad_cross_stream = grad_result + back_third
    grad_cross_branch = grad_cross_stream.astype(jnp.bfloat16)
    grad_cross_output = weight_grad(cross_mixed, grad_cross_branch)
    grad_cross_output_bias = bias_grad(grad_cross_branch)
    grad_cross_mixed = project_back(grad_cross_branch, cross_output).astype(jnp.bfloat16)
    grad_cross_queries, cross_key_terms, cross_value_terms = attend_backward(
        cross_queries, cross_keys, cross_values, cross_allowed, cross_total, grad_cross_mixed
    )
    grad_cross_key, grad_cross_value, grad_cross_value_bias, grad_encoder = summed_cross_back(
        cross_key_terms, cross_value_terms, encoder, cross_key, cross_value
    )
    grad_cross_query = weight_grad(second_norm, grad_cross_queries)
    grad_cross_query_bias = bias_grad(grad_cross_queries)
    back_second, grad_cross_gain, grad_cross_shift = second_back(
        project_back(grad_cross_queries, cross_query)
    )
    grad_self_stream = grad_cross_stream + back_second
    grad_self_branch = grad_self_stream.astype(jnp.bfloat16)
    grad_self_output = weight_grad(self_mixed, grad_self_branch)
    grad_self_output_bias = bias_grad(grad_self_branch)
    grad_self_mixed = project_back(grad_self_branch, self_output).astype(jnp.bfloat16)
    grad_queries, self_key_terms, self_value_terms = attend_backward(
        queries, keys_self, values_self, self_allowed, self_total, grad_self_mixed
    )
    grad_keys_self, grad_values_self = (
        lax.psum_scatter(
            self_key_terms.astype(jnp.bfloat16), "seq", scatter_dimension=1, tiled=True
        ).astype(jnp.float32),
        lax.psum_scatter(
            self_value_terms.astype(jnp.bfloat16), "seq", scatter_dimension=1, tiled=True
        ).astype(jnp.float32),
    )
    grad_keys_self = grad_keys_self.astype(jnp.bfloat16)
    grad_values_self = grad_values_self.astype(jnp.bfloat16)
    grad_self_query = weight_grad(first_norm, grad_queries)
    grad_self_query_bias = bias_grad(grad_queries)
    grad_self_key = weight_grad(first_norm, grad_keys_self)
    grad_self_value = weight_grad(first_norm, grad_values_self)
    grad_self_value_bias = bias_grad(grad_values_self)
    grad_first = (
        project_back(grad_queries, self_query)
        + project_back(grad_keys_self, self_key)
        + project_back(grad_values_self, self_value)
    )
    back_first, grad_self_gain, grad_self_shift = first_back(grad_first)
    grad_inputs = grad_self_stream + back_first
    grads = (
        grad_self_gain,
        grad_self_shift,
        grad_self_query,
        grad_self_query_bias,
        grad_self_key,
        grad_self_value,
        grad_self_value_bias,
        grad_self_output,
        grad_self_output_bias,
        grad_cross_gain,
        grad_cross_shift,
        grad_cross_query,
        grad_cross_query_bias,
        grad_cross_key,
        grad_cross_value,
        grad_cross_value_bias,
        grad_cross_output,
        grad_cross_output_bias,
        grad_final_gain,
        grad_final_shift,
        grad_hidden_in,
        grad_hidden_in_bias,
        grad_hidden_out,
        grad_hidden_out_bias,
    )
    return (result.astype(jnp.bfloat16), grad_inputs, grad_encoder, grads)


def per_device(
    tokens,
    encoder_states,
    segments,
    frame_clips,
    out_grad,
    self_gain,
    self_shift,
    self_query,
    self_query_bias,
    self_key,
    self_value,
    self_value_bias,
    self_output,
    self_output_bias,
    cross_gain,
    cross_shift,
    cross_query,
    cross_query_bias,
    cross_key,
    cross_value,
    cross_value_bias,
    cross_output,
    cross_output_bias,
    final_gain,
    final_shift,
    hidden_in,
    hidden_in_bias,
    hidden_out,
    hidden_out_bias,
):
    place = lax.axis_index("seq")
    micro_count = tokens.shape[0]
    outputs, input_grads, encoder_grads = ([], [], [])
    summed = None
    for micro_step in range(micro_count):
        fetched = (
            lax.all_gather(self_gain, ("win", "seq"), axis=0, tiled=True),
            lax.all_gather(self_shift, ("win", "seq"), axis=0, tiled=True),
            lax.all_gather(self_query, ("win", "seq"), axis=0, tiled=True),
            lax.all_gather(self_query_bias, ("win", "seq"), axis=0, tiled=True),
            lax.all_gather(self_key, ("win", "seq"), axis=0, tiled=True),
            lax.all_gather(self_value, ("win", "seq"), axis=0, tiled=True),
            lax.all_gather(self_value_bias, ("win", "seq"), axis=0, tiled=True),
            lax.all_gather(self_output, ("win", "seq"), axis=0, tiled=True),
            lax.all_gather(self_output_bias, ("win", "seq"), axis=0, tiled=True),
            lax.all_gather(cross_gain, ("win", "seq"), axis=0, tiled=True),
            lax.all_gather(cross_shift, ("win", "seq"), axis=0, tiled=True),
            lax.all_gather(cross_query, ("win", "seq"), axis=0, tiled=True),
            lax.all_gather(cross_query_bias, ("win", "seq"), axis=0, tiled=True),
            lax.all_gather(cross_key, ("win", "seq"), axis=0, tiled=True),
            lax.all_gather(cross_value, ("win", "seq"), axis=0, tiled=True),
            lax.all_gather(cross_value_bias, ("win", "seq"), axis=0, tiled=True),
            lax.all_gather(cross_output, ("win", "seq"), axis=0, tiled=True),
            lax.all_gather(cross_output_bias, ("win", "seq"), axis=0, tiled=True),
            lax.all_gather(final_gain, ("win", "seq"), axis=0, tiled=True),
            lax.all_gather(final_shift, ("win", "seq"), axis=0, tiled=True),
            lax.all_gather(hidden_in, ("win", "seq"), axis=0, tiled=True),
            lax.all_gather(hidden_in_bias, ("win", "seq"), axis=0, tiled=True),
            lax.all_gather(hidden_out, ("win", "seq"), axis=0, tiled=True),
            lax.all_gather(hidden_out_bias, ("win", "seq"), axis=0, tiled=True),
        )
        result, grad_inputs, grad_encoder, grads = layer_pass(
            fetched,
            tokens[micro_step],
            encoder_states[micro_step],
            segments[micro_step],
            frame_clips[micro_step],
            out_grad[micro_step],
            place,
        )
        outputs.append(result)
        input_grads.append(grad_inputs)
        encoder_grads.append(grad_encoder)
        shares = (
            lax.psum_scatter(grads[0], ("win", "seq"), scatter_dimension=0, tiled=True),
            lax.psum_scatter(grads[1], ("win", "seq"), scatter_dimension=0, tiled=True),
            lax.psum_scatter(grads[2], ("win", "seq"), scatter_dimension=0, tiled=True),
            lax.psum_scatter(grads[3], ("win", "seq"), scatter_dimension=0, tiled=True),
            lax.psum_scatter(grads[4], ("win", "seq"), scatter_dimension=0, tiled=True),
            lax.psum_scatter(grads[5], ("win", "seq"), scatter_dimension=0, tiled=True),
            lax.psum_scatter(grads[6], ("win", "seq"), scatter_dimension=0, tiled=True),
            lax.psum_scatter(grads[7], ("win", "seq"), scatter_dimension=0, tiled=True),
            lax.psum_scatter(grads[8], ("win", "seq"), scatter_dimension=0, tiled=True),
            lax.psum_scatter(grads[9], ("win", "seq"), scatter_dimension=0, tiled=True),
            lax.psum_scatter(grads[10], ("win", "seq"), scatter_dimension=0, tiled=True),
            lax.psum_scatter(grads[11], ("win", "seq"), scatter_dimension=0, tiled=True),
            lax.psum_scatter(grads[12], ("win", "seq"), scatter_dimension=0, tiled=True),
            lax.psum_scatter(grads[13], ("win", "seq"), scatter_dimension=0, tiled=True),
            lax.psum_scatter(grads[14], ("win", "seq"), scatter_dimension=0, tiled=True),
            lax.psum_scatter(grads[15], ("win", "seq"), scatter_dimension=0, tiled=True),
            lax.psum_scatter(grads[16], ("win", "seq"), scatter_dimension=0, tiled=True),
            lax.psum_scatter(grads[17], ("win", "seq"), scatter_dimension=0, tiled=True),
            lax.psum_scatter(grads[18], ("win", "seq"), scatter_dimension=0, tiled=True),
            lax.psum_scatter(grads[19], ("win", "seq"), scatter_dimension=0, tiled=True),
            lax.psum_scatter(grads[20], ("win", "seq"), scatter_dimension=0, tiled=True),
            lax.psum_scatter(grads[21], ("win", "seq"), scatter_dimension=0, tiled=True),
            lax.psum_scatter(grads[22], ("win", "seq"), scatter_dimension=0, tiled=True),
            lax.psum_scatter(grads[23], ("win", "seq"), scatter_dimension=0, tiled=True),
        )
        if summed is None:
            summed = shares
        else:
            summed = tuple((first + second for first, second in zip(summed, shares)))
    return (
        jnp.stack(outputs),
        jnp.stack(input_grads),
        jnp.stack(encoder_grads),
        summed[0],
        summed[1],
        summed[2],
        summed[3],
        summed[4],
        summed[5],
        summed[6],
        summed[7],
        summed[8],
        summed[9],
        summed[10],
        summed[11],
        summed[12],
        summed[13],
        summed[14],
        summed[15],
        summed[16],
        summed[17],
        summed[18],
        summed[19],
        summed[20],
        summed[21],
        summed[22],
        summed[23],
    )


def solution(mesh):
    in_specs = (
        P(None, "win", "seq", None),
        P(None, "win", "seq", None),
        P(None, "win", None),
        P(None, "win", None),
        P(None, "win", "seq", None),
        P(("win", "seq")),
        P(("win", "seq")),
        P(("win", "seq"), None),
        P(("win", "seq")),
        P(("win", "seq"), None),
        P(("win", "seq"), None),
        P(("win", "seq")),
        P(("win", "seq"), None),
        P(("win", "seq")),
        P(("win", "seq")),
        P(("win", "seq")),
        P(("win", "seq"), None),
        P(("win", "seq")),
        P(("win", "seq"), None),
        P(("win", "seq"), None),
        P(("win", "seq")),
        P(("win", "seq"), None),
        P(("win", "seq")),
        P(("win", "seq")),
        P(("win", "seq")),
        P(("win", "seq"), None),
        P(("win", "seq")),
        P(("win", "seq"), None),
        P(("win", "seq")),
    )
    out_specs = (
        P(None, "win", "seq", None),
        P(None, "win", "seq", None),
        P(None, "win", "seq", None),
        P(("win", "seq")),
        P(("win", "seq")),
        P(("win", "seq"), None),
        P(("win", "seq")),
        P(("win", "seq"), None),
        P(("win", "seq"), None),
        P(("win", "seq")),
        P(("win", "seq"), None),
        P(("win", "seq")),
        P(("win", "seq")),
        P(("win", "seq")),
        P(("win", "seq"), None),
        P(("win", "seq")),
        P(("win", "seq"), None),
        P(("win", "seq"), None),
        P(("win", "seq")),
        P(("win", "seq"), None),
        P(("win", "seq")),
        P(("win", "seq")),
        P(("win", "seq")),
        P(("win", "seq"), None),
        P(("win", "seq")),
        P(("win", "seq"), None),
        P(("win", "seq")),
    )
    return jax.shard_map(
        per_device, mesh=mesh, in_specs=in_specs, out_specs=out_specs, check_vma=False
    )
```

profile of v0, /device:TPU:1, one launch (start us, length us, event | category | flops | bytes accessed | tf_op | source)
XLA Modules:
  0.0 3806.0 jit_solution(17661369246040802200)
XLA Ops:
  21.4 69.4 %all-reduce.50 = (bf16[768]{0:T(1024)(128)(2,1)S(1)}, bf16[768]{0:T(1024)(128)(2,1)S(1)}, bf16[768]{0:T(1024)(128)(2,1)S(1)}, bf16[768]{0:T(1024)(128)(2,1)S(1)}...) all-reduce(bf16[768]{0:T(1024)(128)(2,1)S(1)} %dynamic-update-slice, ...), channel_id=1, replica_groups=mesh['win'=32,'seq'=4] {'win','seq'}, use_global_device_ids=true, to_apply=%add.2 | all-reduce | flops 13056 | bytes 52224
  90.8 115.5 %all-gather.46.cloned.1.call-done = bf16[128,6,768]{2,1,0:T(8,128)(2,1)} async-done(((bf16[1,6,768]{2,1,0:T(8,128)(2,1)}), bf16[128,6,768]{2,1,0:T(8,128)(2,1)}) %all-gather.46.cloned.1.call-update) | async-done | bytes 1179664 | tf_op jit(solution)/shard_map/all_gather | solution.py:362
  210.2 189.8 %all-gather.52.cloned.1.call-done = bf16[128,6,768]{2,1,0:T(8,128)(2,1)} async-done(((bf16[1,6,768]{2,1,0:T(8,128)(2,1)}), bf16[128,6,768]{2,1,0:T(8,128)(2,1)}) %all-gather.52.cloned.1.call-update) | async-done | bytes 1179664 | tf_op jit(solution)/shard_map/all_gather | solution.py:361
  414.8 178.9 %all-gather.38.cloned.1.call-done = bf16[128,6,768]{2,1,0:T(8,128)(2,1)} async-done(((bf16[1,6,768]{2,1,0:T(8,128)(2,1)}), bf16[128,6,768]{2,1,0:T(8,128)(2,1)}) %all-gather.38.cloned.1.call-update) | async-done | bytes 1179664 | tf_op jit(solution)/shard_map/all_gather | solution.py:353
  597.4 189.7 %all-gather.40.cloned.1.call-done = bf16[128,6,768]{2,1,0:T(8,128)(2,1)} async-done(((bf16[1,6,768]{2,1,0:T(8,128)(2,1)}), bf16[128,6,768]{2,1,0:T(8,128)(2,1)}) %all-gather.40.cloned.1.call-update) | async-done | bytes 1179664 | tf_op jit(solution)/shard_map/all_gather | solution.py:350
  790.5 190.2 %all-gather.42.cloned.1.call-done = bf16[128,6,768]{2,1,0:T(8,128)(2,1)} async-done(((bf16[1,6,768]{2,1,0:T(8,128)(2,1)}), bf16[128,6,768]{2,1,0:T(8,128)(2,1)}) %all-gather.42.cloned.1.call-update) | async-done | bytes 1179664 | tf_op jit(solution)/shard_map/all_gather | solution.py:352
  1008.1 166.2 %all-gather.44.cloned.1.call-done = bf16[128,6,768]{2,1,0:T(8,128)(2,1)} async-done(((bf16[1,6,768]{2,1,0:T(8,128)(2,1)}), bf16[128,6,768]{2,1,0:T(8,128)(2,1)}) %all-gather.44.cloned.1.call-update) | async-done | bytes 1179664 | tf_op jit(solution)/shard_map/all_gather | solution.py:355
  1177.3 191.6 %all-gather.50.cloned.1.call-done = bf16[128,6,768]{2,1,0:T(8,128)(2,1)} async-done(((bf16[1,6,768]{2,1,0:T(8,128)(2,1)}), bf16[128,6,768]{2,1,0:T(8,128)(2,1)}) %all-gather.50.cloned.1.call-update) | async-done | bytes 1179664 | tf_op jit(solution)/shard_map/all_gather | solution.py:359
  1403.8 158.8 %all-gather.56.cloned.1.call-done = bf16[128,6,768]{2,1,0:T(8,128)(2,1)} async-done(((bf16[1,6,768]{2,1,0:T(8,128)(2,1)}), bf16[128,6,768]{2,1,0:T(8,128)(2,1)}) %all-gather.56.cloned.1.call-update) | async-done | bytes 1179664 | tf_op jit(solution)/shard_map/all_gather | solution.py:364
  1566.2 25.8 all-gather.60.cloned.1.call-done
  1631.4 18.8 all-gather.48.cloned.1.call-done
  1710.0 170.4 %all-gather.58.cloned.1.call-done = bf16[128,6,3072]{2,1,0:T(8,128)(2,1)} async-done(((bf16[1,6,3072]{2,1,0:T(8,128)(2,1)}), bf16[128,6,3072]{2,1,0:T(8,128)(2,1)}) %all-gather.58.cloned.1.call-update) | async-done | bytes 4718608 | tf_op jit(solution)/shard_map/all_gather | solution.py:368
  1894.7 185.4 %all-gather.36.cloned.1.call-done = bf16[3072,768]{1,0:T(8,128)(2,1)} async-done(((bf16[24,768]{1,0:T(8,128)(2,1)}), bf16[3072,768]{1,0:T(8,128)(2,1)}) %all-gather.36.cloned.1.call-update) | async-done | bytes 4718608 | tf_op jit(solution)/shard_map/all_gather | solution.py:370
  2216.7 112.2 %all-reduce.58.cloned.1.call-done = (bf16[1,1500,768]{1,2,0:T(8,128)(2,1)}, bf16[1,1500,768]{1,2,0:T(8,128)(2,1)}, bf16[1,1500,768]{1,2,0:T(8,128)(2,1)}, bf16[1,1500,768]{1,2,0:T(8,128)(2,1)}) async-done(((bf16[1,1500,768]{1,2,0:T(8,128)(2,1)}, bf16[1,1500,768]{1,2,0:T(8,128)(2,1)}, bf16[1,1500,768]{1,2,0:T(8,128)(2,1)}, bf16[1,1500,768]{1,2,0:T(8,128)(2,1)}), (bf16[1,1500,768]{1,2,0:T(8,128)(2,1)}, ...) | async-done | bytes 9216016
  2393.9 29.4 reduce-scatter.36.cloned.1.call-done
  2424.7 30.2 reduce-scatter.38.cloned.1.call-done
  2461.6 404.3 %fusion.192 = (f32[8,768]{1,0:T(8,128)}, f32[8,768]{1,0:T(8,128)}, f32[8,768]{1,0:T(8,128)S(1)}, f32[8,768]{1,0:T(8,128)}, f32[8,768]{1,0:T(8,128)}, /*index=5*/f32[8,768]{1,0:T(8,128)S(1)}, f32[8,3072]{1,0:T(8,128)S(1)}) fusion(f32[768,768]{1,0:T(8,128)} %convolution_add_fusion.9, f32[768,768]{1,0:T(8,128)} %convolution_add_fusion.8, ...), kind=kCustom, calls=%all-reduce-scatter.7 | all-reduce-scatter fusion | flops 7864321 | bytes 23838720
  3385.1 46.3 %concatenate = f32[262,768]{1,0:T(8,128)} concatenate(f32[6,768]{1,0:T(8,128)S(1)} %copy-done.176, f32[8,768]{1,0:T(8,128)S(1)} %copy-done.178, f32[8,768]{1,0:T(8,128)S(1)} %copy-done.180, f32[8,768]{1,0:T(8,128)S(1)} %copy-done.182, f32[8,768]{1,0:T(8,128)S(1)} %copy-done.184, f32[8,768]{1,0:T(8,128)S(1)} %copy-done.186, f32[8,768]{1,0:T(8,128)S(1)} %copy-done.188, ...), dimensions={0} | concatenate | bytes 1609728
  3431.6 26.5 concatenate.1
  3458.2 26.5 concatenate.2
  3500.2 27.2 concatenate.4
  3533.2 46.7 %concatenate.5 = f32[262,768]{1,0:T(8,128)} concatenate(f32[6,768]{1,0:T(8,128)S(1)} %copy-done.166, f32[8,768]{1,0:T(8,128)S(1)} %copy-done.294, f32[8,768]{1,0:T(8,128)} %copy-done.295, f32[8,768]{1,0:T(8,128)} %copy-done.297, f32[8,768]{1,0:T(8,128)} %copy-done.299, f32[8,768]{1,0:T(8,128)} %copy-done.300, f32[8,768]{1,0:T(8,128)} %copy-done.301, f32[8,768]{1,0:T(8,128)} %copy-done.302, ...), dimensions={0} | concatenate | bytes 1609728
  3654.5 56.2 %concatenate.6 = f32[262,3072]{1,0:T(8,128)} concatenate(f32[6,3072]{1,0:T(8,128)} %collective-permute-done.223, f32[8,3072]{1,0:T(8,128)} %collective-permute-done.222, f32[8,3072]{1,0:T(8,128)} %collective-permute-done.221, f32[8,3072]{1,0:T(8,128)} %collective-permute-done.220, f32[8,3072]{1,0:T(8,128)} %collective-permute-done.219, f32[8,3072]{1,0:T(8,128)} %copy-done.129, ...), dimensions={0} | concatenate | bytes 6438912
  3723.6 63.8 %all-reduce.48 = (f32[768]{0:T(1024)S(1)}, f32[768]{0:T(1024)S(1)}, f32[768]{0:T(1024)S(1)}, f32[768]{0:T(1024)S(1)}, f32[768]{0:T(1024)S(1)}, /*index=5*/f32[76...) all-reduce(f32[768]{0:T(1024)S(1)} %copy-done.333, ...), channel_id=42, replica_groups=mesh['win'=32,'seq'=4] {'win','seq'}, use_global_device_ids=true, to_apply=%region_45.46.clone | all-reduce | flops 13056 | bytes 104448
  (1563 shorter events, 1063.2 us)
Async XLA Ops:
  7.2 199.1 %all-gather.46.cloned.1.call-start = ((), (), s32[]{:S(2)}) async-start(), calls=%async_computation.11 | async-start | bytes 1585152 | tf_op jit(solution)/shard_map/all_gather | solution.py:362
  7.9 392.0 %all-gather.52.cloned.1.call-start = ((), (), s32[]{:S(2)}) async-start(), calls=%async_computation.14 | async-start | bytes 1585152 | tf_op jit(solution)/shard_map/all_gather | solution.py:361
  8.7 585.0 %all-gather.38.cloned.1.call-start = ((), (), s32[]{:S(2)}) async-start(), calls=%async_computation.7 | async-start | bytes 1585152 | tf_op jit(solution)/shard_map/all_gather | solution.py:353
  9.4 777.8 %all-gather.40.cloned.1.call-start = ((), (), s32[]{:S(2)}) async-start(), calls=%async_computation.8 | async-start | bytes 1585152 | tf_op jit(solution)/shard_map/all_gather | solution.py:350
  10.0 970.7 %all-gather.42.cloned.1.call-start = ((), (), s32[]{:S(2)}) async-start(), calls=%async_computation.9 | async-start | bytes 1585152 | tf_op jit(solution)/shard_map/all_gather | solution.py:352
  10.6 1163.7 %all-gather.44.cloned.1.call-start = ((), (), s32[]{:S(2)}) async-start(), calls=%async_computation.10 | async-start | bytes 1585152 | tf_op jit(solution)/shard_map/all_gather | solution.py:355
  11.2 1357.7 %all-gather.50.cloned.1.call-start = ((), (), s32[]{:S(2)}) async-start(), calls=%async_computation.13 | async-start | bytes 1585152 | tf_op jit(solution)/shard_map/all_gather | solution.py:359
  11.9 1550.7 %all-gather.56.cloned.1.call-start = ((), (), s32[]{:S(2)}) async-start(), calls=%async_computation.16 | async-start | bytes 1585152 | tf_op jit(solution)/shard_map/all_gather | solution.py:364
  12.7 1579.3 %all-gather.60.cloned.1.call-start = ((), (), s32[]{:S(2)}) async-start(), calls=%async_computation.18 | async-start | bytes 2887680 | tf_op jit(solution)/shard_map/all_gather | solution.py:212
  210.1 1410.6 %all-gather.62.cloned.1.call-start = ((), (), s32[]{:S(2)}) async-start(), calls=%async_computation.19 | async-start | bytes 2887680 | tf_op jit(solution)/shard_map/all_gather | solution.py:211
  403.8 1246.4 %all-gather.48.cloned.1.call-start = ((), (), s32[]{:S(2)}) async-start(), calls=%async_computation.12 | async-start | bytes 2887680 | tf_op jit(solution)/shard_map/all_gather | solution.py:212
  407.5 1271.4 %all-gather.54.cloned.1.call-start = ((), (), s32[]{:S(2)}) async-start(), calls=%async_computation.15 | async-start | bytes 2887680 | tf_op jit(solution)/shard_map/all_gather | solution.py:211
  410.1 1470.2 %all-gather.58.cloned.1.call-start = ((), (), s32[]{:S(2)}) async-start(), calls=%async_computation.17 | async-start | bytes 6340608 | tf_op jit(solution)/shard_map/all_gather | solution.py:368
  410.9 1669.2 %all-gather.36.cloned.1.call-start = ((), (), s32[]{:S(2)}) async-start(), calls=%async_computation.5 | async-start | bytes 4755456 | tf_op jit(solution)/shard_map/all_gather | solution.py:370
  411.4 1917.5 %all-reduce.58.cloned.1.call-start = ((), (), s32[]{:S(2)}) async-start(), calls=%async_computation.25 | async-start | bytes 18874368
  2151.1 224.5 %reduce-scatter.40.cloned.1.call-start = ((), (), s32[]{:S(2)}) async-start(), calls=%async_computation.22 | async-start | bytes 860160
  2180.2 211.7 %reduce-scatter.42.cloned.1.call-start = ((), (), s32[]{:S(2)}) async-start(), calls=%async_computation.23 | async-start | bytes 860160
  2190.9 232.4 %reduce-scatter.36.cloned.1.call-start = ((), (), s32[]{:S(2)}) async-start(), calls=%async_computation.20 | async-start | bytes 860160
  2207.7 247.2 %reduce-scatter.38.cloned.1.call-start = ((), (), s32[]{:S(2)}) async-start(), calls=%async_computation.21 | async-start | bytes 860160
  2215.2 1580.4 %all-reduce.56.cloned.1.call-start = ((), (), s32[]{:S(2)}) async-start(), calls=%async_computation.24 | async-start | bytes 9437184
  2339.8 1459.0 %reduce-scatter.34.cloned.1.call-start = ((), (), s32[]{:S(2)}) async-start(), calls=%async_computation.6 | async-start | bytes 9510912 | tf_op jit(solution)/shard_map/reduce_scatter | solution.py:408
  3366.1 161.3 %collective-permute-start.162 = (f32[8,768]{1,0:T(8,128)S(1)}, f32[8,768]{1,0:T(8,128)}, u32[]{:S(2)}, u32[]{:S(2)}) collective-permute-start(f32[8,768]{1,0:T(8,128)S(1)} %copy-done.119), channel_id=1, source_target_pairs={{0,3},{1,4},{2,5},{3,6},{4,7},{5,8},{6,9},{7,10},{8,11},{9,12},{10... | collective-permute-start | bytes 73736
  3378.1 203.1 %collective-permute-start.222 = (f32[8,3072]{1,0:T(8,128)S(1)}, f32[8,3072]{1,0:T(8,128)}, u32[]{:S(2)}, u32[]{:S(2)}) collective-permute-start(f32[8,3072]{1,0:T(8,128)S(1)} %get-tuple-element.185), channel_id=1, source_target_pairs={{0,31},{1,32},{2,33},{3,34},{4,35},{5,36},{6,37},{7,38},{8,39},{9,... | collective-permute-start | bytes 294920
  3380.0 199.9 %collective-permute-start.223 = (f32[6,3072]{1,0:T(8,128)S(1)}, f32[6,3072]{1,0:T(8,128)}, u32[]{:S(2)}, u32[]{:S(2)}) collective-permute-start(f32[6,3072]{1,0:T(8,128)S(1)} %slice.46), channel_id=1, source_target_pairs={{0,32},{1,33},{2,34},{3,35},{4,36},{5,37},{6,38},{7,39},{8,40},{9,... | collective-permute-start | bytes 221192
  (609 other events, 27070.9 us)
Sparse Core Ops, SparseCore 0:
  9.8 196.5 all-gather.45
  208.0 191.8 all-gather.51
  401.7 191.9 all-gather.37
  595.3 191.8 all-gather.39
  788.7 191.9 all-gather.41
  982.3 191.9 all-gather.43
  1176.0 192.8 all-gather.49
  1370.6 191.9 all-gather.55
  1564.8 27.1 all-gather.59
  1593.5 27.1 all-gather.61
  1623.0 27.1 all-gather.47
  1651.7 27.1 all-gather.53
  1680.6 199.6 all-gather.57
  1881.9 198.1 all-gather.35
  2151.2 177.6 all-reduce.57
  2332.0 28.4 reduce-scatter.39
  2363.0 28.8 reduce-scatter.41
  2394.4 28.8 reduce-scatter.35
  2425.9 28.8 reduce-scatter.37
  2459.7 506.2 all-reduce.55
  2969.0 647.0 reduce-scatter.33
where the time goes:
time: 3840 us; the launch traced here: 3810 us
  waiting for transfers between devices  2010 us (52%)
  blocking collectives  577 us (15%)
  starting transfers between devices  545 us (14%)
  local copies, waits for them, and re-layouts  424 us (11%)
  matrix products  185 us (5%)
  other arithmetic  38.8 us (1%)
    unnamed x230, starting transfers between devices  544 us
    unnamed x3, blocking collectives  537 us
    unnamed x871, local copies, waits for them, and re-layouts  360 us
    unnamed x251, waiting for transfers between devices  196 us
    all_gather x1, waiting for transfers between devices, per_device(): lax.all_gather(cross_query, ('win', 'seq'), axis=0, tiled=True)  192 us
    all_gather x1, waiting for transfers between devices, per_device(): lax.all_gather(self_key, ('win', 'seq'), axis=0, tiled=True)  190 us
    all_gather x1, waiting for transfers between devices, per_device(): lax.all_gather(cross_key, ('win', 'seq'), axis=0, tiled=True)  190 us
    all_gather x1, waiting for transfers between devices, per_device(): lax.all_gather(self_query, ('win', 'seq'), axis=0, tiled=True)  190 us
  transfers between devices with their start and end apart: 245, of which 19 were waited for; matrix products, arithmetic and copies ran while one was open for 25% of the time, Pallas kernels for 0%

commit v1 on v0

v1 whole, which is shorter than its diff:
```python
from functools import partial

import jax
import jax.numpy as jnp
from jax import lax
from jax.experimental import pallas as pl
from jax.experimental.pallas import tpu as pltpu
from jax.sharding import PartitionSpec as P

bf, f32 = jnp.bfloat16, jnp.float32
HEADS, HEAD_DIM = 12, 64
EPS = 1e-05
SCALE = 0.125
BLOCKED = -1e30
MESH = pl.DeviceIdType.MESH
PIECES, ROWS, D = 16, 48, 768
HALF = D // 2


def coords():
    win, seq = lax.axis_index("win"), lax.axis_index("seq")
    x, y = win // 8, lax.rem(win // 2, 4)
    z = (seq // 2) * 2 + lax.rem(win, 2)
    return x, y, z, lax.rem(seq, 2)


def device_at(x, y, z, core):
    return (x * 8 + y * 2 + lax.rem(z, 2), (z // 2) * 2 + core)


def member(z, core):
    return lax.rem(z, 2) * 4 + (z // 2) * 2 + core


def enter(peers):
    barrier = pltpu.get_barrier_semaphore()
    for peer in peers:
        pl.semaphore_signal(barrier, inc=1, device_id=peer, device_id_type=MESH)
    pl.semaphore_wait(barrier, len(peers))


def relayout_matrix():
    r = lax.broadcasted_iota(jnp.int32, (784, 1), 0)
    piece, at = r // 48, lax.rem(r, 48)
    narrow = (at // 6) * 112 + piece * 6 + lax.rem(at, 6)
    wide = ((piece - 12) * 2 + at // 24) * 112 + 72 + lax.rem(at, 24)
    small = lax.rem(at, 8) * 112 + 96
    source = jnp.where(piece < 12, narrow, jnp.where(piece < 16, wide, small))
    cols = lax.broadcasted_iota(jnp.int32, (784, 896), 1)
    return jnp.where(cols == source, 1.0, 0.0).astype(bf)


def gather_kernel(shard, tok_in, enc_in, og_in, W, SM, tok, enc, og, zbuf, slab, smbuf,
                  zs, zr, ds, dr, ls, s1, r1, s2, r2, ss1, sr1, ss2, sr2, cs, cr, es, er, fs, fr):
    x, y, z, core = coords()
    hi = z // 2
    other = 1 - core
    partner = device_at(x, y, z, other)
    across = lax.rem(z + 2, 4)
    xp = [device_at(lax.rem(x + o, 4), y, z, core) for o in (1, 2, 3)]
    yp = [device_at(x, lax.rem(y + o, 4), z, core) for o in (1, 2, 3)]
    zp = [device_at(x, y, lax.rem(z + o, 4), core) for o in (1, 2, 3)]
    enter([partner, device_at(x, y, across, other)] + xp + yp + zp)

    def remote(src, dst, send, recv, to):
        return pltpu.make_async_remote_copy(src_ref=src, dst_ref=dst, send_sem=send, recv_sem=recv,
                                            device_id=to, device_id_type=MESH)
    sent = []

    def start(*a):
        c = remote(*a)
        c.start()
        sent.append(c)
        return c
    me = member(z, core)
    mine = pltpu.make_async_copy(shard, zbuf.at[me], ls.at[0])
    mine.start()
    for o in (1, 2, 3):
        start(shard, zbuf.at[me], zs.at[o], zr.at[o], zp[o - 1])
    start(shard, zbuf.at[me], ds.at[0], dr.at[0], partner)

    block = hi * 2 + core
    locals_ = []

    def local(src, dst, sem):
        c = pltpu.make_async_copy(src, dst, sem)
        c.start()
        locals_.append(c)
    home = device_at(x, y, across, core)
    for i, (src, dst) in enumerate(((tok_in, tok), (enc_in, enc))):
        start(src.at[1 - hi], dst.at[block], es.at[i], er.at[i], home)
        start(src.at[hi], dst.at[block], es.at[2 + i], er.at[2 + i], partner)
        local(src.at[hi], dst.at[block], ls.at[1 + i])
    start(og_in.at[1 - hi], og.at[core], es.at[4], er.at[4 + core], device_at(x, y, across, hi))

    @pl.when(core == hi)
    def _():
        c = pltpu.make_async_copy(og_in.at[hi], og.at[core], ls.at[3])
        c.start()
        c.wait()

    @pl.when(core != hi)
    def _():
        c = remote(og_in.at[hi], og.at[core], es.at[5], er.at[6], partner)
        c.start()
        c.wait_send()
    for o in (1, 2, 3):
        remote(shard, zbuf.at[me], zs.at[o], zr.at[o], zp[0]).wait_recv()
        src = member(lax.rem(z + 4 - o, 4), core)
        start(zbuf.at[src], zbuf.at[src], ds.at[o], dr.at[o], partner)
    for o in range(4):
        remote(shard, zbuf.at[me], ds.at[o], dr.at[o], partner).wait_recv()
    mine.wait()
    spread = jnp.dot(relayout_matrix(), zbuf[...].reshape(896, D), preferred_element_type=jnp.float32).astype(bf)
    slab[...] = spread[:768].reshape(PIECES, ROWS, D)
    smbuf[...] = spread[768:, :128]

    def rows(gx, gy):
        return pl.ds(pl.multiple_of((gx * 4 + gy) * 48, 16), 48)
    part = pl.ds(pl.multiple_of(core * 8, 8), 8)
    cols = (pl.ds(0, HALF), pl.ds(HALF, HALF))
    local(slab, W.at[:, rows(x, y), :], ls.at[4])
    local(smbuf, SM.at[x * 4 + y], ls.at[5])
    first, second = (xp, yp), (yp, xp)
    for o in (1, 2, 3):
        for k in (0, 1):
            start(slab.at[part, :, cols[k]], W.at[part, rows(x, y), cols[k]], s1.at[k, o], r1.at[k, o], first[k][o - 1])
        start(smbuf, SM.at[x * 4 + y], ss1.at[o], sr1.at[o], xp[o - 1])
    for o in (1, 2, 3):
        for k in (0, 1):
            start(slab.at[part, :, cols[k]], W.at[part, rows(x, y), cols[k]], s2.at[k, 0, o], r2.at[k, 0, o], second[k][o - 1])
        start(smbuf, SM.at[x * 4 + y], ss2.at[0, o], sr2.at[0, o], yp[o - 1])

    def origin(k, b, p):
        if k == 0:
            return lax.rem(x + 4 - b, 4), lax.rem(y + 4 - p, 4)
        return lax.rem(x + 4 - p, 4), lax.rem(y + 4 - b, 4)

    def hand_over(k, b, p):
        at = W.at[part, rows(*origin(k, b, p)), cols[k]]
        start(at, at, cs.at[k, b * 4 + p], cr.at[k, b * 4 + p], partner)
    for b in (1, 2, 3):
        for k in (0, 1):
            at = W.at[part, rows(*origin(k, b, 0)), cols[k]]
            remote(at, at, s1.at[k, b], r1.at[k, b], partner).wait_recv()
            for p in (1, 2, 3):
                start(at, at, s2.at[k, b, p], r2.at[k, b, p], second[k][p - 1])
            hand_over(k, b, 0)
        at = SM.at[lax.rem(x + 4 - b, 4) * 4 + y]
        remote(at, at, ss1.at[b], sr1.at[b], partner).wait_recv()
        for p in (1, 2, 3):
            start(at, at, ss2.at[b, p], sr2.at[b, p], yp[p - 1])
    for i, (src, dst) in enumerate(((tok_in, tok), (enc_in, enc))):
        far = dst.at[(1 - hi) * 2 + core]
        remote(far, far, es.at[i], er.at[i], partner).wait_recv()
        start(far, far, fs.at[i], fr.at[i], partner)
    for b in range(4):
        for p in (1, 2, 3):
            for k in (0, 1):
                at = W.at[part, rows(*origin(k, b, p)), cols[k]]
                remote(at, at, s2.at[k, b, p], r2.at[k, b, p], partner).wait_recv()
                hand_over(k, b, p)
            at = SM.at[0]
            remote(at, at, ss2.at[b, p], sr2.at[b, p], partner).wait_recv()
    for k in (0, 1):
        for q in range(1, 16):
            at = W.at[part, rows(x, y), cols[k]]
            remote(at, at, cs.at[k, q], cr.at[k, q], partner).wait_recv()
    for i, dst in enumerate((tok, enc)):
        remote(dst.at[0], dst.at[0], es.at[2 + i], er.at[2 + i], partner).wait_recv()
        remote(dst.at[0], dst.at[0], fs.at[i], fr.at[i], partner).wait_recv()
    at = og.at[0]

    @pl.when(hi == core)
    def _():
        remote(at, at, es.at[4], er.at[6], partner).wait_recv()

    @pl.when(hi != core)
    def _():
        for s in (0, 1):
            remote(at, at, es.at[4], er.at[4 + s], partner).wait_recv()
    for c in sent:
        c.wait_send()
    for c in locals_:
        c.wait()


def gather_all(shard, tok, enc, og):
    any_ = pl.BlockSpec(memory_space=pl.ANY)
    DMA = pltpu.SemaphoreType.DMA
    return pl.pallas_call(
        gather_kernel,
        out_shape=[jax.ShapeDtypeStruct((16, D, D), bf), jax.ShapeDtypeStruct((16, 16, 128), bf),
                   jax.ShapeDtypeStruct((4, 112, D), bf), jax.ShapeDtypeStruct((4, 384, D), bf),
                   jax.ShapeDtypeStruct((2, 112, D), bf)],
        in_specs=[any_] * 4, out_specs=[any_] * 5,
        scratch_shapes=[pltpu.VMEM((8, 112, D), bf), pltpu.VMEM((16, 48, D), bf), pltpu.VMEM((16, 128), bf),
                        DMA((4,)), DMA((4,)), DMA((4,)), DMA((4,)), DMA((6,)),
                        DMA((2, 4)), DMA((2, 4)), DMA((2, 4, 4)), DMA((2, 4, 4)),
                        DMA((4,)), DMA((4,)), DMA((4, 4)), DMA((4, 4)),
                        DMA((2, 16)), DMA((2, 16)), DMA((6,)), DMA((7,)), DMA((2,)), DMA((2,))],
        compiler_params=pltpu.CompilerParams(collective_id=0, has_side_effects=True, vmem_limit_bytes=40 << 20),
        name="gather_all",
    )(shard, tok, enc, og)


def split_matrix(core):
    r = lax.broadcasted_iota(jnp.int32, (384, 1), 0)
    k, i = r // 48, lax.rem(r, 48)
    narrow = (i // 6) * 48 + k * 6 + lax.rem(i, 6)
    wide = (4 + k // 2) * 48 + lax.rem(k, 2) * 24 + i - 24
    source = jnp.where((core == 1) & (i >= 24), wide, narrow)
    cols = lax.broadcasted_iota(jnp.int32, (384, 384), 1)
    return jnp.where(cols == source, 1.0, 0.0).astype(bf)


def reduce_kernel(G, SG, BO, PI, EP, gw, gs, bo_out, pi_out, ep_out,
                  db, own, r1, r2, slab, shares, r3, r4, sgb, sd, s1b, s2b, s3b,
                  pib, pio, pz, pf, eib, eio, ez, ef, gwv, gsv,
                  ls, ds, dr, s1, q1, s2, q2, s3, q3, s4, ss, sr, ts, tr, os_):
    x, y, z, core = coords()
    hi = z // 2
    other = 1 - core
    partner = device_at(x, y, z, other)
    across = lax.rem(z + 2, 4)
    home = device_at(x, y, across, core)
    xp = [None] + [device_at(lax.rem(x + o, 4), y, z, core) for o in (1, 2, 3)]
    yp = [None] + [device_at(x, lax.rem(y + o, 4), z, core) for o in (1, 2, 3)]
    zp = [None] + [device_at(x, y, lax.rem(z + o, 4), core) for o in (1, 2, 3)]
    enter([partner, device_at(x, y, across, other)] + xp[1:] + yp[1:] + zp[1:])
    sent = []

    def remote(src, dst, send, recv, to):
        return pltpu.make_async_remote_copy(src_ref=src, dst_ref=dst, send_sem=send, recv_sem=recv,
                                            device_id=to, device_id_type=MESH)

    def start(*a):
        c = remote(*a)
        c.start()
        sent.append(c)

    def arrived(at, sem):
        remote(at, at, s4, sem, partner).wait_recv()

    def local(src, dst, sem):
        c = pltpu.make_async_copy(src, dst, sem)
        c.start()
        return c

    def rows(gx, gy):
        return pl.ds(pl.multiple_of((gx * 4 + gy) * 48, 16), 48)
    cols = (pl.ds(0, HALF), pl.ds(HALF, HALF))
    part = pl.ds(pl.multiple_of(core * 8, 8), 8)
    part_other = pl.ds(pl.multiple_of(other * 8, 8), 8)

    def target(k, b, p):
        if k == 0:
            return lax.rem(x + b, 4), lax.rem(y + p, 4)
        return lax.rem(x + p, 4), lax.rem(y + b, 4)
    order = [(p, b, k) for p in (2, 1, 3, 0) for b in range(4) for k in (0, 1)]
    loads = {}
    start(SG, sd, ss.at[0], sr.at[0], partner)
    sg_load = local(SG, sgb, ls.at[2, 0, 0])
    for p, b, k in order:
        at = rows(*target(k, b, p))
        start(G.at[part_other, at, cols[k]], db.at[k, p, b], ds.at[k, p, b], dr.at[k, p, b], partner)
        loads[k, p, b] = local(G.at[part, at, cols[k]], own.at[k, p, b], ls.at[k, p, b])
    act = []
    for i, (src, buf, mine_buf) in enumerate(((PI, pib, pio), (EP, eib, eio))):
        for s in (0, 1):
            start(src.at[2 * s + other], buf.at[s], ts.at[i, s], tr.at[i, s], partner)
            act.append(local(src.at[2 * s + core], mine_buf.at[s], ls.at[2, 1 + i, s]))
    same = core == hi

    @pl.when(same)
    def _():
        c = pltpu.make_async_copy(BO.at[core], bo_out.at[hi], ls.at[2, 3, 0])
        c.start()
        c.wait()
        d = remote(BO.at[other], bo_out.at[hi], os_.at[0], tr.at[3, 0], partner)
        d.start()
        d.wait_send()

    @pl.when(jnp.logical_not(same))
    def _():
        copies = [remote(BO.at[s], bo_out.at[hi], os_.at[s], tr.at[3, 1], device_at(x, y, across, s)) for s in (0, 1)]
        for c in copies:
            c.start()
        for c in copies:
            c.wait_send()

    first, second = (yp, xp), (xp, yp)
    sg_load.wait()
    arrived(sd, sr.at[0])
    sgb[...] = sgb[...] + sd[...]
    for p in (1, 2, 3):
        start(sgb.at[:, lax.rem(y + p, 4)], s1b.at[p], ss.at[p], sr.at[p], yp[p])
    for p, b, k in order:
        arrived(db.at[k, p, b], dr.at[k, p, b])
        loads[k, p, b].wait()

        @pl.loop(0, 8)
        def _(i):
            db[k, p, b, i] = (db[k, p, b, i].astype(f32) + own[k, p, b, i].astype(f32)).astype(bf)
        if p:
            start(db.at[k, p, b], r1.at[k, p, b], s1.at[k, p, b], q1.at[k, p, b], first[k][p])
    for c in act:
        c.wait()
    for i, (buf, mine_buf, out, zbuf, fb) in enumerate(((pib, pio, pi_out, pz, pf), (eib, eio, ep_out, ez, ef))):
        for s in (0, 1):
            arrived(buf.at[s], tr.at[i, s])
        n = buf.shape[1] // 16

        @pl.loop(0, n)
        def _(t):
            at = pl.ds(pl.multiple_of(t * 16, 16), 16)
            mine_buf[1 - hi, at] = (mine_buf[1 - hi, at].astype(f32) + buf[1 - hi, at].astype(f32)).astype(bf)
        start(mine_buf.at[1 - hi], zbuf, ts.at[2, i], tr.at[2, i], home)

        @pl.loop(0, n)
        def _(t):
            at = pl.ds(pl.multiple_of(t * 16, 16), 16)
            fb[hi, at] = mine_buf[hi, at].astype(f32) + buf[hi, at].astype(f32)
    for b in (1, 2, 3, 0):
        for k in (0, 1):
            for p in (1, 2, 3):
                arrived(r1.at[k, p, b], q1.at[k, p, b])

            @pl.loop(0, 8)
            def _(i):
                total = db[k, 0, b, i].astype(f32)
                for p in (1, 2, 3):
                    total = total + r1[k, p, b, i].astype(f32)
                db[k, 0, b, i] = total.astype(bf)
            if b:
                start(db.at[k, 0, b], r2.at[k, b], s2.at[k, b], q2.at[k, b], second[k][b])
    total = sgb[:, y]
    for p in (1, 2, 3):
        arrived(s1b.at[p], sr.at[p])
        total = total + s1b[p]
    sgb[:, y] = total
    for b in (1, 2, 3):
        start(sgb.at[lax.rem(x + b, 4), y], s2b.at[b], ss.at[3 + b], sr.at[3 + b], xp[b])
    for k in (0, 1):
        for b in (1, 2, 3):
            arrived(r2.at[k, b], q2.at[k, b])

        @pl.loop(0, 8)
        def _(i):
            total = db[k, 0, 0, i].astype(f32)
            for b in (1, 2, 3):
                total = total + r2[k, b, i].astype(f32)
            slab[i, :, k * HALF:(k + 1) * HALF] = total.astype(bf)
    total = sgb[x, y]
    for b in (1, 2, 3):
        arrived(s2b.at[b], sr.at[3 + b])
        total = total + s2b[b]
    s3b[0] = total
    for o in (1, 2, 3):
        start(s3b.at[0], s3b.at[o], ss.at[6 + o], sr.at[6 + o], zp[o])
    shares[...] = jnp.dot(split_matrix(core), slab[...].reshape(384, D), preferred_element_type=f32).astype(bf).reshape(8, 48, D)
    for o in (1, 2, 3):
        to = member(lax.rem(z + o, 4), 0)
        start(shares.at[pl.ds(to, 2)], r3.at[o], s3.at[o], q3.at[o], zp[o])
    for o in (1, 2, 3):
        arrived(r3.at[o], q3.at[o])
    base = member(z, 0)

    def share(c):
        total = shares[base + c].astype(f32)
        for o in (1, 2, 3):
            total = total + r3[o, c].astype(f32)
        return total
    gwv[core] = share(core)
    slab[0] = share(other).astype(bf)
    start(slab.at[0], r4, s4, q3.at[0], partner)
    total = s3b[0]
    for o in (1, 2, 3):
        arrived(s3b.at[o], sr.at[6 + o])
        total = total + s3b[o]
    own_row = lax.broadcasted_iota(jnp.int32, (8, 128), 0) == member(z, core)
    gsv[...] = jnp.broadcast_to(jnp.sum(jnp.where(own_row, total, 0.0), 0, keepdims=True), (8, 128))
    for i, (zbuf, fb) in enumerate(((pz, pf), (ez, ef))):
        arrived(zbuf, tr.at[2, i])

        @pl.loop(0, zbuf.shape[0] // 16)
        def _(t):
            at = pl.ds(pl.multiple_of(t * 16, 16), 16)
            fb[1 - hi, at] = zbuf[at].astype(f32)
    arrived(r4, q3.at[0])
    gwv[other] = r4[...].astype(f32)
    outs = [local(gwv, gw, ls.at[2, 0, 0]), local(gsv, gs, ls.at[2, 0, 1]),
            local(pf, pi_out, ls.at[2, 0, 2]), local(ef, ep_out, ls.at[2, 0, 3])]

    @pl.when(core != hi)
    def _():
        arrived(bo_out.at[0], tr.at[3, 0])
    arrived(bo_out.at[0], tr.at[3, 1])
    for c in sent:
        c.wait_send()
    for c in outs:
        c.wait()


def reduce_all(G, SG, BO, PI, EP):
    any_ = pl.BlockSpec(memory_space=pl.ANY)
    DMA = pltpu.SemaphoreType.DMA
    V = pltpu.VMEM
    return pl.pallas_call(
        reduce_kernel,
        out_shape=[jax.ShapeDtypeStruct((2, 48, D), f32), jax.ShapeDtypeStruct((8, 128), f32),
                   jax.ShapeDtypeStruct((2, 112, D), bf), jax.ShapeDtypeStruct((2, 112, D), f32),
                   jax.ShapeDtypeStruct((2, 384, D), f32)],
        in_specs=[any_] * 5, out_specs=[any_] * 5,
        scratch_shapes=[
            V((2, 4, 4, 8, 48, HALF), bf), V((2, 4, 4, 8, 48, HALF), bf), V((2, 4, 4, 8, 48, HALF), bf), V((2, 4, 8, 48, HALF), bf),
            V((8, 48, D), bf), V((8, 48, D), bf), V((4, 2, 48, D), bf), V((48, D), bf),
            V((4, 4, 8, 128), f32), V((4, 4, 8, 128), f32), V((4, 4, 8, 128), f32), V((4, 8, 128), f32), V((4, 8, 128), f32),
            V((2, 112, D), bf), V((2, 112, D), bf), V((112, D), bf), V((2, 112, D), f32),
            V((2, 384, D), bf), V((2, 384, D), bf), V((384, D), bf), V((2, 384, D), f32),
            V((2, 48, D), f32), V((8, 128), f32),
            DMA((3, 4, 4)), DMA((2, 4, 4)), DMA((2, 4, 4)), DMA((2, 4, 4)), DMA((2, 4, 4)), DMA((2, 4)), DMA((2, 4)),
            DMA((4,)), DMA((4,)), DMA, DMA((10,)), DMA((10,)), DMA((4, 2)), DMA((4, 2)), DMA((2,))],
        compiler_params=pltpu.CompilerParams(collective_id=1, has_side_effects=True, vmem_limit_bytes=60 << 20),
        name="reduce_all",
    )(G, SG, BO, PI, EP)


def layer_norm(values):
    mean = jnp.mean(values, -1, keepdims=True)
    centered = values - mean
    spread = jnp.mean(centered * centered, -1, keepdims=True)
    r = lax.rsqrt(spread + EPS)
    return centered * r, r


def norm_back(e, n, r, gain):
    eg = e * gain
    return r * (eg - jnp.mean(eg, -1, keepdims=True) - n * jnp.mean(eg * n, -1, keepdims=True))


def dot(a, b):
    return jnp.dot(a, b, preferred_element_type=f32)


def dot_back(a, b):
    return lax.dot_general(a, b, (((1,), (1,)), ((), ())), preferred_element_type=f32)


def dot_grad(a, b):
    return lax.dot_general(a, b, (((0,), (0,)), ((), ())), preferred_element_type=f32).astype(bf)


def heads(v):
    return v.reshape(v.shape[0], HEADS, HEAD_DIM)


def attend(q, k, v, allowed):
    s = jnp.einsum("qhe,khe->hqk", heads(q), heads(k), preferred_element_type=f32) * SCALE
    s = jnp.where(allowed[None], s, BLOCKED)
    top = jnp.max(s, -1, keepdims=True)
    p = jnp.exp(s - top)
    total = jnp.sum(p, -1, keepdims=True)
    mixed = jnp.einsum("hqk,khe->qhe", (p / total).astype(bf), heads(v), preferred_element_type=f32)
    return mixed.reshape(q.shape).astype(bf), top + jnp.log(total)


def attend_back(q, k, v, allowed, log_total, g):
    s = jnp.einsum("qhe,khe->hqk", heads(q), heads(k), preferred_element_type=f32) * SCALE
    p = jnp.exp(jnp.where(allowed[None], s, BLOCKED) - log_total)
    dp = jnp.einsum("qhe,khe->hqk", heads(g), heads(v), preferred_element_type=f32)
    ds = (p * (dp - jnp.sum(p * dp, -1, keepdims=True))).astype(bf)
    gq = jnp.einsum("hqk,khe->qhe", ds, heads(k), preferred_element_type=f32) * SCALE
    gk = jnp.einsum("hqk,qhe->khe", ds, heads(q), preferred_element_type=f32) * SCALE
    gv = jnp.einsum("hqk,qhe->khe", p.astype(bf), heads(g), preferred_element_type=f32)
    return gq.reshape(q.shape).astype(bf), gk.reshape(k.shape).astype(bf), gv.reshape(k.shape).astype(bf)


def middle(W, vec, hidden_in_bias, tok, enc, og, seg, clip, core):
    (self_gain, self_shift, bq, bv, bo, cross_gain, cross_shift, bcq, bcv, bco, final_gain, final_shift, bho) = vec
    half = lax.dynamic_slice_in_dim
    tokens = tok.reshape(448, D).astype(f32)
    enc = enc.reshape(1536, D)
    og = og.reshape(224, D)
    places = jnp.arange(448, dtype=jnp.int32)
    my_seg = half(seg, core * 224, 224, 0)
    my_places = half(places, core * 224, 224, 0)
    self_allowed = (my_seg[:, None] == seg[None]) & (places[None] <= my_places[:, None])
    cross_allowed = my_seg[:, None] == clip[None]
    n1, rs1 = layer_norm(tokens)
    first = (n1 * self_gain + self_shift).astype(bf)
    first_q = half(first, core * 224, 224, 0)
    q = (dot(first_q, W[0]) + bq).astype(bf)
    k = dot(first, W[1]).astype(bf)
    v = (dot(first, W[2]) + bv).astype(bf)
    mixed, total = attend(q, k, v, self_allowed)
    after_self = half(tokens, core * 224, 224, 0) + dot(mixed, W[3]) + bo
    n2, rs2 = layer_norm(after_self)
    second = (n2 * cross_gain + cross_shift).astype(bf)
    cq = (dot(second, W[4]) + bcq).astype(bf)
    ck = dot(enc, W[5]).astype(bf)
    cv = (dot(enc, W[6]) + bcv).astype(bf)
    cmixed, ctotal = attend(cq, ck, cv, cross_allowed)
    after_cross = after_self + dot(cmixed, W[7]) + bco
    n3, rs3 = layer_norm(after_cross)
    third = (n3 * final_gain + final_shift).astype(bf)
    acts, g_pres, dW = [], [], [None] * 16
    g_third = jnp.zeros((224, D), f32)
    result = after_cross + bho
    g_hib = []
    for n in range(4):
        pre = dot(third, W[8 + n]) + hidden_in_bias[n]
        act, back = jax.vjp(lambda t: jax.nn.gelu(t, approximate=False), pre)
        act = act.astype(bf)
        result = result + dot(act, W[12 + n])
        dW[12 + n] = dot_grad(act, og)
        g_pre = back(dot_back(og, W[12 + n]))[0].astype(bf)
        dW[8 + n] = dot_grad(third, g_pre)
        g_third = g_third + dot_back(g_pre, W[8 + n])
        g_hib.append(jnp.sum(g_pre.astype(f32), 0))
    block_output = result.astype(bf).reshape(2, 112, D)
    ogf = og.astype(f32)
    g_bho = jnp.sum(ogf, 0)
    g_fg, g_fs = jnp.sum(g_third * n3, 0), jnp.sum(g_third, 0)
    g_cross = ogf + norm_back(g_third, n3, rs3, final_gain)
    branch = g_cross.astype(bf)
    dW[7] = dot_grad(cmixed, branch)
    g_bco = jnp.sum(branch.astype(f32), 0)
    g_cmixed = dot_back(branch, W[7]).astype(bf)
    gcq, gck, gcv = attend_back(cq, ck, cv, cross_allowed, ctotal, g_cmixed)
    dW[5] = dot_grad(enc, gck)
    dW[6] = dot_grad(enc, gcv)
    g_bcv = jnp.sum(gcv.astype(f32), 0)
    enc_grad = (dot_back(gck, W[5]) + dot_back(gcv, W[6])).astype(bf).reshape(4, 384, D)
    dW[4] = dot_grad(second, gcq)
    g_bcq = jnp.sum(gcq.astype(f32), 0)
    e2 = dot_back(gcq, W[4])
    g_cg, g_cs = jnp.sum(e2 * n2, 0), jnp.sum(e2, 0)
    g_self = g_cross + norm_back(e2, n2, rs2, cross_gain)
    branch = g_self.astype(bf)
    dW[3] = dot_grad(mixed, branch)
    g_bo = jnp.sum(branch.astype(f32), 0)
    g_mixed = dot_back(branch, W[3]).astype(bf)
    gq, gk, gv = attend_back(q, k, v, self_allowed, total, g_mixed)
    dW[0] = dot_grad(first_q, gq)
    dW[1] = dot_grad(first, gk)
    dW[2] = dot_grad(first, gv)
    g_bq, g_bv = jnp.sum(gq.astype(f32), 0), jnp.sum(gv.astype(f32), 0)
    e1 = dot_back(gk, W[1]) + dot_back(gv, W[2])
    e1 = lax.dynamic_update_slice_in_dim(e1, half(e1, core * 224, 224, 0) + dot_back(gq, W[0]), core * 224, 0)
    g_sg, g_ss = jnp.sum(e1 * n1, 0), jnp.sum(e1, 0)
    g_in = norm_back(e1, n1, rs1, self_gain)
    g_in = lax.dynamic_update_slice_in_dim(g_in, half(g_in, core * 224, 224, 0) + g_self, core * 224, 0)
    input_grad = g_in.astype(bf).reshape(4, 112, D)
    g_vec = jnp.stack([g_sg, g_ss, g_bq, g_bv, g_bo, g_cg, g_cs, g_bcq, g_bcv, g_bco, g_fg, g_fs, g_bho])
    return block_output, input_grad, enc_grad, jnp.stack(dW), g_vec, jnp.stack(g_hib)


def per_device(
    tokens, encoder_states, segments, frame_clips, out_grad,
    self_gain, self_shift, self_query, self_query_bias, self_key, self_value, self_value_bias, self_output,
    self_output_bias, cross_gain, cross_shift, cross_query, cross_query_bias, cross_key, cross_value,
    cross_value_bias, cross_output, cross_output_bias, final_gain, final_shift, hidden_in, hidden_in_bias,
    hidden_out, hidden_out_bias,
):
    seq = lax.axis_index("seq")
    hi, core = seq // 2, lax.rem(seq, 2)
    hidden = hidden_in.reshape(6, 16, 4, 48).transpose(2, 0, 1, 3).reshape(24, D)
    vectors = (self_gain, self_shift, self_query_bias, self_value_bias, self_output_bias, cross_gain, cross_shift,
               cross_query_bias, cross_value_bias, cross_output_bias, final_gain, final_shift, hidden_out_bias)
    small = jnp.pad(jnp.concatenate(vectors + (hidden_in_bias,)), (0, D - 102))[None]
    shard = jnp.concatenate([self_query, self_key, self_value, self_output, cross_query, cross_key, cross_value,
                             cross_output, hidden, hidden_out, small, jnp.zeros((15, D), bf)])
    frames = jnp.pad(encoder_states[:, 0], ((0, 0), (0, 9), (0, 0)))
    W, SM, tok, enc, og = gather_all(shard, tokens[:, 0], frames, out_grad[:, 0])
    small = SM[:, :8].reshape(128, 128).astype(f32)
    vec = small[:, :78].reshape(128, 13, 6).transpose(1, 0, 2).reshape(13, D)
    hib = small[:, 78:102].reshape(16, 4, 48).transpose(1, 0, 2).reshape(4, D)
    seg = segments[:, 0][hi]
    clip = jnp.pad(frame_clips[:, 0][hi].reshape(4, 375), ((0, 0), (0, 9)), constant_values=-1).reshape(1536)
    block_output, input_grad, enc_grad, dW, g_vec, g_hib = middle(W, vec, hib, tok, enc, og, seg, clip, core)
    g_small = jnp.concatenate([g_vec.reshape(13, 128, 6).transpose(1, 0, 2).reshape(128, 78),
                               g_hib.reshape(4, 16, 48).transpose(1, 0, 2).reshape(128, 24),
                               jnp.zeros((128, 26), f32)], 1).reshape(4, 4, 8, 128)
    gw, gs, bo, gi, ge = reduce_all(dW, g_small, block_output, input_grad, enc_grad)
    gv = [gs[0, 6 * i:6 * i + 6] for i in range(13)]
    m = [gw[0, 6 * i:6 * i + 6] for i in range(8)]
    g_hidden_in = gw[1, :24].reshape(4, 6, 16, 48).transpose(1, 2, 0, 3).reshape(6, 4 * D)
    return (bo[:, None], gi[:, None], ge[:, None, :375],
            gv[0], gv[1], m[0], gv[2], m[1], m[2], gv[3], m[3], gv[4],
            gv[5], gv[6], m[4], gv[7], m[5], m[6], gv[8], m[7], gv[9],
            gv[10], gv[11], g_hidden_in, gs[0, 78:102], gw[1, 24:], gv[12])


def solution(mesh):
    rows = P(None, "win", "seq", None)
    vector, matrix = P(("win", "seq")), P(("win", "seq"), None)
    kinds = "vvmvmmvmvvvmvmmvmvvvmvmv"
    weights = tuple(matrix if kind == "m" else vector for kind in kinds)
    in_specs = (rows, rows, P(None, "win", None), P(None, "win", None), rows) + weights
    return jax.shard_map(per_device, mesh=mesh, in_specs=in_specs, out_specs=(rows, rows, rows) + weights, check_vma=False)
```

time: 3840 us -> 489 us (0.13)
  waiting for transfers between devices: 2010 us -> 0 us
  blocking collectives: 577 us -> 0 us
  starting transfers between devices: 545 us -> 0 us
  local copies, waits for them, and re-layouts: 424 us -> 60.9 us
  Pallas kernels: 0 us -> 199 us
    all_gather x14 -> x0, waiting for transfers between devices: 1820 us -> none  [the longest x1 192 us: per_device(): lax.all_gather(cross_query, ('win', 'seq'), axis=0, tiled=True)]
    unnamed x230 -> x0, starting transfers between devices: 544 us -> none
    unnamed x3 -> x0, blocking collectives: 537 us -> none
    unnamed x871 -> x268, local copies, waits for them, and re-layouts: 360 us -> 16 us
    pallas_call x0 -> x2, Pallas kernels: none -> 199 us  [the longest x1 112 us: gather_all(): pl.pallas_call(gather_kernel, out_shape=[jax.ShapeDtypeStruct((16, D, D),...]
    unnamed x251 -> x0, waiting for transfers between devices: 196 us -> none
    all_gather x4 -> x0, blocking collectives: 39.7 us -> none  [the longest x2 20 us: layer_pass(): lax.all_gather(values_own, 'seq', axis=1, tiled=True)]
    dot_general x84 -> x60, matrix products: 185 us -> 182 us  [the longest x16 44.2 us: dot(): return jnp.dot(a, b, preferred_element_type=f32)]
  transfers between devices with their start and end apart: 245 -> 0, of which waited for: 19 -> 0; matrix products, arithmetic and copies ran while one was open for 25% -> 0% of each run, Pallas kernels for 0% -> 0%
where the time goes in v1:
time: 489 us; the launch traced here: 480 us
  Pallas kernels  199 us (41%)
  matrix products  182 us (37%)
  local copies, waits for them, and re-layouts  60.9 us (12%)
  other arithmetic  34.9 us (7%)
    pallas_call x1, Pallas kernels, gather_all(): pl.pallas_call(gather_kernel, out_shape=[jax.ShapeDtypeStruct((16, D, D),...  112 us
    pallas_call x1, Pallas kernels, reduce_all(): pl.pallas_call(reduce_kernel, out_shape=[jax.ShapeDtypeStruct((2, 48, D),...  87 us
    dot_general x16, matrix products, dot(): return jnp.dot(a, b, preferred_element_type=f32)  44.2 us
    dot_general x16, matrix products, dot_back(): lax.dot_general(a, b, (((1,), (1,)), ((), ())), preferred_element_type=f32)  43.8 us
    dot_general x16, matrix products, dot_grad(): lax.dot_general(a, b, (((0,), (0,)), ((), ())), preferred_element_type=f32)  28.9 us
    dot_general x2, matrix products, attend_back(): jnp.einsum('qhe,khe->hqk', heads(g), heads(v), preferred_element_type=f32)  20.8 us
    unnamed x268, local copies, waits for them, and re-layouts  16 us
    dot_general x2, matrix products, attend(): jnp.einsum('hqk,khe->qhe', (p / total).astype(bf), heads(v), preferred_el...  14.4 us

profile of v1, /device:TPU:1, one launch (start us, length us, event | category | flops | bytes accessed | tf_op | source)
XLA Modules:
  0.0 479.7 jit_solution(6677746775713199428)
XLA Ops:
  5.7 111.8 %gather_all.1 = (bf16[16,768,768]{2,1,0:T(8,128)(2,1)}, bf16[16,16,128]{2,1,0:T(8,128)(2,1)S(1)}, bf16[4,112,768]{2,1,0:T(8,128)(2,1)S(1)}, bf16[4,384,768]{2,1,0:T(8,128)(2,1)S(1)}, bf16[2,112,768]{2,1,0:T(8,128)(2,1)S(1)}) custom-call(bf16[112,768]{1,0:T(8,128)(2,1)S(1)} %concatenate.17.shard, bf16[2,112,768]{2,1,0:T(8,128)(2,1)S(1)} %bitcast.392, ...), custom_call_target="tpu_custom_call" | custom-call | tf_op jit(solution)/shard_map/gather_all/pallas_call | solution.py:191
  136.9 5.0 %fusion.54 = bf16[12,64,224]{2,1,0:T(8,128)(2,1)} fusion(bf16[448,12,64]{0,2,1:T(8,128)(2,1)S(1)} %bitcast.417, f32[12,224,448]{2,1,0:T(8,128)} %copy-done.6, f32[12,224]{1,0:T(8,128)S(1)} %fusion.6, f32[12,224]{1,0:T(8,128)S(1)} %get-tuple-element.192), kind=kOutput, calls=%fused_computation.111 | convolution fusion | flops 157925376 | bytes 5870592 | tf_op jit(solution)/shard_map/hqk,khe->qhe/dot_general | solution.py:464
  155.6 3.4 convolution_convert_fusion
  159.0 7.3 %fusion.183 = (f32[12,224]{1,0:T(8,128)S(1)}, f32[12,224,1536]{2,1,0:T(8,128)}) fusion(bf16[224,12,64]{0,2,1:T(8,128)(2,1)S(1)} %bitcast.406, bf16[1536,12,64]{0,2,1:T(8,128)(2,1)S(1)} %bitcast.400, pred[224,1536]{1,0:T(8,128)(4,1)S(1)} %broadcast_compare_fusion), kind=kOutput, calls=%fused_computation.350 | convolution fusion | flops 540865920 | bytes 19573248 | tf_op jit(solution)/shard_map/qhe,khe->hqk/dot_general | solution.py:459
  166.3 8.7 %fusion = f32[12,224]{1,0:T(8,128)} fusion(f32[12,224,1536]{2,1,0:T(8,128)} %get-tuple-element.197, f32[12,224]{1,0:T(8,128)S(1)} %get-tuple-element.196), kind=kLoop, calls=%fused_computation.6 | loop fusion | flops 8254848 | bytes 16536576 | tf_op jit(solution)/shard_map/reduce_sum | solution.py:463
  175.3 3.4 add_convert_fusion.1
  178.7 9.3 %fusion.57 = bf16[12,64,224]{2,1,0:T(8,128)(2,1)} fusion(bf16[1536,12,64]{0,2,1:T(8,128)(2,1)S(1)} %bitcast.424, f32[12,224,1536]{2,1,0:T(8,128)} %get-tuple-element.197, f32[12,224]{1,0:T(8,128)S(1)} %copy-done.72, f32[12,224]{1,0:T(8,128)S(1)} %copy-done.66), kind=kOutput, calls=%fused_computation.114 | convolution fusion | flops 541040640 | bytes 19239936 | tf_op jit(solution)/shard_map/hqk,khe->qhe/dot_general | solution.py:464
  195.0 3.9 multiply_convert_fusion.4
  198.9 3.3 convert_reduce_fusion.5
  202.2 3.9 multiply_convert_fusion.5
  206.1 3.3 convert_reduce_fusion.6
  209.5 3.9 multiply_convert_fusion.6
  213.3 3.2 convert_reduce_fusion.7
  216.7 3.9 multiply_convert_fusion.7
  238.6 15.8 %multiply_reduce_fusion = (f32[12,224]{1,0:T(8,128)S(1)}, f32[12,224,1536]{2,1,0:T(8,128)}) fusion(f32[12,224,1536]{2,1,0:T(8,128)} %get-tuple-element.197, f32[12,224]{1,0:T(8,128)S(1)} %log_add_fusion, bf16[224,12,64]{0,2,1:T(8,128)(2,1)} %bitcast.409, bf16[1536,12,64]{0,2,1:T(8,128)(2,1)} %bitcast.425), kind=kOutput, calls=%fused_computation.1 | convolution fusion | flops 540865920 | bytes 35755008 | tf_op jit(solution)/shard_map/qhe,khe->hqk/dot_general | solution.py:471
  254.4 11.7 %multiply_convert_fusion = bf16[12,224,1536]{2,1,0:T(8,128)(2,1)S(1)} fusion(f32[12,224,1536]{2,1,0:T(8,128)} %get-tuple-element.206, f32[12,224,1536]{2,1,0:T(8,128)} %get-tuple-element.197, f32[12,224]{1,0:T(8,128)S(1)} %get-tuple-element.205, f32[12,224]{1,0:T(8,128)S(1)} %log_add_fusion), kind=kLoop, calls=%fused_computation | loop fusion | flops 16515072 | bytes 41309184 | tf_op jit(solution)/shard_map/convert_element_type | solution.py:472
  266.2 3.3 convert_reduce_fusion.3
  278.7 5.0 %multiply_reduce_fusion.1 = (f32[12,224]{1,0:T(8,128)S(1)}, f32[12,224,448]{2,1,0:T(8,128)S(1)}) fusion(f32[12,224,448]{2,1,0:T(8,128)} %copy-done.6, f32[12,224]{1,0:T(8,128)S(1)} %log_add_fusion.1, bf16[224,12,64]{0,2,1:T(8,128)(2,1)} %bitcast.411, bf16[448,12,64]{0,2,1:T(8,128)(2,1)} %bitcast.418), kind=kOutput, calls=%fused_computation.12 | convolution fusion | flops 157750656 | bytes 10687488 | tf_op jit(solution)/shard_map/qhe,khe->hqk/dot_general | solution.py:471
  309.3 9.9 %convert_reduce_fusion = (f32[12,64]{1,0:T(8,128)S(1)}, bf16[12,64,1536]{2,1,0:T(8,128)(2,1)}) fusion(bf16[224,12,64]{0,2,1:T(8,128)(2,1)S(1)} %bitcast.410, f32[12,224,1536]{2,1,0:T(8,128)} %get-tuple-element.197, f32[12,224]{1,0:T(8,128)S(1)} %log_add_fusion), kind=kOutput, calls=%fused_computation.19 | convolution fusion | flops 540278016 | bytes 19232256 | tf_op jit(solution)/shard_map/hqk,qhe->khe/dot_general | solution.py:475
  338.9 4.9 %multiply_convert_fusion.2 = bf16[12,64,1536]{2,1,0:T(8,128)(2,1)S(1)} fusion(bf16[224,12,64]{0,2,1:T(8,128)(2,1)S(1)} %bitcast.407, bf16[12,224,1536]{2,1,0:T(8,128)(2,1)} %copy-done.7), kind=kOutput, calls=%fused_computation.20 | convolution fusion | flops 530841600 | bytes 10960896 | tf_op jit(solution)/shard_map/hqk,qhe->khe/dot_general | solution.py:474
  343.8 3.7 fusion.84
  347.6 5.0 %add_convert_fusion = bf16[1536,768]{1,0:T(8,128)(2,1)} fusion(f32[1536,768]{1,0:T(8,128)S(1)} %fusion.84, bf16[1536,768]{0,1:T(8,128)(2,1)S(1)} %bitcast.422, bf16[16,768,768]{2,1,0:T(8,128)(2,1)} %get-tuple-element.39), kind=kOutput, calls=%fused_computation.18 | convolution fusion | flops 1814298624 | bytes 10616832 | tf_op jit(solution)/shard_map/dot_general | solution.py:447
  381.7 87.0 %reduce_all.1 = (f32[2,48,768]{2,1,0:T(8,128)}, f32[8,128]{1,0:T(8,128)}, bf16[2,112,768]{2,1,0:T(8,128)(2,1)}, f32[2,112,768]{2,1,0:T(8,128)}, f32[2,384,768]{2,1,0:T(8,128)}) custom-call(bf16[16,768,768]{2,1,0:T(8,128)(2,1)} %fusion.46.G, f32[4,4,8,128]{3,2,1,0:T(8,128)} %maximum_maximum_fusion.SG, bf16[2,112,768]{2,1,0:T(8,128)(2,1)} %bitcast.431, ...), custom_call_target="tpu_custom_call" | custom-call | tf_op jit(solution)/shard_map/reduce_all/pallas_call | solution.py:409
  470.5 3.8 copy.142
  (450 shorter events, 152.6 us)
Async XLA Ops:
  0.7 154.5 %copy-start = (s32[2,1,1500]{2,1,0:T(1,128)S(1)}, s32[2,1,1500]{2,1,0:T(1,128)}, u32[]{:S(2)}) copy-start(s32[2,1,1500]{2,1,0:T(1,128)} %param.32) | copy-start | bytes 36004
  119.9 5.7 %copy-start.24 = (f32[448,768]{1,0:T(8,128)}, f32[448,768]{1,0:T(8,128)S(1)}, u32[]{:S(2)}) copy-start(f32[448,768]{1,0:T(8,128)S(1)} %subtract_multiply_fusion.1) | copy-start | bytes 4128772
  121.1 176.2 %copy-start.68 = (f32[768]{0:T(1024)}, f32[768]{0:T(1024)S(1)}, u32[]{:S(2)}) copy-start(f32[768]{0:T(1024)S(1)} %mul.321) | copy-start | bytes 9220
  125.3 5.4 %copy-start.31 = (bf16[224,768]{0,1:T(8,128)(2,1)}, bf16[224,768]{0,1:T(8,128)(2,1)S(1)}, u32[]{:S(2)}) copy-start(bf16[224,768]{0,1:T(8,128)(2,1)S(1)} %copy.109) | copy-start | bytes 1032196
  145.3 10.3 %copy-start.5 = (bf16[4,384,768]{2,1,0:T(8,128)(2,1)S(1)}, bf16[4,384,768]{2,1,0:T(8,128)(2,1)}, u32[]{:S(2)}) copy-start(bf16[4,384,768]{2,1,0:T(8,128)(2,1)} %copy-done.4) | copy-start | bytes 7077892
  159.0 7.3 %copy-start.17 = (bf16[1536,768]{0,1:T(8,128)(2,1)}, bf16[1536,768]{0,1:T(8,128)(2,1)S(1)}, u32[]{:S(2)}) copy-start(bf16[1536,768]{0,1:T(8,128)(2,1)S(1)} %convolution_convert_fusion) | copy-start | bytes 7077892
  166.3 8.7 %copy-start.65 = (f32[12,224]{1,0:T(8,128)}, f32[12,224]{1,0:T(8,128)S(1)}, u32[]{:S(2)}) copy-start(f32[12,224]{1,0:T(8,128)S(1)} %get-tuple-element.196) | copy-start | bytes 32260
  166.3 8.7 %copy-start.92 = (f32[1,128,6]{1,2,0:T(8,128)S(1)}, f32[1,128,6]{1,2,0:T(8,128)}, u32[]{:S(2)}) copy-start(f32[1,128,6]{1,2,0:T(8,128)} %get-tuple-element.173) | copy-start | bytes 9220
  178.7 9.4 %copy-start.39 = (bf16[1536,768]{0,1:T(8,128)(2,1)}, bf16[1536,768]{0,1:T(8,128)(2,1)S(1)}, u32[]{:S(2)}) copy-start(bf16[1536,768]{0,1:T(8,128)(2,1)S(1)} %add_convert_fusion.1) | copy-start | bytes 7077892
  178.7 9.4 %copy-start.91 = (f32[1,128,6]{1,2,0:T(8,128)S(1)}, f32[1,128,6]{1,2,0:T(8,128)}, u32[]{:S(2)}) copy-start(f32[1,128,6]{1,2,0:T(8,128)} %get-tuple-element.169) | copy-start | bytes 9220
  232.4 6.2 %copy-start.67 = (f32[12,224]{1,0:T(8,128)S(1)}, f32[12,224]{1,0:T(8,128)}, u32[]{:S(2)}) copy-start(f32[12,224]{1,0:T(8,128)} %copy-done.65) | copy-start | bytes 32260
  232.4 6.2 %copy-start.73 = (f32[12,224]{1,0:T(8,128)S(1)}, f32[12,224]{1,0:T(8,128)}, u32[]{:S(2)}) copy-start(f32[12,224]{1,0:T(8,128)} %fusion) | copy-start | bytes 32260
  254.4 11.7 %copy-start.18 = (bf16[1536,768]{0,1:T(8,128)(2,1)S(1)}, bf16[1536,768]{0,1:T(8,128)(2,1)}, u32[]{:S(2)}) copy-start(bf16[1536,768]{0,1:T(8,128)(2,1)} %copy-done.17) | copy-start | bytes 7077892
  272.4 6.2 %copy-start.71 = (f32[12,224]{1,0:T(8,128)S(1)}, f32[12,224]{1,0:T(8,128)}, u32[]{:S(2)}) copy-start(f32[12,224]{1,0:T(8,128)} %copy-done.70) | copy-start | bytes 32260
  303.5 5.8 %copy-start.29 = (bf16[224,768]{0,1:T(8,128)(2,1)S(1)}, bf16[224,768]{0,1:T(8,128)(2,1)}, u32[]{:S(2)}) copy-start(bf16[224,768]{0,1:T(8,128)(2,1)} %copy.121) | copy-start | bytes 1032196
  309.3 11.7 %copy-start.85 = (f32[768]{0:T(1024)S(1)}, f32[768]{0:T(1024)}, u32[]{:S(2)}) copy-start(f32[768]{0:T(1024)} %get-tuple-element.146) | copy-start | bytes 9220
  309.3 15.4 %copy-start.76 = (f32[12,64]{1,0:T(8,128)S(1)}, f32[12,64]{1,0:T(8,128)}, u32[]{:S(2)}) copy-start(f32[12,64]{1,0:T(8,128)} %get-tuple-element.222) | copy-start | bytes 9220
  309.3 16.2 %copy-start.84 = (f32[768]{0:T(1024)S(1)}, f32[768]{0:T(1024)}, u32[]{:S(2)}) copy-start(f32[768]{0:T(1024)} %get-tuple-element.144) | copy-start | bytes 9220
  309.3 18.5 %copy-start.113 = (f32[768]{0:T(1024)S(1)}, f32[768]{0:T(1024)}, u32[]{:S(2)}) copy-start(f32[768]{0:T(1024)} %get-tuple-element.138) | copy-start | bytes 9220
  319.2 19.7 %copy-start.28 = (bf16[224,768]{0,1:T(8,128)(2,1)S(1)}, bf16[224,768]{0,1:T(8,128)(2,1)}, u32[]{:S(2)}) copy-start(bf16[224,768]{0,1:T(8,128)(2,1)} %copy.117) | copy-start | bytes 1032196
  470.5 6.2 %copy-start.103 = (f32[8,128]{1,0:T(8,128)S(1)}, f32[8,128]{1,0:T(8,128)}, u32[]{:S(2)}) copy-start(f32[8,128]{1,0:T(8,128)} %get-tuple-element.45) | copy-start | bytes 12292
  470.5 7.4 %copy-start.53 = (bf16[2,112,768]{2,1,0:T(8,128)(2,1)S(1)}, bf16[2,112,768]{2,1,0:T(8,128)(2,1)}, u32[]{:S(2)}) copy-start(bf16[2,112,768]{2,1,0:T(8,128)(2,1)} %get-tuple-element.42) | copy-start | bytes 1032196
  470.5 8.2 %copy-start.46 = (f32[2,112,768]{2,1,0:T(8,128)S(1)}, f32[2,112,768]{2,1,0:T(8,128)}, u32[]{:S(2)}) copy-start(f32[2,112,768]{2,1,0:T(8,128)} %get-tuple-element.43) | copy-start | bytes 2064388
  470.5 9.0 %copy-start.1 = (s32[2,1,1500]{2,1,0:T(1,128)S(1)}, s32[2,1,1500]{2,1,0:T(1,128)}, u32[]{:S(2)}) copy-start(s32[2,1,1500]{2,1,0:T(1,128)} %param.32) | copy-start | bytes 36004
  (108 other events, 310.1 us)

commit v2 on v1

--- a/solution.py
+++ b/solution.py
@@ -426,7 +426,23 @@
     )(G, SG, BO, PI, EP)
 
 
-def layer_norm(values):
+WIDE = 12 * HEAD_DIM
+KEYS, FRAMES, SPAN = 448, 1536, 224
+
+
+def dot(a, b):
+    return jnp.dot(a, b, preferred_element_type=f32)
+
+
+def dot_back(a, b):
+    return lax.dot_general(a, b, (((1,), (1,)), ((), ())), preferred_element_type=f32)
+
+
+def dot_grad(a, b):
+    return lax.dot_general(a, b, (((0,), (0,)), ((), ())), preferred_element_type=f32)
+
+
+def normed(values):
     mean = jnp.mean(values, -1, keepdims=True)
     centered = values - mean
     spread = jnp.mean(centered * centered, -1, keepdims=True)
@@ -439,121 +455,226 @@
     return r * (eg - jnp.mean(eg, -1, keepdims=True) - n * jnp.mean(eg * n, -1, keepdims=True))
 
 
-def dot(a, b):
-    return jnp.dot(a, b, preferred_element_type=f32)
-
-
-def dot_back(a, b):
-    return lax.dot_general(a, b, (((1,), (1,)), ((), ())), preferred_element_type=f32)
-
-
-def dot_grad(a, b):
-    return lax.dot_general(a, b, (((0,), (0,)), ((), ())), preferred_element_type=f32).astype(bf)
-
-
-def heads(v):
-    return v.reshape(v.shape[0], HEADS, HEAD_DIM)
-
-
-def attend(q, k, v, allowed):
-    s = jnp.einsum("qhe,khe->hqk", heads(q), heads(k), preferred_element_type=f32) * SCALE
-    s = jnp.where(allowed[None], s, BLOCKED)
-    top = jnp.max(s, -1, keepdims=True)
-    p = jnp.exp(s - top)
-    total = jnp.sum(p, -1, keepdims=True)
-    mixed = jnp.einsum("hqk,khe->qhe", (p / total).astype(bf), heads(v), preferred_element_type=f32)
-    return mixed.reshape(q.shape).astype(bf), top + jnp.log(total)
-
-
-def attend_back(q, k, v, allowed, log_total, g):
-    s = jnp.einsum("qhe,khe->hqk", heads(q), heads(k), preferred_element_type=f32) * SCALE
-    p = jnp.exp(jnp.where(allowed[None], s, BLOCKED) - log_total)
-    dp = jnp.einsum("qhe,khe->hqk", heads(g), heads(v), preferred_element_type=f32)
-    ds = (p * (dp - jnp.sum(p * dp, -1, keepdims=True))).astype(bf)
-    gq = jnp.einsum("hqk,khe->qhe", ds, heads(k), preferred_element_type=f32) * SCALE
-    gk = jnp.einsum("hqk,qhe->khe", ds, heads(q), preferred_element_type=f32) * SCALE
-    gv = jnp.einsum("hqk,qhe->khe", p.astype(bf), heads(g), preferred_element_type=f32)
-    return gq.reshape(q.shape).astype(bf), gk.reshape(k.shape).astype(bf), gv.reshape(k.shape).astype(bf)
+def row_sum(v):
+    return jnp.sum(v, 0, keepdims=True)
+
+
+def one_head(v, e):
+    at = lax.broadcasted_iota(jnp.int32, v.shape, 1)
+    return jnp.where((at < 64) if e == 0 else (at >= 64), v, jnp.zeros_like(v))
+
+
+def two_heads(a, b):
+    at = lax.broadcasted_iota(jnp.int32, a.shape, 1)
+    return jnp.where(at < 64, a, b)
+
+
+def attend(q, k, v, bias, mixed, lse):
+    @pl.loop(0, 6)
+    def _(j):
+        at = pl.ds(pl.multiple_of(j * 128, 128), 128)
+        qp, kp, vp = q[:, at], k[:, at], v[:, at]
+        outs, logs = [], []
+        for e in (0, 1):
+            s = dot_back(one_head(qp, e), kp) + bias[...]
+            top = jnp.max(s, 1, keepdims=True)
+            p = jnp.exp(s - top)
+            total = jnp.sum(p, 1, keepdims=True)
+            outs.append(dot(p.astype(bf), vp) / total)
+            logs.append(top + jnp.log(total))
+        mixed[:, at] = two_heads(*outs).astype(bf)
+        lse[j] = two_heads(*[jnp.broadcast_to(log, (SPAN, 128)) for log in logs])
+
+
+def attend_back(q, k, v, bias, mixed, lse, g, gq, gk, gv):
+    @pl.loop(0, 6)
+    def _(j):
+        at = pl.ds(pl.multiple_of(j * 128, 128), 128)
+        qp, kp, vp, gp = q[:, at], k[:, at], v[:, at], g[:, at]
+        product = gp.astype(f32) * mixed[:, at].astype(f32)
+        dq, dk, dv = [], 0.0, 0.0
+        for e in (0, 1):
+            qe, ge = one_head(qp, e), one_head(gp, e)
+            s = dot_back(qe, kp) + bias[...]
+            p = jnp.exp(s - lse[j, :, 64 * e:64 * e + 1])
+            dp = dot_back(ge, vp)
+            delta = jnp.sum(one_head(product, e), 1, keepdims=True)
+            ds = (p * (dp - delta)).astype(bf)
+            dk = dk + dot_grad(ds, qe)
+            dv = dv + dot_grad(p.astype(bf), ge)
+            dq.append(dot(ds, kp) * SCALE)
+        gk[:, at] = dk.astype(bf)
+        gv[:, at] = dv.astype(bf)
+        gq[:, at] = two_heads(*dq).astype(bf)
+
+
+def blocks(total, step, body):
+    @pl.loop(0, total // step)
+    def _(i):
+        body(pl.ds(pl.multiple_of(i * step, step), step))
+
+
+def layer_kernel(W, vec, hib, tok, enc_hbm, og, qcol, krow, crow, G, BO, PI, EP, gvec, ghib,
+                 w, enc, first, q, k, v, mixed, lse, second, cq, ck, cv, cmixed, clse, after_self, stream, third,
+                 acc, bias_s, bias_c, g, gq, gk, gv, gck, gcv, wide, wsem, gsem, esem):
+    core = lax.rem(lax.axis_index("seq"), 2)
+    mine = pl.ds(pl.multiple_of(core * SPAN, 32), SPAN)
+    loads, stores = {}, {}
+    enc_load = pltpu.make_async_copy(enc_hbm, enc, esem)
+    for u in (1, 2, 0, 3, 4, 5, 6, 7, 8, 12, 9, 13, 10, 14, 11, 15):
+        loads[u] = pltpu.make_async_copy(W.at[u], w.at[u], wsem.at[u])
+        loads[u].start()
+        if u == 3:
+            enc_load.start()
+
+    def ready(u):
+        loads[u].wait()
+        return w.at[u]
+
+    def put(u):
+        stores[u] = pltpu.make_async_copy(w.at[u], G.at[u], gsem.at[u])
+        stores[u].start()
+
+    def weight_grad(u, a, b):
+        def body(at):
+            w[u, :, at] = dot_grad(a[...], b[:, at]).astype(bf)
+        blocks(D, 256, body)
+        put(u)
+
+    same = qcol[...] == krow[...]
+    key_at = lax.broadcasted_iota(jnp.int32, (SPAN, KEYS), 1)
+    query_at = lax.broadcasted_iota(jnp.int32, (SPAN, KEYS), 0) + core * SPAN
+    bias_s[...] = jnp.where(same & (key_at <= query_at), 0.0, BLOCKED)
+    bias_c[...] = jnp.where(qcol[...] == crow[...], 0.0, BLOCKED)
+
+    def norm_first(at):
+        n, _ = normed(tok[at].astype(f32))
+        first[at] = (n * vec[0:1] + vec[1:2]).astype(bf)
+    blocks(KEYS, 112, norm_first)
+    wk = ready(1)
+
+    def keys(at):
+        k[at] = dot(first[at], wk[...]).astype(bf)
+    blocks(KEYS, SPAN, keys)
+    wv = ready(2)
+
+    def values(at):
+        v[at] = (dot(first[at], wv[...]) + vec[3:4]).astype(bf)
+    blocks(KEYS, SPAN, values)
+    wq = ready(0)
+    q[...] = (dot(first[mine], wq[...]) + vec[2:3]).astype(bf) * SCALE
+    attend(q, k, v, bias_s, mixed, lse)
+    wo = ready(3)
+    after_self[...] = tok[mine].astype(f32) + dot(mixed[...], wo[...]) + vec[4:5]
+    n, _ = normed(after_self[...])
+    second[...] = (n * vec[5:6] + vec[6:7]).astype(bf)
+    wcq = ready(4)
+    cq[...] = (dot(second[...], wcq[...]) + vec[7:8]).astype(bf) * SCALE
+    enc_load.wait()
+    wck = ready(5)
+
+    def cross_keys(at):
+        ck[at] = dot(enc[at], wck[...]).astype(bf)
+    blocks(FRAMES, 384, cross_keys)
+    wcv = ready(6)
+
+    def cross_values(at):
+        cv[at] = (dot(enc[at], wcv[...]) + vec[8:9]).astype(bf)
+    blocks(FRAMES, 384, cross_values)
+    attend(cq, ck, cv, bias_c, cmixed, clse)
+    wco = ready(7)
+    stream[...] = after_self[...] + dot(cmixed[...], wco[...]) + vec[9:10]
+    n, r = normed(stream[...])
+    third[...] = (n * vec[10:11] + vec[11:12]).astype(bf)
+    acc[0] = stream[...] + vec[12:13]
+    acc[1] = jnp.zeros((SPAN, D), f32)
+    for i in range(4):
+        w1, w2 = ready(8 + i), ready(12 + i)
+        pre = dot(third[...], w1[...]) + hib[i:i + 1]
+        cdf = 0.5 * (1.0 + lax.erf(pre * 0.7071067811865476))
+        act = (pre * cdf).astype(bf)
+        slope = cdf + pre * (0.3989422804014327 * jnp.exp(-0.5 * pre * pre))
+        wide[0] = act
+        acc[0] += dot(act, w2[...])
+        g_pre = (dot_back(og[...], w2[...]) * slope).astype(bf)
+        wide[1] = g_pre
+        weight_grad(12 + i, wide.at[0], og)
+        ghib[i:i + 1] = row_sum(g_pre.astype(f32))
+        acc[1] += dot_back(g_pre, w1[...])
+        weight_grad(8 + i, third, wide.at[1])
+    BO[...] = acc[0].astype(bf)
+    e = acc[1]
+    ogf = og[...].astype(f32)
+    n, r = normed(stream[...])
+    gvec[12:13] = row_sum(ogf)
+    gvec[10:11] = row_sum(e * n)
+    gvec[11:12] = row_sum(e)
+    stream[...] = ogf + norm_back(e, n, r, vec[10:11])
+    wide[0] = stream[...].astype(bf)
+    gvec[9:10] = row_sum(wide[0].astype(f32))
+    g[...] = dot_back(wide[0], wco[...]).astype(bf)
+    weight_grad(7, cmixed, wide.at[0])
+    attend_back(cq, ck, cv, bias_c, cmixed, clse, g, gq, gck, gcv)
+    gvec[7:8] = row_sum(gq[...].astype(f32))
+    gvec[8:9] = row_sum(gcv[...].astype(f32))
+
+    def frames_back(at):
+        EP[at] = (dot_back(gck[at], wck[...]) + dot_back(gcv[at], wcv[...])).astype(bf)
+    blocks(FRAMES, 384, frames_back)
+    weight_grad(5, enc, gck)
+    weight_grad(6, enc, gcv)
+    e = dot_back(gq[...], wcq[...])
+    weight_grad(4, second, gq)
+    n, r = normed(after_self[...])
+    gvec[5:6] = row_sum(e * n)
+    gvec[6:7] = row_sum(e)
+    stream[...] += norm_back(e, n, r, vec[5:6])
+    wide[0] = stream[...].astype(bf)
+    gvec[4:5] = row_sum(wide[0].astype(f32))
+    g[...] = dot_back(wide[0], wo[...]).astype(bf)
+    weight_grad(3, mixed, wide.at[0])
+    attend_back(q, k, v, bias_s, mixed, lse, g, gq, gk, gv)
+    gvec[2:3] = row_sum(gq[...].astype(f32))
+    gvec[3:4] = row_sum(gv[...].astype(f32))
+    gvec[0:2] = jnp.zeros((2, D), f32)
+    acc[0] = dot_back(gq[...], wq[...])
+
+    for h in (0, 1):
+        at = pl.ds(h * SPAN, SPAN)
+        own = core == h
+        e = dot_back(gk[at], wk[...]) + dot_back(gv[at], wv[...]) + jnp.where(own, acc[0], 0.0)
+        n, r = normed(tok[at].astype(f32))
+        gvec[0:1] += row_sum(e * n)
+        gvec[1:2] += row_sum(e)
+        PI[at] = (norm_back(e, n, r, vec[0:1]) + jnp.where(own, stream[...], 0.0)).astype(bf)
+    wide[0] = first[mine]
+    weight_grad(0, wide.at[0], gq)
+    weight_grad(1, first, gk)
+    weight_grad(2, first, gv)
+    for u in range(16):
+        stores[u].wait()
 
 
 def middle(W, vec, hidden_in_bias, tok, enc, og, seg, clip, core):
-    (self_gain, self_shift, bq, bv, bo, cross_gain, cross_shift, bcq, bcv, bco, final_gain, final_shift, bho) = vec
-    half = lax.dynamic_slice_in_dim
-    tokens = tok.reshape(448, D).astype(f32)
-    enc = enc.reshape(1536, D)
-    og = og.reshape(224, D)
-    places = jnp.arange(448, dtype=jnp.int32)
-    my_seg = half(seg, core * 224, 224, 0)
-    my_places = half(places, core * 224, 224, 0)
-    self_allowed = (my_seg[:, None] == seg[None]) & (places[None] <= my_places[:, None])
-    cross_allowed = my_seg[:, None] == clip[None]
-    n1, rs1 = layer_norm(tokens)
-    first = (n1 * self_gain + self_shift).astype(bf)
-    first_q = half(first, core * 224, 224, 0)
-    q = (dot(first_q, W[0]) + bq).astype(bf)
-    k = dot(first, W[1]).astype(bf)
-    v = (dot(first, W[2]) + bv).astype(bf)
-    mixed, total = attend(q, k, v, self_allowed)
-    after_self = half(tokens, core * 224, 224, 0) + dot(mixed, W[3]) + bo
-    n2, rs2 = layer_norm(after_self)
-    second = (n2 * cross_gain + cross_shift).astype(bf)
-    cq = (dot(second, W[4]) + bcq).astype(bf)
-    ck = dot(enc, W[5]).astype(bf)
-    cv = (dot(enc, W[6]) + bcv).astype(bf)
-    cmixed, ctotal = attend(cq, ck, cv, cross_allowed)
-    after_cross = after_self + dot(cmixed, W[7]) + bco
-    n3, rs3 = layer_norm(after_cross)
-    third = (n3 * final_gain + final_shift).astype(bf)
-    acts, g_pres, dW = [], [], [None] * 16
-    g_third = jnp.zeros((224, D), f32)
-    result = after_cross + bho
-    g_hib = []
-    for n in range(4):
-        pre = dot(third, W[8 + n]) + hidden_in_bias[n]
-        act, back = jax.vjp(lambda t: jax.nn.gelu(t, approximate=False), pre)
-        act = act.astype(bf)
-        result = result + dot(act, W[12 + n])
-        dW[12 + n] = dot_grad(act, og)
-        g_pre = back(dot_back(og, W[12 + n]))[0].astype(bf)
-        dW[8 + n] = dot_grad(third, g_pre)
-        g_third = g_third + dot_back(g_pre, W[8 + n])
-        g_hib.append(jnp.sum(g_pre.astype(f32), 0))
-    block_output = result.astype(bf).reshape(2, 112, D)
-    ogf = og.astype(f32)
-    g_bho = jnp.sum(ogf, 0)
-    g_fg, g_fs = jnp.sum(g_third * n3, 0), jnp.sum(g_third, 0)
-    g_cross = ogf + norm_back(g_third, n3, rs3, final_gain)
-    branch = g_cross.astype(bf)
-    dW[7] = dot_grad(cmixed, branch)
-    g_bco = jnp.sum(branch.astype(f32), 0)
-    g_cmixed = dot_back(branch, W[7]).astype(bf)
-    gcq, gck, gcv = attend_back(cq, ck, cv, cross_allowed, ctotal, g_cmixed)
-    dW[5] = dot_grad(enc, gck)
-    dW[6] = dot_grad(enc, gcv)
-    g_bcv = jnp.sum(gcv.astype(f32), 0)
-    enc_grad = (dot_back(gck, W[5]) + dot_back(gcv, W[6])).astype(bf).reshape(4, 384, D)
-    dW[4] = dot_grad(second, gcq)
-    g_bcq = jnp.sum(gcq.astype(f32), 0)
-    e2 = dot_back(gcq, W[4])
-    g_cg, g_cs = jnp.sum(e2 * n2, 0), jnp.sum(e2, 0)
-    g_self = g_cross + norm_back(e2, n2, rs2, cross_gain)
-    branch = g_self.astype(bf)
-    dW[3] = dot_grad(mixed, branch)
-    g_bo = jnp.sum(branch.astype(f32), 0)
-    g_mixed = dot_back(branch, W[3]).astype(bf)
-    gq, gk, gv = attend_back(q, k, v, self_allowed, total, g_mixed)
-    dW[0] = dot_grad(first_q, gq)
-    dW[1] = dot_grad(first, gk)
-    dW[2] = dot_grad(first, gv)
-    g_bq, g_bv = jnp.sum(gq.astype(f32), 0), jnp.sum(gv.astype(f32), 0)
-    e1 = dot_back(gk, W[1]) + dot_back(gv, W[2])
-    e1 = lax.dynamic_update_slice_in_dim(e1, half(e1, core * 224, 224, 0) + dot_back(gq, W[0]), core * 224, 0)
-    g_sg, g_ss = jnp.sum(e1 * n1, 0), jnp.sum(e1, 0)
-    g_in = norm_back(e1, n1, rs1, self_gain)
-    g_in = lax.dynamic_update_slice_in_dim(g_in, half(g_in, core * 224, 224, 0) + g_self, core * 224, 0)
-    input_grad = g_in.astype(bf).reshape(4, 112, D)
-    g_vec = jnp.stack([g_sg, g_ss, g_bq, g_bv, g_bo, g_cg, g_cs, g_bcq, g_bcv, g_bco, g_fg, g_fs, g_bho])
-    return block_output, input_grad, enc_grad, jnp.stack(dW), g_vec, jnp.stack(g_hib)
+    V, DMA, S = pltpu.VMEM, pltpu.SemaphoreType.DMA, jax.ShapeDtypeStruct
+    vec = jnp.pad(vec, ((0, 3), (0, 0)))
+    qcol = lax.dynamic_slice_in_dim(seg, core * SPAN, SPAN, 0).reshape(SPAN, 1)
+    vm, hbm = pl.BlockSpec(memory_space=pltpu.VMEM), pl.BlockSpec(memory_space=pl.ANY)
+    G, BO, PI, EP, gvec, ghib = pl.pallas_call(
+        layer_kernel,
+        out_shape=[S((16, D, D), bf), S((SPAN, D), bf), S((KEYS, D), bf), S((FRAMES, D), bf), S((16, D), f32), S((4, D), f32)],
+        in_specs=[hbm, vm, vm, vm, hbm, vm, vm, vm, vm], out_specs=[hbm, vm, vm, vm, vm, vm],
+        scratch_shapes=[
+            V((16, D, D), bf), V((FRAMES, D), bf), V((KEYS, D), bf), V((SPAN, D), bf), V((KEYS, D), bf), V((KEYS, D), bf),
+            V((SPAN, D), bf), V((6, SPAN, 128), f32), V((SPAN, D), bf), V((SPAN, D), bf), V((FRAMES, D), bf), V((FRAMES, D), bf),
+            V((SPAN, D), bf), V((6, SPAN, 128), f32), V((SPAN, D), f32), V((SPAN, D), f32), V((SPAN, D), bf),
+            V((2, SPAN, D), f32), V((SPAN, KEYS), f32), V((SPAN, FRAMES), f32), V((SPAN, D), bf), V((SPAN, D), bf),
+            V((KEYS, D), bf), V((KEYS, D), bf), V((FRAMES, D), bf), V((FRAMES, D), bf), V((2, SPAN, D), bf),
+            DMA((16,)), DMA((16,)), DMA],
+        compiler_params=pltpu.CompilerParams(vmem_limit_bytes=60 << 20),
+        name="layer",
+    )(W, vec, hidden_in_bias, tok.reshape(KEYS, D), enc.reshape(FRAMES, D), og.reshape(SPAN, D), qcol, seg[None], clip[None])
+    return BO.reshape(2, 112, D), PI.reshape(4, 112, D), EP.reshape(4, 384, D), G, gvec[:13], ghib
 
 
 def per_device(

time: 489 us -> 316 us (0.65); the launches traced: 480 us -> 312 us
  matrix products: 182 us -> 0 us
  Pallas kernels: 199 us -> 284 us
  local copies, waits for them, and re-layouts: 60.9 us -> 25.8 us
  other arithmetic: 34.9 us -> 0.72 us
    dot_general x60 -> x0, matrix products: 182 us -> none  [the longest x16 44.2 us: dot(): return jnp.dot(a, b, preferred_element_type=f32)]
    pallas_call x0 -> x1, Pallas kernels: none -> 85.2 us  [middle(): pl.pallas_call(layer_kernel, out_shape=[S((16, D, D), bf), S((SPAN, D), b...]
    another operation x45 -> x0, local copies, waits for them, and re-layouts: 20.1 us -> none  [the longest x27 12.6 us: middle(): jnp.stack([g_sg, g_ss, g_bq, g_bv, g_bo, g_cg, g_cs, g_bcq, g_bcv, g_bco,...]
    convert_element_type x6 -> x0, other arithmetic: 16.3 us -> none  [the longest x2 13 us: attend_back(): ds = (p * (dp - jnp.sum(p * dp, -1, keepdims=True))).astype(bf)]
    reduce_sum x10 -> x0, other arithmetic: 14.5 us -> none  [the longest x2 10.4 us: attend(): total = jnp.sum(p, -1, keepdims=True)]
    convert_element_type x6 -> x0, local copies, waits for them, and re-layouts: 8.55 us -> none  [the longest x1 1.95 us: middle(): g_mixed = dot_back(branch, W[3]).astype(bf)]
    unnamed x268 -> x76, local copies, waits for them, and re-layouts: 16 us -> 10.6 us
where the time goes in v2:
time: 316 us; the launch traced here: 312 us
  Pallas kernels  284 us (90%)
  local copies, waits for them, and re-layouts  25.8 us (8%)
    pallas_call x1, Pallas kernels, gather_all(): pl.pallas_call(gather_kernel, out_shape=[jax.ShapeDtypeStruct((16, D, D),...  112 us
    pallas_call x1, Pallas kernels, reduce_all(): pl.pallas_call(reduce_kernel, out_shape=[jax.ShapeDtypeStruct((2, 48, D),...  86.9 us
    pallas_call x1, Pallas kernels, middle(): pl.pallas_call(layer_kernel, out_shape=[S((16, D, D), bf), S((SPAN, D), b...  85.2 us
    unnamed x76, local copies, waits for them, and re-layouts  10.6 us

profile of v2, /device:TPU:1, one launch (start us, length us, event | category | flops | bytes accessed | tf_op | source)
XLA Modules:
  0.0 312.4 jit_solution(3622962275170841924)
XLA Ops:
  0.7 0.8 dynamic-slice_bitcast_fusion.1
  1.5 0.8 copy.69.qcol
  3.0 1.3 dynamic-slice_bitcast_fusion.krow
  4.5 1.5 copy.81
  6.8 0.6 concatenate.15.shard
  7.5 112.0 %gather_all.1 = (bf16[16,768,768]{2,1,0:T(8,128)(2,1)}, bf16[16,16,128]{2,1,0:T(8,128)(2,1)S(1)}, bf16[4,112,768]{2,1,0:T(8,128)(2,1)S(1)}, bf16[4,384,768]{2,1,0:T(8,128)(2,1)S(1)}, bf16[2,112,768]{2,1,0:T(8,128)(2,1)S(1)}) custom-call(bf16[112,768]{1,0:T(8,128)(2,1)S(1)} %concatenate.15.shard, bf16[2,112,768]{2,1,0:T(8,128)(2,1)S(1)} %bitcast.97, ...), custom_call_target="tpu_custom_call" | custom-call | tf_op jit(solution)/shard_map/gather_all/pallas_call | solution.py:191
  119.5 1.4 copy-done.1
  120.9 0.8 copy-done.2
  121.7 0.7 copy-done.3
  123.3 0.6 pad.18.vec
  124.1 0.7 reshape.124.hib
  124.8 85.2 %layer.1 = (bf16[16,768,768]{2,1,0:T(8,128)(2,1)}, bf16[224,768]{1,0:T(8,128)(2,1)}, bf16[448,768]{1,0:T(8,128)(2,1)}, bf16[1536,768]{1,0:T(8,128)(2,1)}, f32[16,768]{1,0:T(8,128)}, /*index=5*/f32[4,768]{1,0:T(4,128)}) custom-call(bf16[16,768,768]{2,1,0:T(8,128)(2,1)} %get-tuple-element.43.W, f32[16,768]{1,0:T(8,128)} %pad.18.vec, f32[4,768]{1,0:T(4,128)} %reshape.124.hib, ...), custom_call_target="tpu_custom_call" | custom-call | tf_op jit(solution)/shard_map/layer/pallas_call | solution.py:663
  210.0 1.6 reshape.129
  211.9 0.8 concatenate.16
  213.4 0.7 maximum_maximum_fusion.SG
  214.1 86.9 %reduce_all.1 = (f32[2,48,768]{2,1,0:T(8,128)}, f32[8,128]{1,0:T(8,128)}, bf16[2,112,768]{2,1,0:T(8,128)(2,1)}, f32[2,112,768]{2,1,0:T(8,128)}, f32[2,384,768]{2,1,0:T(8,128)}) custom-call(bf16[16,768,768]{2,1,0:T(8,128)(2,1)} %get-tuple-element.48.G, f32[4,4,8,128]{3,2,1,0:T(8,128)} %maximum_maximum_fusion.SG, bf16[2,112,768]{2,1,0:T(8,128)(2,1)} %bitcast.107, ...), custom_call_target="tpu_custom_call" | custom-call | tf_op jit(solution)/shard_map/reduce_all/pallas_call | solution.py:409
  301.1 1.8 slice_bitcast_fusion
  302.9 3.8 %copy.76 = f32[2,1,375,768]{3,1,2,0:T(1,128)} copy(f32[2,1,375,768]{3,2,0,1:T(8,128)S(1)} %slice_bitcast_fusion) | data formatting | bytes 4608000
  306.7 0.6 slice_bitcast_fusion.1
  307.6 0.9 reshape.134
  308.4 0.7 slice_bitcast_fusion.2
  309.1 0.6 slice_bitcast_fusion.10
  310.3 0.7 copy.86
  311.1 0.8 copy.87
  (97 shorter events, 4.2 us)
Async XLA Ops:
  2.3 3.8 %copy-start.9 = (bf16[6,3072]{1,0:T(8,128)(2,1)S(1)}, bf16[6,3072]{1,0:T(8,128)(2,1)}, u32[]{:S(2)}) copy-start(bf16[6,3072]{1,0:T(8,128)(2,1)} %param.54) | copy-start | bytes 110596
  4.2 2.2 copy-start.24
  4.2 2.2 copy-start.25
  4.3 2.2 copy-start.26
  4.3 2.2 copy-start.27
  4.3 2.2 copy-start.28
  4.3 2.2 copy-start.29
  4.3 2.2 copy-start.30
  4.4 2.3 copy-start.10
  4.4 2.3 copy-start.11
  4.4 2.3 copy-start.12
  4.4 2.3 copy-start.13
  4.4 2.3 copy-start.14
  4.4 2.3 copy-start.15
  4.4 2.3 copy-start.16
  4.5 2.3 copy-start.17
  4.5 2.3 copy-start.18
  4.5 3.0 copy-start.4
  4.5 3.0 copy-start.5
  210.0 3.1 copy-start.19
  302.9 3.8 %copy-start.7 = (f32[2,48,768]{2,1,0:T(8,128)S(1)}, f32[2,48,768]{2,1,0:T(8,128)}, u32[]{:S(2)}) copy-start(f32[2,48,768]{2,1,0:T(8,128)} %get-tuple-element.58) | copy-start | bytes 884740
  302.9 6.2 %copy-start.20 = (f32[8,128]{1,0:T(8,128)S(1)}, f32[8,128]{1,0:T(8,128)}, u32[]{:S(2)}) copy-start(f32[8,128]{1,0:T(8,128)} %get-tuple-element.57) | copy-start | bytes 12292
  302.9 7.4 %copy-start.8 = (bf16[2,112,768]{2,1,0:T(8,128)(2,1)S(1)}, bf16[2,112,768]{2,1,0:T(8,128)(2,1)}, u32[]{:S(2)}) copy-start(bf16[2,112,768]{2,1,0:T(8,128)(2,1)} %get-tuple-element.54) | copy-start | bytes 1032196
  302.9 8.2 %copy-start.6 = (f32[2,112,768]{2,1,0:T(8,128)S(1)}, f32[2,112,768]{2,1,0:T(8,128)}, u32[]{:S(2)}) copy-start(f32[2,112,768]{2,1,0:T(8,128)} %get-tuple-element.55) | copy-start | bytes 2064388
  (11 other events, 19.8 us)

commit v3 on v2

v3 whole, which is shorter than its diff:
```python
import jax
import jax.numpy as jnp
from jax import lax
from jax.experimental import pallas as pl
from jax.experimental.pallas import tpu as pltpu
from jax.sharding import PartitionSpec as P

bf, f32 = jnp.bfloat16, jnp.float32
HEAD_DIM = 64
EPS = 1e-05
SCALE = 0.125
BLOCKED = -1e30
MESH = pl.DeviceIdType.MESH
D = 768
HALF = D // 2


def coords():
    win, seq = lax.axis_index("win"), lax.axis_index("seq")
    x, y = win // 8, lax.rem(win // 2, 4)
    z = (seq // 2) * 2 + lax.rem(win, 2)
    return x, y, z, lax.rem(seq, 2)


def device_at(x, y, z, core):
    return (x * 8 + y * 2 + lax.rem(z, 2), (z // 2) * 2 + core)


def member(z, core):
    return lax.rem(z, 2) * 4 + (z // 2) * 2 + core


KEYS, FRAMES, SPAN = 448, 1536, 224


def dot(a, b):
    return jnp.dot(a, b, preferred_element_type=f32)


def dot_back(a, b):
    return lax.dot_general(a, b, (((1,), (1,)), ((), ())), preferred_element_type=f32)


def dot_grad(a, b):
    return lax.dot_general(a, b, (((0,), (0,)), ((), ())), preferred_element_type=f32)


def normed(values):
    mean = jnp.mean(values, -1, keepdims=True)
    centered = values - mean
    spread = jnp.mean(centered * centered, -1, keepdims=True)
    r = lax.rsqrt(spread + EPS)
    return centered * r, r


def norm_back(e, n, r, gain):
    eg = e * gain
    return r * (eg - jnp.mean(eg, -1, keepdims=True) - n * jnp.mean(eg * n, -1, keepdims=True))


def row_sum(v):
    return jnp.sum(v, 0, keepdims=True)


def one_head(v, e):
    at = lax.broadcasted_iota(jnp.int32, v.shape, 1)
    return jnp.where((at < 64) if e == 0 else (at >= 64), v, jnp.zeros_like(v))


def two_heads(a, b):
    at = lax.broadcasted_iota(jnp.int32, a.shape, 1)
    return jnp.where(at < 64, a, b)


def attend(q, k, v, bias, mixed, lse, begin, end):
    @pl.loop(begin, end)
    def _(j):
        at = pl.ds(pl.multiple_of(j * 128, 128), 128)
        qp, kp, vp = q[:, at], k[:, at], v[:, at]
        outs, logs = [], []
        for e in (0, 1):
            s = dot_back(one_head(qp, e), kp) + bias[...]
            top = jnp.max(s, 1, keepdims=True)
            p = jnp.exp(s - top)
            total = jnp.sum(p, 1, keepdims=True)
            outs.append(dot(p.astype(bf), vp) / total)
            logs.append(top + jnp.log(total))
        mixed[:, at] = two_heads(*outs).astype(bf)
        lse[j] = two_heads(*[jnp.broadcast_to(log, (SPAN, 128)) for log in logs])


def attend_back(q, k, v, bias, mixed, lse, g, gq, gk, gv, begin, end):
    @pl.loop(begin, end)
    def _(j):
        at = pl.ds(pl.multiple_of(j * 128, 128), 128)
        qp, kp, vp, gp = q[:, at], k[:, at], v[:, at], g[:, at]
        product = gp.astype(f32) * mixed[:, at].astype(f32)
        dq, dk, dv = [], 0.0, 0.0
        for e in (0, 1):
            qe, ge = one_head(qp, e), one_head(gp, e)
            s = dot_back(qe, kp) + bias[...]
            p = jnp.exp(s - lse[j, :, 64 * e:64 * e + 1])
            dp = dot_back(ge, vp)
            delta = jnp.sum(one_head(product, e), 1, keepdims=True)
            ds = (p * (dp - delta)).astype(bf)
            dk = dk + dot_grad(ds, qe)
            dv = dv + dot_grad(p.astype(bf), ge)
            dq.append(dot(ds, kp) * SCALE)
        gk[:, at] = dk.astype(bf)
        gv[:, at] = dv.astype(bf)
        gq[:, at] = two_heads(*dq).astype(bf)


def blocks(total, step, body):
    @pl.loop(0, total // step)
    def _(i):
        body(pl.ds(pl.multiple_of(i * step, step), step))


class Chunk:
    def __init__(self, index, base, out, slot):
        self.index, self.base, self.out, self.slot = index, base, out, slot
        self.sent, self.back = [], []


def one_hot(source, width):
    cols = lax.broadcasted_iota(jnp.int32, (source.shape[0], width), 1)
    return jnp.where(cols == source, 1.0, 0.0).astype(bf)


def spread_matrix(core):
    r = lax.broadcasted_iota(jnp.int32, (96, 1), 0)
    piece, at = r // 48, lax.rem(r, 48)
    return one_hot((at // 6) * 32 + (2 * core + piece) * 6 + lax.rem(at, 6), 256)


def split_matrix():
    r = lax.broadcasted_iota(jnp.int32, (128, 1), 0)
    k, i = r // 16, lax.rem(r, 16)
    return one_hot(jnp.where(i < 12, (i // 6) * 48 + 6 * k + lax.rem(i, 6), -1), 96)


def vector_tables():
    f = lax.broadcasted_iota(jnp.int32, (D, 128), 0)
    c = lax.broadcasted_iota(jnp.int32, (D, 128), 1)
    owner = jnp.where((f >= 6 * c) & (f < 6 * c + 6), 1.0, 0.0).astype(bf)
    inner = jnp.where(lax.rem(f, 6) == lax.rem(c, 6), 1.0, 0.0)
    v = lax.broadcasted_iota(jnp.int32, (16, 128), 0)
    c = lax.broadcasted_iota(jnp.int32, (16, 128), 1)
    which = jnp.where((c >= 6 * v) & (c < 6 * v + 6) & (v < 13), 1.0, 0.0).astype(bf)
    return owner, inner, which


def hidden_tables(n):
    q = lax.broadcasted_iota(jnp.int32, (D, 128), 0)
    c = lax.broadcasted_iota(jnp.int32, (D, 128), 1)
    start = 24 * (c - 32 * n)
    owner = jnp.where((q >= start) & (q < start + 24), 1.0, 0.0).astype(bf)
    inner = jnp.where(c == 78 + lax.rem(q, 24), 1.0, 0.0)
    return owner, inner


def layer_kernel(m0, m1, m2, m3, m4, m5, m6, m7, h_in, h_out, small, tok_in, enc_in, og_in, seg2, clip2,
                 fin, fin2, gs, bo_out, pi_out, ep_out,
                 w, s6, sh1, sh2, zbuf, c2buf, sm, smbuf, tok, enc, og, vec, hib, first, q, k, v, mixed, lse, second, cq, ck, cv,
                 cmixed, clse, after_self, stream, third, acc, bias_s, bias_c, g, gq, wide, gvec, ghib,
                 BO, PI, pib, eib, db, r1, r2, r2b, red, shares, r3, sx, r4, c2sum, c2r, SG, sd, s1b, s2b, s3b,
                 ls, zs, zr, ds, dr, as1, ar1, as2, ar2, cs, cr, ss1, sr1, ss2, sr2, es, er, fs, fr,
                 bds, bdr, b1s, b1r, b2s, b2r, b3s, b3r, b4s, b4r, gss, gsr, ts, tr, os_, credit):
    x, y, z, core = coords()
    hi = z // 2
    other = 1 - core
    s = 1 - 2 * core
    partner = device_at(x, y, z, other)
    across = lax.rem(z + 2, 4)
    home = device_at(x, y, across, core)
    pos = (x, y, z)

    def turn(axis, off):
        return lax.rem(pos[axis] + off + 8, 4)

    def peer(axis, off):
        at = list(pos)
        at[axis] = turn(axis, off)
        return device_at(at[0], at[1], at[2], core)
    xp = [None] + [peer(0, o) for o in (1, 2, 3)]
    yp = [None] + [peer(1, o) for o in (1, 2, 3)]
    zp = [None] + [peer(2, o) for o in (1, 2, 3)]
    near = [partner] + xp[1:] + yp[1:]
    peers = near + [device_at(x, y, across, other)] + zp[1:]
    barrier = pltpu.get_barrier_semaphore()
    for to in peers:
        pl.semaphore_signal(barrier, inc=1, device_id=to, device_id_type=MESH)
    me = member(z, core)
    qm = me // 2
    lanes = pl.ds(pl.multiple_of(core * HALF, 128), HALF)
    lanes_other = pl.ds(pl.multiple_of(other * HALF, 128), HALF)
    halves = (pl.ds(0, HALF), pl.ds(HALF, HALF))
    A, B, C1, C2 = Chunk(0, 0, 8, 0), Chunk(1, 4, 12, 1), Chunk(2, 8, 8, 1), Chunk(3, 12, 12, 0)
    moved = []

    def remote(src, dst, send, recv, to):
        return pltpu.make_async_remote_copy(src_ref=src, dst_ref=dst, send_sem=send, recv_sem=recv,
                                            device_id=to, device_id_type=MESH)

    def start(sent, *a):
        c = remote(*a)
        c.start()
        sent.append(c)

    def arrived(at, sem):
        remote(at, at, fs.at[0], sem, partner).wait_recv()

    def local(src, dst, sem):
        c = pltpu.make_async_copy(src, dst, sem)
        c.start()
        return c

    def sends_done(sent):
        for c in sent:
            c.wait_send()
        sent.clear()

    def z_start(t):
        at = pl.ds(32 * t.index, 32)
        for o in (1, 3, 2):
            start(t.sent, zbuf.at[me, at], zbuf.at[me, at], zs.at[t.index, o], zr.at[t.index, o], zp[o])
        start(t.sent, zbuf.at[me, at], zbuf.at[me, at], ds.at[t.index, 0], dr.at[t.index, 0], partner)

    def z_mid(t):
        at = pl.ds(32 * t.index, 32)
        for o in (1, 3, 2):
            here = zbuf.at[member(turn(2, -o), core), at]
            arrived(here, zr.at[t.index, o])
            start(t.sent, here, here, ds.at[t.index, o], dr.at[t.index, o], partner)

    def spread(t):
        at = pl.ds(32 * t.index, 32)
        for o in range(4):
            arrived(zbuf.at[me, at], dr.at[t.index, o])
        packed = zbuf[:, at].reshape(256, D)
        w[pl.ds(t.base + core * 2, 2), x, y] = dot(spread_matrix(core), packed).astype(bf).reshape(2, 48, D)
        if t is A:
            r = lax.broadcasted_iota(jnp.int32, (16, 1), 0)
            smbuf[...] = dot(one_hot(lax.rem(r, 8) * 32 + 24, 256), packed[:, :128]).astype(bf)
            sm[x, y] = smbuf[...]

    def xy1(t):
        for o in (1, 3, 2):
            for c in (0, 1):
                here = w.at[t.base + core * 2 + c, x, y]
                start(t.sent, here, here, as1.at[t.index, c, o], ar1.at[t.index, c, o], (xp, yp)[c][o])
            if t is A:
                start(t.sent, smbuf, sm.at[x, y], ss1.at[o], sr1.at[o], xp[o])

    def line(t, c, off):
        if c == 0:
            return w.at[t.base + core * 2, :, turn(1, off)]
        return w.at[t.base + core * 2 + 1, turn(0, off)]

    def hand(t, c, p, off):
        start(t.sent, line(t, c, off), line(t, c, off), cs.at[t.index, c, p], cr.at[t.index, c, p], partner)

    def xy2(t):
        for c in (0, 1):
            here = w.at[t.base + core * 2 + c, x, y]
            for o in (1, 2, 3):
                arrived(here, ar1.at[t.index, c, o])
            here = line(t, c, 0)
            for p, off in ((1, s), (3, -s)):
                start(t.sent, here, here, as2.at[t.index, c, p], ar2.at[t.index, c, p], peer(1 - c, off))
            hand(t, c, 0, 0)
        if t is A:
            for o in (1, 2, 3):
                arrived(smbuf, sr1.at[o])
            for p in (1, 2, 3):
                start(t.sent, sm.at[:, y], sm.at[:, y], ss2.at[p], sr2.at[p], yp[p])

    def relay(t):
        for c in (0, 1):
            here = line(t, c, -s)
            arrived(here, ar2.at[t.index, c, 1])
            start(t.sent, here, here, as2.at[t.index, c, 2], ar2.at[t.index, c, 2], peer(1 - c, s))
            hand(t, c, 1, -s)

    def hand_over(t):
        for p, off in ((3, s), (2, 2)):
            for c in (0, 1):
                arrived(line(t, c, off), ar2.at[t.index, c, p])
                hand(t, c, p, off)
        if t is A:
            for p in (1, 2, 3):
                arrived(sm.at[:, y], sr2.at[p])

    def finish(t):
        for p in (0, 1, 3, 2):
            for c in (0, 1):
                arrived(line(t, c, 0), cr.at[t.index, c, p])

    def plane(off):
        there = turn(2, off)
        return w.at[12:16, :, lax.rem(there, 2) * 2 + there // 2, :, lanes]

    def c2_first():
        arrived(c2buf.at[0], dr.at[3, 0])
        both = c2buf[...].astype(f32)[:, :24].reshape(48, D).astype(bf)
        w[12 + x, y, qm, :, lanes] = jnp.where(core == 0, both[:, :HALF], both[:, HALF:])
        here = w.at[12 + x, y, qm, :, lanes]
        for o in (1, 3, 2):
            start(C2.sent, here, here, as1.at[3, 0, o], ar1.at[3, 0, o], xp[o])

    def c2_second():
        here = w.at[12 + x, y, qm, :, lanes]
        for o in (1, 2, 3):
            arrived(here, ar1.at[3, 0, o])
        here = w.at[12:16, y, qm, :, lanes]
        for o in (1, 3, 2):
            start(C2.sent, here, here, as1.at[3, 1, o], ar1.at[3, 1, o], yp[o])

    def c2_third():
        for o in (1, 2, 3):
            arrived(w.at[12:16, y, qm, :, lanes], ar1.at[3, 1, o])
        here = plane(0)
        for p, off in ((1, s), (3, -s)):
            start(C2.sent, here, here, as2.at[3, 0, p], ar2.at[3, 0, p], peer(2, off))
        start(C2.sent, here, here, cs.at[3, 0, 0], cr.at[3, 0, 0], partner)

    def c2_relay():
        here = plane(-s)
        arrived(here, ar2.at[3, 0, 1])
        start(C2.sent, here, here, as2.at[3, 0, 2], ar2.at[3, 0, 2], peer(2, s))
        start(C2.sent, here, here, cs.at[3, 0, 1], cr.at[3, 0, 1], partner)

    def c2_hand():
        for p, off in ((3, s), (2, 2)):
            here = plane(off)
            arrived(here, ar2.at[3, 0, p])
            start(C2.sent, here, here, cs.at[3, 0, p], cr.at[3, 0, p], partner)

    def c2_finish():
        for p in range(4):
            arrived(plane(0), cr.at[3, 0, p])

    block = hi * 2 + core
    pairs = ((tok_in, tok), (enc_in, enc))
    own = {}

    def input_start(i):
        src, dst = pairs[i]
        start(moved, src.at[1 - hi], dst.at[block], es.at[i], er.at[i], home)
        start(moved, src.at[hi], dst.at[block], es.at[2 + i], er.at[2 + i], partner)
        own[i] = local(src.at[hi], dst.at[block], ls.at[1 + i])

    def input_forward(i):
        far = pairs[i][1].at[(1 - hi) * 2 + core]
        arrived(far, er.at[i])
        start(moved, far, far, fs.at[i], fr.at[i], partner)

    def input_ready(i):
        here = pairs[i][1].at[0]
        own[i].wait()
        arrived(here, er.at[2 + i])
        arrived(here, fr.at[i])

    def grad_start():
        start(moved, og_in.at[1 - hi], og.at[core], es.at[4], er.at[4 + core], device_at(x, y, across, hi))

        @pl.when(core == hi)
        def _():
            c = pltpu.make_async_copy(og_in.at[hi], og.at[core], ls.at[3])
            c.start()
            c.wait()

        @pl.when(core != hi)
        def _():
            c = remote(og_in.at[hi], og.at[core], es.at[5], er.at[6], partner)
            c.start()
            c.wait_send()

    def grad_ready():
        @pl.when(hi == core)
        def _():
            arrived(og.at[0], er.at[6])

        @pl.when(hi != core)
        def _():
            for i in (0, 1):
                arrived(og.at[0], er.at[4 + i])

    def out_start(t):
        for i in range(4):
            src = w.at[12 + i, :, :, :, lanes_other] if t is C2 else w.at[t.out + 2 * other + i // 2, :, :, :, halves[i % 2]]
            start(t.sent, src, db.at[t.slot, i], bds.at[t.index, i], bdr.at[t.index, i], partner)

    def out_line(t, c, off):
        if t is C2:
            there = turn(2, off)
            return db.at[t.slot, :, :, lax.rem(there, 2) * 2 + there // 2]
        if c == 0:
            return db.at[t.slot, 0:2, :, turn(1, off)]
        return db.at[t.slot, 2:4, turn(0, off)]

    def out_axis(t, c):
        return 2 if t is C2 else 1 - c

    def out_colors(t):
        return (0,) if t is C2 else (0, 1)

    def out_slot(t, c, p):
        return r1.at[t.slot, p] if t is C2 else r1.at[t.slot, p, 2 * c:2 * c + 2]

    def add_into(to, *terms):
        n = to.shape[0]

        @pl.loop(0, n)
        def _(i):
            total = to[i].astype(f32)
            for term in terms:
                total = total + term[i].astype(f32)
            to[i] = total.astype(bf)

    def out_first(t):
        for i in range(4):
            arrived(db.at[t.slot, i], bdr.at[t.index, i])
            if t is C2:
                add_into(db.at[t.slot, i], w.at[12 + i, :, :, :, lanes])
            else:
                add_into(db.at[t.slot, i], w.at[t.out + 2 * core + i // 2, :, :, :, halves[i % 2]])
            if t is C2 and i < 3 or i % 2 == 0:
                continue
            c = 0 if t is C2 else i // 2
            for p, off, to in ((0, 2, s), (1, -s, -s)):
                start(t.back, out_line(t, c, off), out_slot(t, c, p), b1s.at[t.index, c, p], b1r.at[t.index, c, p],
                      peer(out_axis(t, c), to))

    def out_second(t):
        for c in out_colors(t):
            arrived(out_slot(t, c, 0), b1r.at[t.index, c, 0])
            here = out_line(t, c, s)
            add_into(here, out_slot(t, c, 0))
            start(t.back, here, out_slot(t, c, 2), b1s.at[t.index, c, 2], b1r.at[t.index, c, 2], peer(out_axis(t, c), s))

    def out_third(t):
        for c in out_colors(t):
            for p in (1, 2):
                arrived(out_slot(t, c, p), b1r.at[t.index, c, p])
            add_into(out_line(t, c, 0), out_slot(t, c, 1), out_slot(t, c, 2))
            for o in (1, 3, 2):
                if t is C2:
                    src, dst, to = db.at[t.slot, :, turn(1, o), qm], r2.at[t.slot, o - 1], yp[o]
                elif c == 0:
                    src, dst, to = db.at[t.slot, 0:2, turn(0, o), y], r2.at[t.slot, o - 1, 0:2], xp[o]
                else:
                    src, dst, to = db.at[t.slot, 2:4, x, turn(1, o)], r2.at[t.slot, o - 1, 2:4], yp[o]
                start(t.back, src, dst, b2s.at[t.index, c, o - 1], b2r.at[t.index, c, o - 1], to)

    def out_fourth(t):
        if t is C2:
            for o in (0, 1, 2):
                arrived(r2.at[t.slot, o], b2r.at[3, 0, o])
            add_into(db.at[t.slot, :, y, qm], *[r2.at[t.slot, o] for o in (0, 1, 2)])
            for o in (1, 3, 2):
                start(t.back, db.at[t.slot, turn(0, o), y, qm], r2b.at[o - 1], b2s.at[3, 1, o - 1], b2r.at[3, 1, o - 1], xp[o])
            return
        for c in (0, 1):
            for o in (0, 1, 2):
                arrived(r2.at[t.slot, o, 2 * c:2 * c + 2], b2r.at[t.index, c, o])
            for h in (0, 1):
                total = db[t.slot, 2 * c + h, x, y].astype(f32)
                for o in (0, 1, 2):
                    total = total + r2[t.slot, o, 2 * c + h].astype(f32)
                red[c, :, h * HALF:(h + 1) * HALF] = total.astype(bf)
        shares[t.index] = dot(split_matrix(), red[...].reshape(96, D)).astype(bf).reshape(8, 16, D)
        for o in (1, 3, 2):
            start(t.back, shares.at[t.index, pl.ds(member(turn(2, o), 0), 2)], r3.at[t.index, o - 1], b3s.at[t.index, o - 1],
                  b3r.at[t.index, o - 1], zp[o])

    def out_fifth(t):
        if t is C2:
            for o in (0, 1, 2):
                arrived(r2b.at[o], b2r.at[3, 1, o])
            total = db[t.slot, x, y, qm].astype(f32)
            for o in (0, 1, 2):
                total = total + r2b[o].astype(f32)
            c2sum[core] = total.astype(bf)
            start(t.back, c2sum.at[core], c2sum.at[core], b4s.at[3], b4r.at[3], partner)
            return
        for o in (0, 1, 2):
            arrived(r3.at[t.index, o], b3r.at[t.index, o])
        base = member(z, 0)

        def share(c):
            total = shares[t.index, base + c].astype(f32)
            for o in (0, 1, 2):
                total = total + r3[t.index, o, c].astype(f32)
            return total
        fin[t.index, core] = share(core)
        sx[t.index] = share(other).astype(bf)
        start(t.back, sx.at[t.index], r4.at[t.index], b4s.at[t.index], b4r.at[t.index], partner)

    def out_last(t):
        if t is C2:
            arrived(c2sum.at[other], b4r.at[3])
            rows = jnp.concatenate([c2sum[0], c2sum[1]], 1).astype(f32)
            fin2[...] = jnp.where(core == 0, rows[:24], rows[24:])
            return
        arrived(r4.at[t.index], b4r.at[t.index])
        fin[t.index, other] = r4[t.index].astype(f32)

    def give_credit(t):
        sends_done(t.back)
        for to in near:
            pl.semaphore_signal(credit.at[t.slot], inc=1, device_id=to, device_id_type=MESH)

    def take_credit(t):
        pl.semaphore_wait(credit.at[t.slot], len(near))

    def home_start(i, src, buf):
        for n in (0, 1):
            start(moved, src.at[2 * n + other], buf.at[n], ts.at[i, n], tr.at[i, n], partner)

    def home_sum(i, src, buf, out):
        for n in (0, 1):
            arrived(buf.at[n], tr.at[i, n])

            @pl.loop(0, buf.shape[1] // 16)
            def _(a):
                at = pl.ds(pl.multiple_of(a * 16, 16), 16)
                src[2 * n + core, at] = (src[2 * n + core, at].astype(f32) + buf[n, at].astype(f32)).astype(bf)
        start(moved, src.at[2 * (1 - hi) + core], out.at[hi], ts.at[2, i], tr.at[2, i], home)
        return local(src.at[2 * hi + core], out.at[hi], ls.at[4 + i])

    def result_start():
        @pl.when(core == hi)
        def _():
            c = pltpu.make_async_copy(BO.at[core], bo_out.at[hi], ls.at[3])
            c.start()
            d = remote(BO.at[other], bo_out.at[hi], os_.at[0], tr.at[3, 0], partner)
            d.start()
            c.wait()
            d.wait_send()

        @pl.when(core != hi)
        def _():
            copies = [remote(BO.at[n], bo_out.at[hi], os_.at[n], tr.at[3, 1], device_at(x, y, across, n)) for n in (0, 1)]
            for c in copies:
                c.start()
            for c in copies:
                c.wait_send()

    def weight(u):
        return w[u].reshape(D, D)

    def weight_grad(u, a, b):
        @pl.loop(0, 3)
        def _(i):
            at = pl.ds(pl.multiple_of(i * 256, 256), 256)
            w[u, :, :, :, at] = dot_grad(a[...].reshape(-1, D), b[:, at]).astype(bf).reshape(4, 4, 48, 256)

    mine = pl.ds(pl.multiple_of(core * SPAN, 32), SPAN)

    loads = [local(m, s6.at[i], ls.at[6 + i]) for i, m in enumerate((m0, m1, m2, m3, m4, m5, m6, m7))]
    loads += [local(h_in, sh1, ls.at[14]), local(h_out, sh2, ls.at[15])]
    acc[0, 0:96] = jnp.zeros((96, D), f32)
    acc[1, 0:32] = jnp.zeros((32, D), f32)
    for c in loads:
        c.wait()
    for i in range(4):
        acc[0, 6 * i:6 * i + 6] = s6[i].astype(f32)
        acc[0, 32 + 6 * i:38 + 6 * i] = s6[4 + i].astype(f32)
        acc[0, 64 + 6 * i:70 + 6 * i] = sh1[:, D * i:D * i + D].astype(f32)
    acc[0, 24:25, 0:128] = small[0:1].astype(f32)
    acc[1, 0:24] = sh2[...].astype(f32)
    zbuf[me] = acc[0, 0:96].astype(bf)
    c2buf[core] = acc[1, 0:32].astype(bf)
    krow = seg2[pl.ds(hi, 1)]
    crow = clip2[pl.ds(hi, 1)]
    ids = jnp.broadcast_to(krow, (8, KEYS)).astype(f32).T[:, 0:1].astype(jnp.int32)
    qcol = jnp.where(core == 0, ids[:SPAN], ids[SPAN:])
    key_at = lax.broadcasted_iota(jnp.int32, (SPAN, KEYS), 1)
    query_at = lax.broadcasted_iota(jnp.int32, (SPAN, KEYS), 0) + core * SPAN
    bias_s[...] = jnp.where((qcol == krow) & (key_at <= query_at), 0.0, BLOCKED)
    bias_c[...] = jnp.where(qcol == crow, 0.0, BLOCKED)
    pl.semaphore_wait(barrier, len(peers))
    z_start(A)
    z_start(B)
    z_start(C1)
    start(C2.sent, c2buf.at[core], c2buf.at[core], ds.at[3, 0], dr.at[3, 0], partner)
    input_start(0)
    z_mid(A)
    spread(A)
    xy1(A)
    c2_first()
    z_mid(B)
    spread(B)
    xy1(B)
    input_start(1)
    xy2(A)
    z_mid(C1)
    spread(C1)
    input_forward(0)
    relay(A)
    xy2(B)
    c2_second()
    xy1(C1)
    input_ready(0)
    hand_over(A)

    S = sm[...].astype(f32).reshape(16, 16, 128)[:, :8].reshape(128, 128).astype(bf)
    owner, inner, which = vector_tables()
    vec[...] = dot_back(which, (dot(owner, S) * inner).astype(bf))
    for n in range(4):
        owner, inner = hidden_tables(n)
        hib[n:n + 1] = dot_back(jnp.ones((8, 128), bf), (dot(owner, S) * inner).astype(bf))[0:1]

    @pl.loop(0, 4)
    def _(i):
        n, _ = normed(tok[i].astype(f32))
        first[pl.ds(pl.multiple_of(i * 112, 16), 112)] = (n * vec[0:1] + vec[1:2]).astype(bf)
    c2_third()
    grad_start()
    finish(A)

    def keys(at):
        k[at] = dot(first[at], weight(1)).astype(bf)
    blocks(KEYS, SPAN, keys)
    relay(B)
    xy2(C1)

    def values(at):
        v[at] = (dot(first[at], weight(2)) + vec[3:4]).astype(bf)
    blocks(KEYS, SPAN, values)
    q[...] = (dot(first[mine], weight(0)) + vec[2:3]).astype(bf) * SCALE
    hand_over(B)
    attend(q, k, v, bias_s, mixed, lse, 0, 3)
    input_forward(1)
    relay(C1)
    attend(q, k, v, bias_s, mixed, lse, 3, 6)
    after_self[...] = tok[pl.ds(2 * core, 2)].reshape(SPAN, D).astype(f32) + dot(mixed[...], weight(3)) + vec[4:5]
    n, r = normed(after_self[...])
    second[...] = (n * vec[5:6] + vec[6:7]).astype(bf)
    finish(B)
    c2_relay()
    cq[...] = (dot(second[...], weight(4)) + vec[7:8]).astype(bf) * SCALE
    hand_over(C1)
    input_ready(1)

    @pl.loop(0, 4)
    def _(i):
        ck[pl.ds(pl.multiple_of(i * 384, 128), 384)] = dot(enc[i], weight(5)).astype(bf)

    @pl.loop(0, 4)
    def _(i):
        cv[pl.ds(pl.multiple_of(i * 384, 128), 384)] = (dot(enc[i], weight(6)) + vec[8:9]).astype(bf)
    attend(cq, ck, cv, bias_c, cmixed, clse, 0, 3)
    c2_hand()
    attend(cq, ck, cv, bias_c, cmixed, clse, 3, 6)
    stream[...] = after_self[...] + dot(cmixed[...], weight(7)) + vec[9:10]
    n, r = normed(stream[...])
    third[...] = (n * vec[10:11] + vec[11:12]).astype(bf)
    acc[0] = stream[...] + vec[12:13]
    acc[1] = jnp.zeros((SPAN, D), f32)
    grad_ready()
    g[...] = og[...].reshape(SPAN, D)
    finish(C1)
    c2_finish()
    for t in (A, B, C1, C2):
        sends_done(t.sent)
    sends_done(moved)
    for i in range(4):
        pre = dot(third[...], weight(8 + i)) + hib[i:i + 1]
        cdf = 0.5 * (1.0 + lax.erf(pre * 0.7071067811865476))
        act = (pre * cdf).astype(bf)
        slope = cdf + pre * (0.3989422804014327 * jnp.exp(-0.5 * pre * pre))
        wide[0] = act
        acc[0] += dot(act, weight(12 + i))
        g_pre = (dot_back(g[...], weight(12 + i)) * slope).astype(bf)
        wide[1] = g_pre
        weight_grad(12 + i, wide.at[0], g)
        ghib[i:i + 1] = row_sum(g_pre.astype(f32))
        acc[1] += dot_back(g_pre, weight(8 + i))
        weight_grad(8 + i, third, wide.at[1])
    out_start(C2)
    out_start(C1)
    BO[...] = acc[0].astype(bf).reshape(2, 112, D)
    e = acc[1]
    ogf = g[...].astype(f32)
    n, r = normed(stream[...])
    gvec[13:16] = jnp.zeros((3, D), f32)
    gvec[12:13] = row_sum(ogf)
    gvec[10:11] = row_sum(e * n)
    gvec[11:12] = row_sum(e)
    stream[...] = ogf + norm_back(e, n, r, vec[10:11])
    wide[0] = stream[...].astype(bf)
    gvec[9:10] = row_sum(wide[0].astype(f32))
    out_first(C2)
    g[...] = dot_back(wide[0], weight(7)).astype(bf)
    out_first(C1)
    result_start()
    sends_done(C2.sent)
    sends_done(C1.sent)
    weight_grad(15, cmixed, wide.at[0])
    attend_back(cq, ck, cv, bias_c, cmixed, clse, g, gq, ck, cv, 0, 2)
    out_second(C1)
    attend_back(cq, ck, cv, bias_c, cmixed, clse, g, gq, ck, cv, 2, 4)
    out_third(C1)
    out_second(C2)
    attend_back(cq, ck, cv, bias_c, cmixed, clse, g, gq, ck, cv, 4, 6)
    out_fourth(C1)
    weight_grad(13, enc, ck)
    out_third(C2)
    weight_grad(14, enc, cv)
    out_fifth(C1)
    weight_grad(12, second, gq)
    give_credit(C1)
    take_credit(B)
    out_start(B)

    @pl.loop(0, 4)
    def _(i):
        at = pl.ds(pl.multiple_of(i * 384, 128), 384)
        enc[i] = (dot_back(ck[at], weight(5)) + dot_back(cv[at], weight(6))).astype(bf)
    home_start(1, enc, eib)
    out_first(B)
    out_fourth(C2)
    e = dot_back(gq[...], weight(4))
    gvec[7:8] = row_sum(gq[...].astype(f32))
    gvec[8:9] = row_sum(cv[...].astype(f32))
    n, r = normed(after_self[...])
    gvec[5:6] = row_sum(e * n)
    gvec[6:7] = row_sum(e)
    stream[...] += norm_back(e, n, r, vec[5:6])
    wide[0] = stream[...].astype(bf)
    gvec[4:5] = row_sum(wide[0].astype(f32))
    g[...] = dot_back(wide[0], weight(3)).astype(bf)
    ends = [home_sum(1, enc, eib, ep_out)]
    weight_grad(11, mixed, wide.at[0])
    out_fifth(C2)
    out_second(B)
    attend_back(q, k, v, bias_s, mixed, lse, g, gq, k, v, 0, 6)
    give_credit(C2)
    out_third(B)
    wide[0] = first[mine]
    weight_grad(8, wide.at[0], gq)
    weight_grad(9, first, k)
    weight_grad(10, first, v)
    take_credit(A)
    out_start(A)
    gvec[2:3] = row_sum(gq[...].astype(f32))
    gvec[3:4] = row_sum(v[...].astype(f32))
    gvec[0:2] = jnp.zeros((2, D), f32)
    acc[0] = dot_back(gq[...], weight(0))
    for h in (0, 1):
        at = pl.ds(h * SPAN, SPAN)
        is_own = core == h
        e = dot_back(k[at], weight(1)) + dot_back(v[at], weight(2)) + jnp.where(is_own, acc[0], 0.0)
        n, r = normed(tok[2 * h:2 * h + 2].reshape(SPAN, D).astype(f32))
        gvec[0:1] += row_sum(e * n)
        gvec[1:2] += row_sum(e)
        PI[2 * h:2 * h + 2] = (norm_back(e, n, r, vec[0:1]) + jnp.where(is_own, stream[...], 0.0)).astype(bf).reshape(2, 112, D)
        if h == 0:
            out_first(A)
    home_start(0, PI, pib)
    out_fourth(B)
    owner, inner, which = vector_tables()
    spread_out = lax.dot_general(gvec[...].astype(bf), which, (((0,), (0,)), ((), ())), preferred_element_type=f32)
    total = dot_grad(owner, (spread_out * inner).astype(bf))
    for n in range(4):
        owner, inner = hidden_tables(n)
        column = jnp.broadcast_to(ghib[n:n + 1], (8, D)).T[:, 0:1]
        total = total + dot_grad(owner, (column * inner).astype(bf))
    SG[...] = total.reshape(4, 4, 8, 128)
    swap = remote(SG, sd, gss.at[0], gsr.at[0], partner)
    swap.start()
    out_second(A)
    swap.wait()
    SG[...] = SG[...] + sd[...]
    for p in (1, 2, 3):
        start(moved, SG.at[:, turn(1, p)], s1b.at[p], gss.at[p], gsr.at[p], yp[p])
    ends.append(home_sum(0, PI, pib, pi_out))
    out_fifth(B)
    out_third(A)
    total = SG[:, y]
    for p in (1, 2, 3):
        arrived(s1b.at[p], gsr.at[p])
        total = total + s1b[p]
    SG[:, y] = total
    for b in (1, 2, 3):
        start(moved, SG.at[turn(0, b), y], s2b.at[b], gss.at[3 + b], gsr.at[3 + b], xp[b])
    out_last(C2)
    out_last(C1)
    out_last(B)
    out_fourth(A)
    total = SG[x, y]
    for b in (1, 2, 3):
        arrived(s2b.at[b], gsr.at[3 + b])
        total = total + s2b[b]
    s3b[0] = total
    for o in (1, 2, 3):
        start(moved, s3b.at[0], s3b.at[o], gss.at[6 + o], gsr.at[6 + o], zp[o])
    out_fifth(A)
    total = s3b[0]
    for o in (1, 2, 3):
        arrived(s3b.at[o], gsr.at[6 + o])
        total = total + s3b[o]
    own_row = lax.broadcasted_iota(jnp.int32, (8, 128), 0) == me
    gs[...] = jnp.broadcast_to(jnp.sum(jnp.where(own_row, total, 0.0), 0, keepdims=True), (8, 128))
    arrived(ep_out.at[0], tr.at[2, 1])
    arrived(pi_out.at[0], tr.at[2, 0])

    @pl.when(core != hi)
    def _():
        arrived(bo_out.at[0], tr.at[3, 0])
    arrived(bo_out.at[0], tr.at[3, 1])
    out_last(A)
    for c in ends:
        c.wait()
    for t in (A, B, C1, C2):
        sends_done(t.sent)
        sends_done(t.back)
    sends_done(moved)


def layer(*operands):
    V, DMA, S = pltpu.VMEM, pltpu.SemaphoreType.DMA, jax.ShapeDtypeStruct
    vm, hbm = pl.BlockSpec(memory_space=pltpu.VMEM), pl.BlockSpec(memory_space=pl.ANY)
    return pl.pallas_call(
        layer_kernel,
        out_shape=[S((3, 2, 16, D), f32), S((24, D), f32), S((8, 128), f32), S((2, 112, D), bf), S((2, 112, D), bf), S((2, 384, D), bf)],
        in_specs=[hbm] * 10 + [vm] + [hbm] * 3 + [vm] * 2, out_specs=[vm] * 3 + [hbm] * 3,
        scratch_shapes=[
            V((16, 4, 4, 48, D), bf), V((8, 6, D), bf), V((6, 4 * D), bf), V((24, D), bf), V((8, 96, D), bf), V((2, 32, D), bf),
            V((4, 4, 16, 128), bf), V((16, 128), bf), V((4, 112, D), bf), V((4, 384, D), bf), V((2, 112, D), bf),
            V((16, D), f32), V((8, D), f32), V((KEYS, D), bf), V((SPAN, D), bf), V((KEYS, D), bf), V((KEYS, D), bf),
            V((SPAN, D), bf), V((6, SPAN, 128), f32), V((SPAN, D), bf), V((SPAN, D), bf), V((FRAMES, D), bf), V((FRAMES, D), bf),
            V((SPAN, D), bf), V((6, SPAN, 128), f32), V((SPAN, D), f32), V((SPAN, D), f32), V((SPAN, D), bf),
            V((2, SPAN, D), f32), V((SPAN, KEYS), f32), V((SPAN, FRAMES), f32), V((SPAN, D), bf), V((SPAN, D), bf),
            V((2, SPAN, D), bf), V((16, D), f32), V((8, D), f32),
            V((2, 112, D), bf), V((4, 112, D), bf), V((2, 112, D), bf), V((2, 384, D), bf),
            V((2, 4, 4, 4, 48, HALF), bf), V((2, 3, 4, 4, 48, HALF), bf), V((2, 3, 4, 48, HALF), bf), V((3, 48, HALF), bf),
            V((2, 48, D), bf), V((3, 8, 16, D), bf), V((3, 3, 2, 16, D), bf), V((3, 16, D), bf), V((3, 16, D), bf),
            V((2, 48, HALF), bf), V((16, 128), f32),
            V((4, 4, 8, 128), f32), V((4, 4, 8, 128), f32), V((4, 4, 8, 128), f32), V((4, 8, 128), f32), V((4, 8, 128), f32),
            DMA((16,)), DMA((4, 4)), DMA((4, 4)), DMA((4, 4)), DMA((4, 4)), DMA((4, 2, 4)), DMA((4, 2, 4)), DMA((4, 2, 4)), DMA((4, 2, 4)),
            DMA((4, 2, 4)), DMA((4, 2, 4)), DMA((4,)), DMA((4,)), DMA((4,)), DMA((4,)), DMA((6,)), DMA((7,)), DMA((2,)), DMA((2,)),
            DMA((4, 4)), DMA((4, 4)), DMA((4, 2, 3)), DMA((4, 2, 3)), DMA((4, 2, 3)), DMA((4, 2, 3)), DMA((3, 3)), DMA((3, 3)),
            DMA((4,)), DMA((4,)), DMA((10,)), DMA((10,)), DMA((3, 2)), DMA((4, 2)), DMA((2,)), pltpu.SemaphoreType.REGULAR((2,))],
        compiler_params=pltpu.CompilerParams(collective_id=0, has_side_effects=True, vmem_limit_bytes=63 << 20),
        name="layer",
    )(*operands)


def unpack_kernel(fin, fin2, bo, pi, ep, *outs):
    out, gi, ge, mats, h_in, h_out = outs[0], outs[1], outs[2], outs[3:11], outs[11], outs[12]
    out[...] = bo[...][:, None]
    gi[...] = pi[...].astype(f32)[:, None]
    ge[...] = ep[:, :375].astype(f32)[:, None]
    for i in range(4):
        mats[i][...] = fin[0, i // 2, 6 * (i % 2):6 * (i % 2) + 6]
        mats[4 + i][...] = fin[1, i // 2, 6 * (i % 2):6 * (i % 2) + 6]
        h_in[:, D * i:D * i + D] = fin[2, i // 2, 6 * (i % 2):6 * (i % 2) + 6]
    h_out[...] = fin2[...]


def unpack(fin, fin2, bo, pi, ep):
    S = jax.ShapeDtypeStruct
    return pl.pallas_call(
        unpack_kernel,
        out_shape=[S((2, 1, 112, D), bf), S((2, 1, 112, D), f32), S((2, 1, 375, D), f32)] + [S((6, D), f32)] * 8 + [S((6, 4 * D), f32), S((24, D), f32)],
        compiler_params=pltpu.CompilerParams(vmem_limit_bytes=32 << 20),
        name="unpack",
    )(fin, fin2, bo, pi, ep)


def per_device(
    tokens, encoder_states, segments, frame_clips, out_grad,
    self_gain, self_shift, self_query, self_query_bias, self_key, self_value, self_value_bias, self_output,
    self_output_bias, cross_gain, cross_shift, cross_query, cross_query_bias, cross_key, cross_value,
    cross_value_bias, cross_output, cross_output_bias, final_gain, final_shift, hidden_in, hidden_in_bias,
    hidden_out, hidden_out_bias,
):
    vectors = (self_gain, self_shift, self_query_bias, self_value_bias, self_output_bias, cross_gain, cross_shift,
               cross_query_bias, cross_value_bias, cross_output_bias, final_gain, final_shift, hidden_out_bias)
    small = jnp.pad(hidden_in_bias.astype(f32), (78, 26))
    for i, vector in enumerate(vectors):
        small = small + jnp.pad(vector.astype(f32), (6 * i, 122 - 6 * i))
    small = jnp.broadcast_to(small[None], (8, 128))
    frames = jnp.pad(encoder_states, ((0, 0), (0, 0), (0, 9), (0, 0))).reshape(2, 384, D)
    clip = jnp.pad(frame_clips.reshape(2, 4, 375), ((0, 0), (0, 0), (0, 9)), constant_values=-1).reshape(2, FRAMES)
    fin, fin2, gs, bo, pi, ep = layer(
        self_query, self_key, self_value, self_output, cross_query, cross_key, cross_value, cross_output, hidden_in, hidden_out,
        small, tokens[:, 0], frames, out_grad[:, 0], segments[:, 0], clip)
    out, gi, ge, *m = unpack(fin, fin2, bo, pi, ep)
    gv = [gs[0, 6 * i:6 * i + 6] for i in range(13)]
    return (out, gi, ge,
            gv[0], gv[1], m[0], gv[2], m[1], m[2], gv[3], m[3], gv[4],
            gv[5], gv[6], m[4], gv[7], m[5], m[6], gv[8], m[7], gv[9],
            gv[10], gv[11], m[8], gs[0, 78:102], m[9], gv[12])


def solution(mesh):
    rows = P(None, "win", "seq", None)
    vector, matrix = P(("win", "seq")), P(("win", "seq"), None)
    kinds = "vvmvmmvmvvvmvmmvmvvvmvmv"
    weights = tuple(matrix if kind == "m" else vector for kind in kinds)
    in_specs = (rows, rows, P(None, "win", None), P(None, "win", None), rows) + weights
    return jax.shard_map(per_device, mesh=mesh, in_specs=in_specs, out_specs=(rows, rows, rows) + weights, check_vma=False)
```

time: 316 us -> 229 us (0.72)
  Pallas kernels: 284 us -> 210 us
  local copies, waits for them, and re-layouts: 25.8 us -> 14.5 us
    pallas_call x3 -> x2, Pallas kernels: 284 us -> 210 us  [the longest x1 209 us: layer(): pl.pallas_call(layer_kernel, out_shape=[S((3, 2, 16, D), f32), S((24, D),...]
    reshape x13 -> x2, local copies, waits for them, and re-layouts: 5.63 us -> 1.18 us  [the longest x1 1.09 us: per_device(): jnp.pad(encoder_states, ((0, 0), (0, 0), (0, 9), (0, 0))).reshape(2, 384, D)]
    unnamed x76 -> x49, local copies, waits for them, and re-layouts: 10.6 us -> 11.5 us
where the time goes in v3:
time: 229 us; the launch traced here: 226 us
  Pallas kernels  210 us (92%)
  local copies, waits for them, and re-layouts  14.5 us (6%)
    pallas_call x1, Pallas kernels, layer(): pl.pallas_call(layer_kernel, out_shape=[S((3, 2, 16, D), f32), S((24, D),...  209 us
    unnamed x49, local copies, waits for them, and re-layouts  11.5 us

profile of v3, /device:TPU:1, one launch (start us, length us, event | category | flops | bytes accessed | tf_op | source)
XLA Modules:
  0.0 225.9 jit_solution(5475018273683253191)
XLA Ops:
  0.7 1.4 copy.56
  2.1 0.0 copy-start.8
  2.1 0.0 copy-start.9
  2.1 0.0 copy-start.12
  2.1 0.0 copy-start.13
  2.2 0.0 copy-start.16
  2.2 0.0 copy-start.17
  2.2 0.0 copy-start.20
  2.2 1.1 pad_bitcast_fusion.enc_in
  3.4 0.1 reshape.65
  3.5 0.6 copy.59
  4.2 0.1 convert_add_fusion
  4.3 0.6 broadcast_in_dim.2.small
  4.9 0.6 copy.61
  5.5 208.9 %layer.1 = (f32[3,2,16,768]{3,2,1,0:T(8,128)}, f32[24,768]{1,0:T(8,128)}, f32[8,128]{1,0:T(8,128)}, bf16[2,112,768]{2,1,0:T(8,128)(2,1)}, bf16[2,112,768]{2,1,0:T(8,128)(2,1)}, /*index=5*/bf16[2,384,768]{2,1,0:T(8,128)(2,1)}) custom-call(bf16[6,768]{1,0:T(8,128)(2,1)} %m0.1, bf16[6,768]{1,0:T(8,128)(2,1)} %m1.1, bf16[6,768]{1,0:T(8,128)(2,1)} %m2.1, ...), custom_call_target="tpu_custom_call" | custom-call | tf_op jit(solution)/shard_map/layer/pallas_call | solution.py:827
  214.4 1.3 copy-done
  215.7 1.0 copy-done.1
  216.7 1.0 copy-done.2
  217.6 1.0 copy-done.3
  218.6 0.9 copy-done.4
  219.5 1.1 unpack.1
  220.6 3.8 %copy.57 = f32[2,1,375,768]{3,1,2,0:T(1,128)} copy(f32[2,1,375,768]{3,2,1,0:T(8,128)S(1)} %get-tuple-element.67) | data formatting | bytes 4608000
  224.4 0.6 slice_bitcast_fusion
  225.0 0.6 slice_bitcast_fusion.1
  (34 shorter events, 0.1 us)
Async XLA Ops:
  2.0 1.3 copy-start.5
  2.1 2.0 copy-start.8
  2.1 2.0 copy-start.9
  2.1 2.0 copy-start.10
  2.1 2.0 copy-start.11
  2.1 2.0 copy-start.12
  2.1 2.0 copy-start.13
  2.1 2.0 copy-start.14
  2.1 2.0 copy-start.15
  2.2 2.0 copy-start.16
  2.2 2.0 copy-start.17
  2.2 2.0 copy-start.18
  2.2 2.0 copy-start.19
  2.2 2.0 copy-start.20
  2.2 2.0 copy-start.21
  2.2 2.7 %copy-start.7 = (s32[2,1,448]{2,1,0:T(1,128)S(1)}, s32[2,1,448]{2,1,0:T(1,128)}, u32[]{:S(2)}) copy-start(s32[2,1,448]{2,1,0:T(1,128)} %param.31) | copy-start | bytes 10756
  214.4 1.3 copy-start
  215.7 1.0 copy-start.1
  216.7 1.0 copy-start.2
  217.6 1.0 copy-start.3
  218.6 0.9 copy-start.4
  220.6 3.8 %copy-start.6 = (f32[8,128]{1,0:T(8,128)S(1)}, f32[8,128]{1,0:T(8,128)}, u32[]{:S(2)}) copy-start(f32[8,128]{1,0:T(8,128)} %get-tuple-element.54) | copy-start | bytes 12292

commit v4 on v3

--- a/solution.py
+++ b/solution.py
@@ -120,7 +120,7 @@
 class Chunk:
     def __init__(self, index, base, out, slot):
         self.index, self.base, self.out, self.slot = index, base, out, slot
-        self.sent, self.back = [], []
+        self.sent, self.back, self.late = [], [], []
 
 
 def one_hot(source, width):
@@ -164,7 +164,7 @@
                  fin, fin2, gs, bo_out, pi_out, ep_out,
                  w, s6, sh1, sh2, zbuf, c2buf, sm, smbuf, tok, enc, og, vec, hib, first, q, k, v, mixed, lse, second, cq, ck, cv,
                  cmixed, clse, after_self, stream, third, acc, bias_s, bias_c, g, gq, wide, gvec, ghib,
-                 BO, PI, pib, eib, db, r1, r2, r2b, red, shares, r3, sx, r4, c2sum, c2r, SG, sd, s1b, s2b, s3b,
+                 BO, PI, pib, eib, db, r1, r2, r2a, r2b, ptot, red, shares, r3, sx, r4, c2sum, c2r, SG, sd, s1b, s2b, s3b,
                  ls, zs, zr, ds, dr, as1, ar1, as2, ar2, cs, cr, ss1, sr1, ss2, sr2, es, er, fs, fr,
                  bds, bdr, b1s, b1r, b2s, b2r, b3s, b3r, b4s, b4r, gss, gsr, ts, tr, os_, credit):
     x, y, z, core = coords()
@@ -253,23 +253,31 @@
             if t is A:
                 start(t.sent, smbuf, sm.at[x, y], ss1.at[o], sr1.at[o], xp[o])
 
-    def line(t, c, off):
+    both = (0, 1)
+
+    def line(t, c, off, h):
+        at = pl.ds(2 * h, 2)
         if c == 0:
-            return w.at[t.base + core * 2, :, turn(1, off)]
-        return w.at[t.base + core * 2 + 1, turn(0, off)]
-
-    def hand(t, c, p, off):
-        start(t.sent, line(t, c, off), line(t, c, off), cs.at[t.index, c, p], cr.at[t.index, c, p], partner)
+            return w.at[t.base + core * 2, at, turn(1, off)]
+        return w.at[t.base + core * 2 + 1, turn(0, off), at]
+
+    def hand(t, c, p, off, h):
+        here = line(t, c, off, h)
+        start(t.sent, here, here, cs.at[t.index, c, 2 * p + h], cr.at[t.index, c, 2 * p + h], partner)
 
     def xy2(t):
         for c in (0, 1):
             here = w.at[t.base + core * 2 + c, x, y]
             for o in (1, 2, 3):
                 arrived(here, ar1.at[t.index, c, o])
-            here = line(t, c, 0)
-            for p, off in ((1, s), (3, -s)):
-                start(t.sent, here, here, as2.at[t.index, c, p], ar2.at[t.index, c, p], peer(1 - c, off))
-            hand(t, c, 0, 0)
+        for p, off in ((1, s), (3, -s)):
+            for h in both:
+                for c in (0, 1):
+                    here = line(t, c, 0, h)
+                    start(t.sent, here, here, as2.at[t.index, c, 2 * p + h], ar2.at[t.index, c, 2 * p + h], peer(1 - c, off))
+        for h in both:
+            for c in (0, 1):
+                hand(t, c, 0, 0, h)
         if t is A:
             for o in (1, 2, 3):
                 arrived(smbuf, sr1.at[o])
@@ -277,29 +285,35 @@
                 start(t.sent, sm.at[:, y], sm.at[:, y], ss2.at[p], sr2.at[p], yp[p])
 
     def relay(t):
-        for c in (0, 1):
-            here = line(t, c, -s)
-            arrived(here, ar2.at[t.index, c, 1])
-            start(t.sent, here, here, as2.at[t.index, c, 2], ar2.at[t.index, c, 2], peer(1 - c, s))
-            hand(t, c, 1, -s)
+        for h in both:
+            for c in (0, 1):
+                here = line(t, c, -s, h)
+                arrived(here, ar2.at[t.index, c, 2 + h])
+                start(t.sent, here, here, as2.at[t.index, c, 4 + h], ar2.at[t.index, c, 4 + h], peer(1 - c, s))
+                hand(t, c, 1, -s, h)
 
     def hand_over(t):
         for p, off in ((3, s), (2, 2)):
-            for c in (0, 1):
-                arrived(line(t, c, off), ar2.at[t.index, c, p])
-                hand(t, c, p, off)
+            for h in both:
+                for c in (0, 1):
+                    arrived(line(t, c, off, h), ar2.at[t.index, c, 2 * p + h])
+                    hand(t, c, p, off, h)
         if t is A:
             for p in (1, 2, 3):
                 arrived(sm.at[:, y], sr2.at[p])
 
     def finish(t):
         for p in (0, 1, 3, 2):
-            for c in (0, 1):
-                arrived(line(t, c, 0), cr.at[t.index, c, p])
-
-    def plane(off):
+            for h in both:
+                for c in (0, 1):
+                    arrived(line(t, c, 0, h), cr.at[t.index, c, 2 * p + h])
+
+    def plane(off, h):
         there = turn(2, off)
-        return w.at[12:16, :, lax.rem(there, 2) * 2 + there // 2, :, lanes]
+        return w.at[pl.ds(12 + 2 * h, 2), :, lax.rem(there, 2) * 2 + there // 2, :, lanes]
+
+    def plane_hand(p, off, h):
+        start(C2.sent, plane(off, h), plane(off, h), cs.at[3, 0, 2 * p + h], cr.at[3, 0, 2 * p + h], partner)
 
     def c2_first():
         arrived(c2buf.at[0], dr.at[3, 0])
@@ -320,26 +334,29 @@
     def c2_third():
         for o in (1, 2, 3):
             arrived(w.at[12:16, y, qm, :, lanes], ar1.at[3, 1, o])
-        here = plane(0)
         for p, off in ((1, s), (3, -s)):
-            start(C2.sent, here, here, as2.at[3, 0, p], ar2.at[3, 0, p], peer(2, off))
-        start(C2.sent, here, here, cs.at[3, 0, 0], cr.at[3, 0, 0], partner)
+            for h in both:
+                start(C2.sent, plane(0, h), plane(0, h), as2.at[3, 0, 2 * p + h], ar2.at[3, 0, 2 * p + h], peer(2, off))
+        for h in both:
+            plane_hand(0, 0, h)
 
     def c2_relay():
-        here = plane(-s)
-        arrived(here, ar2.at[3, 0, 1])
-        start(C2.sent, here, here, as2.at[3, 0, 2], ar2.at[3, 0, 2], peer(2, s))
-        start(C2.sent, here, here, cs.at[3, 0, 1], cr.at[3, 0, 1], partner)
+        for h in both:
+            here = plane(-s, h)
+            arrived(here, ar2.at[3, 0, 2 + h])
+            start(C2.sent, here, here, as2.at[3, 0, 4 + h], ar2.at[3, 0, 4 + h], peer(2, s))
+            plane_hand(1, -s, h)
 
     def c2_hand():
         for p, off in ((3, s), (2, 2)):
-            here = plane(off)
-            arrived(here, ar2.at[3, 0, p])
-            start(C2.sent, here, here, cs.at[3, 0, p], cr.at[3, 0, p], partner)
+            for h in both:
+                arrived(plane(off, h), ar2.at[3, 0, 2 * p + h])
+                plane_hand(p, off, h)
 
     def c2_finish():
         for p in range(4):
-            arrived(plane(0), cr.at[3, 0, p])
+            for h in both:
+                arrived(plane(0, h), cr.at[3, 0, 2 * p + h])
 
     block = hi * 2 + core
     pairs = ((tok_in, tok), (enc_in, enc))
@@ -387,18 +404,39 @@
             for i in (0, 1):
                 arrived(og.at[0], er.at[4 + i])
 
+    def out_piece(t, i):
+        if t is C2:
+            src = w.at[12 + i, :, :, :, lanes_other]
+        else:
+            src = w.at[t.out + 2 * other + i // 2, :, :, :, halves[i % 2]]
+        return remote(src, db.at[t.slot, i], bds.at[t.index, i], bdr.at[t.index, i], partner)
+
     def out_start(t):
         for i in range(4):
-            src = w.at[12 + i, :, :, :, lanes_other] if t is C2 else w.at[t.out + 2 * other + i // 2, :, :, :, halves[i % 2]]
-            start(t.sent, src, db.at[t.slot, i], bds.at[t.index, i], bdr.at[t.index, i], partner)
-
-    def out_line(t, c, off):
+            c = out_piece(t, i)
+            c.start()
+            t.sent.append(c)
+
+    def out_early(i):
+        c = out_piece(C2, i)
+        c.start()
+        C2.sent.append(c)
+        pieces = [out_piece(C1, 2 * (i % 2) + h) for h in both]
+
+        @pl.when(other == i // 2)
+        def _():
+            for c in pieces:
+                c.start()
+        if i < 2:
+            C1.sent.extend(pieces)
+
+    def out_line(t, c, off, at):
         if t is C2:
             there = turn(2, off)
-            return db.at[t.slot, :, :, lax.rem(there, 2) * 2 + there // 2]
+            return db.at[t.slot, at, :, lax.rem(there, 2) * 2 + there // 2]
         if c == 0:
-            return db.at[t.slot, 0:2, :, turn(1, off)]
-        return db.at[t.slot, 2:4, turn(0, off)]
+            return db.at[t.slot, 0:2, at, turn(1, off)]
+        return db.at[t.slot, 2:4, turn(0, off), at]
 
     def out_axis(t, c):
         return 2 if t is C2 else 1 - c
@@ -406,18 +444,24 @@
     def out_colors(t):
         return (0,) if t is C2 else (0, 1)
 
-    def out_slot(t, c, p):
-        return r1.at[t.slot, p] if t is C2 else r1.at[t.slot, p, 2 * c:2 * c + 2]
+    def out_slot(t, c, p, at):
+        return r1.at[t.slot, p, at] if t is C2 else r1.at[t.slot, p, 2 * c:2 * c + 2, at]
+
+    parts = (pl.ds(0, 2), pl.ds(2, 2))
+    whole = pl.ds(0, 4)
 
     def add_into(to, *terms):
         n = to.shape[0]
 
         @pl.loop(0, n)
         def _(i):
-            total = to[i].astype(f32)
-            for term in terms:
-                total = total + term[i].astype(f32)
-            to[i] = total.astype(bf)
+            if len(terms) == 1:
+                to[i] = to[i] + terms[0][i]
+            else:
+                total = to[i].astype(f32)
+                for term in terms:
+                    total = total + term[i].astype(f32)
+                to[i] = total.astype(bf)
 
     def out_first(t):
         for i in range(4):
@@ -430,37 +474,49 @@
                 continue
             c = 0 if t is C2 else i // 2
             for p, off, to in ((0, 2, s), (1, -s, -s)):
-                start(t.back, out_line(t, c, off), out_slot(t, c, p), b1s.at[t.index, c, p], b1r.at[t.index, c, p],
-                      peer(out_axis(t, c), to))
+                for h, at in enumerate(parts):
+                    start(t.back, out_line(t, c, off, at), out_slot(t, c, p, at), b1s.at[t.index, c, 2 * p + h],
+                          b1r.at[t.index, c, 2 * p + h], peer(out_axis(t, c), to))
 
     def out_second(t):
-        for c in out_colors(t):
-            arrived(out_slot(t, c, 0), b1r.at[t.index, c, 0])
-            here = out_line(t, c, s)
-            add_into(here, out_slot(t, c, 0))
-            start(t.back, here, out_slot(t, c, 2), b1s.at[t.index, c, 2], b1r.at[t.index, c, 2], peer(out_axis(t, c), s))
+        for h, at in enumerate(parts):
+            for c in out_colors(t):
+                arrived(out_slot(t, c, 0, at), b1r.at[t.index, c, h])
+                here = out_line(t, c, s, at)
+                add_into(here, out_slot(t, c, 0, at))
+                start(t.back, here, out_slot(t, c, 2, at), b1s.at[t.index, c, 4 + h], b1r.at[t.index, c, 4 + h],
+                      peer(out_axis(t, c), s))
 
     def out_third(t):
         for c in out_colors(t):
             for p in (1, 2):
-                arrived(out_slot(t, c, p), b1r.at[t.index, c, p])
-            add_into(out_line(t, c, 0), out_slot(t, c, 1), out_slot(t, c, 2))
+                for h, at in enumerate(parts):
+                    arrived(out_slot(t, c, p, at), b1r.at[t.index, c, 2 * p + h])
+            if t is C2:
+                @pl.loop(0, 4)
+                def _(i):
+                    total = db[t.slot, i, :, qm].astype(f32)
+                    for p in (1, 2):
+                        total = total + r1[t.slot, p, i].astype(f32)
+                    ptot[i] = total.astype(bf)
+            else:
+                add_into(out_line(t, c, 0, whole), out_slot(t, c, 1, whole), out_slot(t, c, 2, whole))
             for o in (1, 3, 2):
                 if t is C2:
-                    src, dst, to = db.at[t.slot, :, turn(1, o), qm], r2.at[t.slot, o - 1], yp[o]
+                    src, dst, to, sent = ptot.at[:, turn(1, o)], r2a.at[o - 1], yp[o], t.late
                 elif c == 0:
-                    src, dst, to = db.at[t.slot, 0:2, turn(0, o), y], r2.at[t.slot, o - 1, 0:2], xp[o]
+                    src, dst, to, sent = db.at[t.slot, 0:2, turn(0, o), y], r2.at[t.slot, o - 1, 0:2], xp[o], t.back
                 else:
-                    src, dst, to = db.at[t.slot, 2:4, x, turn(1, o)], r2.at[t.slot, o - 1, 2:4], yp[o]
-                start(t.back, src, dst, b2s.at[t.index, c, o - 1], b2r.at[t.index, c, o - 1], to)
+                    src, dst, to, sent = db.at[t.slot, 2:4, x, turn(1, o)], r2.at[t.slot, o - 1, 2:4], yp[o], t.back
+                start(sent, src, dst, b2s.at[t.index, c, o - 1], b2r.at[t.index, c, o - 1], to)
 
     def out_fourth(t):
         if t is C2:
             for o in (0, 1, 2):
-                arrived(r2.at[t.slot, o], b2r.at[3, 0, o])
-            add_into(db.at[t.slot, :, y, qm], *[r2.at[t.slot, o] for o in (0, 1, 2)])
+                arrived(r2a.at[o], b2r.at[3, 0, o])
+            add_into(ptot.at[:, y], *[r2a.at[o] for o in (0, 1, 2)])
             for o in (1, 3, 2):
-                start(t.back, db.at[t.slot, turn(0, o), y, qm], r2b.at[o - 1], b2s.at[3, 1, o - 1], b2r.at[3, 1, o - 1], xp[o])
+                start(t.late, ptot.at[turn(0, o), y], r2b.at[o - 1], b2s.at[3, 1, o - 1], b2r.at[3, 1, o - 1], xp[o])
             return
         for c in (0, 1):
             for o in (0, 1, 2):
@@ -472,18 +528,18 @@
                 red[c, :, h * HALF:(h + 1) * HALF] = total.astype(bf)
         shares[t.index] = dot(split_matrix(), red[...].reshape(96, D)).astype(bf).reshape(8, 16, D)
         for o in (1, 3, 2):
-            start(t.back, shares.at[t.index, pl.ds(member(turn(2, o), 0), 2)], r3.at[t.index, o - 1], b3s.at[t.index, o - 1],
+            start(t.late, shares.at[t.index, pl.ds(member(turn(2, o), 0), 2)], r3.at[t.index, o - 1], b3s.at[t.index, o - 1],
                   b3r.at[t.index, o - 1], zp[o])
 
     def out_fifth(t):
         if t is C2:
             for o in (0, 1, 2):
                 arrived(r2b.at[o], b2r.at[3, 1, o])
-            total = db[t.slot, x, y, qm].astype(f32)
+            total = ptot[x, y].astype(f32)
             for o in (0, 1, 2):
                 total = total + r2b[o].astype(f32)
             c2sum[core] = total.astype(bf)
-            start(t.back, c2sum.at[core], c2sum.at[core], b4s.at[3], b4r.at[3], partner)
+            start(t.late, c2sum.at[core], c2sum.at[core], b4s.at[3], b4r.at[3], partner)
             return
         for o in (0, 1, 2):
             arrived(r3.at[t.index, o], b3r.at[t.index, o])
@@ -496,7 +552,7 @@
             return total
         fin[t.index, core] = share(core)
         sx[t.index] = share(other).astype(bf)
-        start(t.back, sx.at[t.index], r4.at[t.index], b4s.at[t.index], b4r.at[t.index], partner)
+        start(t.late, sx.at[t.index], r4.at[t.index], b4s.at[t.index], b4r.at[t.index], partner)
 
     def out_last(t):
         if t is C2:
@@ -526,27 +582,41 @@
             @pl.loop(0, buf.shape[1] // 16)
             def _(a):
                 at = pl.ds(pl.multiple_of(a * 16, 16), 16)
-                src[2 * n + core, at] = (src[2 * n + core, at].astype(f32) + buf[n, at].astype(f32)).astype(bf)
+                src[2 * n + core, at] = src[2 * n + core, at] + buf[n, at]
         start(moved, src.at[2 * (1 - hi) + core], out.at[hi], ts.at[2, i], tr.at[2, i], home)
         return local(src.at[2 * hi + core], out.at[hi], ls.at[4 + i])
+
+    def result_copies():
+        stays = pltpu.make_async_copy(BO.at[core], bo_out.at[hi], ls.at[3])
+        passed = remote(BO.at[other], bo_out.at[hi], os_.at[0], tr.at[3, 0], partner)
+        crossed = [remote(BO.at[n], bo_out.at[hi], os_.at[n], tr.at[3, 1], device_at(x, y, across, n)) for n in (0, 1)]
+        return stays, passed, crossed
 
     def result_start():
         @pl.when(core == hi)
         def _():
-            c = pltpu.make_async_copy(BO.at[core], bo_out.at[hi], ls.at[3])
-            c.start()
-            d = remote(BO.at[other], bo_out.at[hi], os_.at[0], tr.at[3, 0], partner)
-            d.start()
-            c.wait()
-            d.wait_send()
+            stays, passed, _ = result_copies()
+            stays.start()
+            passed.start()
 
         @pl.when(core != hi)
         def _():
-            copies = [remote(BO.at[n], bo_out.at[hi], os_.at[n], tr.at[3, 1], device_at(x, y, across, n)) for n in (0, 1)]
-            for c in copies:
+            for c in result_copies()[2]:
                 c.start()
-            for c in copies:
+
+    def result_done():
+        @pl.when(core == hi)
+        def _():
+            stays, passed, _ = result_copies()
+            stays.wait()
+            passed.wait_send()
+
+        @pl.when(core != hi)
+        def _():
+            for c in result_copies()[2]:
                 c.wait_send()
+            arrived(bo_out.at[0], tr.at[3, 0])
+        arrived(bo_out.at[0], tr.at[3, 1])
 
     def weight(u):
         return w[u].reshape(D, D)
@@ -573,6 +643,21 @@
     acc[1, 0:24] = sh2[...].astype(f32)
     zbuf[me] = acc[0, 0:96].astype(bf)
     c2buf[core] = acc[1, 0:32].astype(bf)
+    pl.semaphore_wait(barrier, len(peers))
+    z_start(A)
+    start(C2.sent, c2buf.at[core], c2buf.at[core], ds.at[3, 0], dr.at[3, 0], partner)
+    z_start(B)
+    z_start(C1)
+    input_start(0)
+    input_start(1)
+    c2_first()
+    z_mid(A)
+    spread(A)
+    xy1(A)
+    c2_second()
+    z_mid(B)
+    spread(B)
+    xy1(B)
     krow = seg2[pl.ds(hi, 1)]
     crow = clip2[pl.ds(hi, 1)]
     ids = jnp.broadcast_to(krow, (8, KEYS)).astype(f32).T[:, 0:1].astype(jnp.int32)
@@ -580,29 +665,15 @@
     key_at = lax.broadcasted_iota(jnp.int32, (SPAN, KEYS), 1)
     query_at = lax.broadcasted_iota(jnp.int32, (SPAN, KEYS), 0) + core * SPAN
     bias_s[...] = jnp.where((qcol == krow) & (key_at <= query_at), 0.0, BLOCKED)
-    bias_c[...] = jnp.where(qcol == crow, 0.0, BLOCKED)
-    pl.semaphore_wait(barrier, len(peers))
-    z_start(A)
-    z_start(B)
-    z_start(C1)
-    start(C2.sent, c2buf.at[core], c2buf.at[core], ds.at[3, 0], dr.at[3, 0], partner)
-    input_start(0)
-    z_mid(A)
-    spread(A)
-    xy1(A)
-    c2_first()
-    z_mid(B)
-    spread(B)
-    xy1(B)
-    input_start(1)
+    bias_c[...] = jnp.where(qcol == crow, 0.0, BLOCKED).astype(bf)
     xy2(A)
     z_mid(C1)
     spread(C1)
     input_forward(0)
     relay(A)
     xy2(B)
-    c2_second()
     xy1(C1)
+    c2_third()
     input_ready(0)
     hand_over(A)
 
@@ -617,7 +688,6 @@
     def _(i):
         n, _ = normed(tok[i].astype(f32))
         first[pl.ds(pl.multiple_of(i * 112, 16), 112)] = (n * vec[0:1] + vec[1:2]).astype(bf)
-    c2_third()
     grad_start()
     finish(A)
 
@@ -633,8 +703,8 @@
     q[...] = (dot(first[mine], weight(0)) + vec[2:3]).astype(bf) * SCALE
     hand_over(B)
     attend(q, k, v, bias_s, mixed, lse, 0, 3)
+    relay(C1)
     input_forward(1)
-    relay(C1)
     attend(q, k, v, bias_s, mixed, lse, 3, 6)
     after_self[...] = tok[pl.ds(2 * core, 2)].reshape(SPAN, D).astype(f32) + dot(mixed[...], weight(3)) + vec[4:5]
     n, r = normed(after_self[...])
@@ -680,8 +750,7 @@
         ghib[i:i + 1] = row_sum(g_pre.astype(f32))
         acc[1] += dot_back(g_pre, weight(8 + i))
         weight_grad(8 + i, third, wide.at[1])
-    out_start(C2)
-    out_start(C1)
+        out_early(i)
     BO[...] = acc[0].astype(bf).reshape(2, 112, D)
     e = acc[1]
     ogf = g[...].astype(f32)
@@ -707,22 +776,13 @@
     out_second(C2)
     attend_back(cq, ck, cv, bias_c, cmixed, clse, g, gq, ck, cv, 4, 6)
     out_fourth(C1)
+    give_credit(C1)
     weight_grad(13, enc, ck)
-    out_third(C2)
     weight_grad(14, enc, cv)
-    out_fifth(C1)
     weight_grad(12, second, gq)
-    give_credit(C1)
     take_credit(B)
     out_start(B)
-
-    @pl.loop(0, 4)
-    def _(i):
-        at = pl.ds(pl.multiple_of(i * 384, 128), 384)
-        enc[i] = (dot_back(ck[at], weight(5)) + dot_back(cv[at], weight(6))).astype(bf)
-    home_start(1, enc, eib)
-    out_first(B)
-    out_fourth(C2)
+    out_third(C2)
     e = dot_back(gq[...], weight(4))
     gvec[7:8] = row_sum(gq[...].astype(f32))
     gvec[8:9] = row_sum(cv[...].astype(f32))
@@ -730,22 +790,31 @@
     gvec[5:6] = row_sum(e * n)
     gvec[6:7] = row_sum(e)
     stream[...] += norm_back(e, n, r, vec[5:6])
+    out_first(B)
+    give_credit(C2)
     wide[0] = stream[...].astype(bf)
     gvec[4:5] = row_sum(wide[0].astype(f32))
     g[...] = dot_back(wide[0], weight(3)).astype(bf)
-    ends = [home_sum(1, enc, eib, ep_out)]
     weight_grad(11, mixed, wide.at[0])
-    out_fifth(C2)
+    attend_back(q, k, v, bias_s, mixed, lse, g, gq, k, v, 0, 6)
     out_second(B)
-    attend_back(q, k, v, bias_s, mixed, lse, g, gq, k, v, 0, 6)
-    give_credit(C2)
-    out_third(B)
     wide[0] = first[mine]
     weight_grad(8, wide.at[0], gq)
     weight_grad(9, first, k)
     weight_grad(10, first, v)
     take_credit(A)
     out_start(A)
+    out_third(B)
+
+    @pl.loop(0, 4)
+    def _(i):
+        at = pl.ds(pl.multiple_of(i * 384, 128), 384)
+        enc[i] = (dot_back(ck[at], weight(5)) + dot_back(cv[at], weight(6))).astype(bf)
+    home_start(1, enc, eib)
+    out_first(A)
+    out_fourth(B)
+    out_fourth(C2)
+    ends = [home_sum(1, enc, eib, ep_out)]
     gvec[2:3] = row_sum(gq[...].astype(f32))
     gvec[3:4] = row_sum(v[...].astype(f32))
     gvec[0:2] = jnp.zeros((2, D), f32)
@@ -758,10 +827,8 @@
         gvec[0:1] += row_sum(e * n)
         gvec[1:2] += row_sum(e)
         PI[2 * h:2 * h + 2] = (norm_back(e, n, r, vec[0:1]) + jnp.where(is_own, stream[...], 0.0)).astype(bf).reshape(2, 112, D)
-        if h == 0:
-            out_first(A)
     home_start(0, PI, pib)
-    out_fourth(B)
+    out_second(A)
     owner, inner, which = vector_tables()
     spread_out = lax.dot_general(gvec[...].astype(bf), which, (((0,), (0,)), ((), ())), preferred_element_type=f32)
     total = dot_grad(owner, (spread_out * inner).astype(bf))
@@ -772,14 +839,15 @@
     SG[...] = total.reshape(4, 4, 8, 128)
     swap = remote(SG, sd, gss.at[0], gsr.at[0], partner)
     swap.start()
-    out_second(A)
     swap.wait()
     SG[...] = SG[...] + sd[...]
     for p in (1, 2, 3):
         start(moved, SG.at[:, turn(1, p)], s1b.at[p], gss.at[p], gsr.at[p], yp[p])
     ends.append(home_sum(0, PI, pib, pi_out))
+    out_third(A)
+    out_fifth(C2)
+    out_fifth(C1)
     out_fifth(B)
-    out_third(A)
     total = SG[:, y]
     for p in (1, 2, 3):
         arrived(s1b.at[p], gsr.at[p])
@@ -787,9 +855,6 @@
     SG[:, y] = total
     for b in (1, 2, 3):
         start(moved, SG.at[turn(0, b), y], s2b.at[b], gss.at[3 + b], gsr.at[3 + b], xp[b])
-    out_last(C2)
-    out_last(C1)
-    out_last(B)
     out_fourth(A)
     total = SG[x, y]
     for b in (1, 2, 3):
@@ -798,6 +863,9 @@
     s3b[0] = total
     for o in (1, 2, 3):
         start(moved, s3b.at[0], s3b.at[o], gss.at[6 + o], gsr.at[6 + o], zp[o])
+    out_last(C2)
+    out_last(C1)
+    out_last(B)
     out_fifth(A)
     total = s3b[0]
     for o in (1, 2, 3):
@@ -808,16 +876,14 @@
     arrived(ep_out.at[0], tr.at[2, 1])
     arrived(pi_out.at[0], tr.at[2, 0])
 
-    @pl.when(core != hi)
-    def _():
-        arrived(bo_out.at[0], tr.at[3, 0])
-    arrived(bo_out.at[0], tr.at[3, 1])
+    result_done()
     out_last(A)
     for c in ends:
         c.wait()
     for t in (A, B, C1, C2):
         sends_done(t.sent)
         sends_done(t.back)
+        sends_done(t.late)
     sends_done(moved)
 
 
@@ -834,27 +900,34 @@
             V((16, D), f32), V((8, D), f32), V((KEYS, D), bf), V((SPAN, D), bf), V((KEYS, D), bf), V((KEYS, D), bf),
             V((SPAN, D), bf), V((6, SPAN, 128), f32), V((SPAN, D), bf), V((SPAN, D), bf), V((FRAMES, D), bf), V((FRAMES, D), bf),
             V((SPAN, D), bf), V((6, SPAN, 128), f32), V((SPAN, D), f32), V((SPAN, D), f32), V((SPAN, D), bf),
-            V((2, SPAN, D), f32), V((SPAN, KEYS), f32), V((SPAN, FRAMES), f32), V((SPAN, D), bf), V((SPAN, D), bf),
+            V((2, SPAN, D), f32), V((SPAN, KEYS), f32), V((SPAN, FRAMES), bf), V((SPAN, D), bf), V((SPAN, D), bf),
             V((2, SPAN, D), bf), V((16, D), f32), V((8, D), f32),
             V((2, 112, D), bf), V((4, 112, D), bf), V((2, 112, D), bf), V((2, 384, D), bf),
-            V((2, 4, 4, 4, 48, HALF), bf), V((2, 3, 4, 4, 48, HALF), bf), V((2, 3, 4, 48, HALF), bf), V((3, 48, HALF), bf),
+            V((2, 4, 4, 4, 48, HALF), bf), V((2, 3, 4, 4, 48, HALF), bf), V((2, 3, 4, 48, HALF), bf), V((3, 4, 48, HALF), bf), V((3, 48, HALF), bf), V((4, 4, 48, HALF), bf),
             V((2, 48, D), bf), V((3, 8, 16, D), bf), V((3, 3, 2, 16, D), bf), V((3, 16, D), bf), V((3, 16, D), bf),
             V((2, 48, HALF), bf), V((16, 128), f32),
             V((4, 4, 8, 128), f32), V((4, 4, 8, 128), f32), V((4, 4, 8, 128), f32), V((4, 8, 128), f32), V((4, 8, 128), f32),
-            DMA((16,)), DMA((4, 4)), DMA((4, 4)), DMA((4, 4)), DMA((4, 4)), DMA((4, 2, 4)), DMA((4, 2, 4)), DMA((4, 2, 4)), DMA((4, 2, 4)),
-            DMA((4, 2, 4)), DMA((4, 2, 4)), DMA((4,)), DMA((4,)), DMA((4,)), DMA((4,)), DMA((6,)), DMA((7,)), DMA((2,)), DMA((2,)),
-            DMA((4, 4)), DMA((4, 4)), DMA((4, 2, 3)), DMA((4, 2, 3)), DMA((4, 2, 3)), DMA((4, 2, 3)), DMA((3, 3)), DMA((3, 3)),
+            DMA((16,)), DMA((4, 4)), DMA((4, 4)), DMA((4, 4)), DMA((4, 4)), DMA((4, 2, 4)), DMA((4, 2, 4)), DMA((4, 2, 8)), DMA((4, 2, 8)),
+            DMA((4, 2, 8)), DMA((4, 2, 8)), DMA((4,)), DMA((4,)), DMA((4,)), DMA((4,)), DMA((6,)), DMA((7,)), DMA((2,)), DMA((2,)),
+            DMA((4, 4)), DMA((4, 4)), DMA((4, 2, 6)), DMA((4, 2, 6)), DMA((4, 2, 3)), DMA((4, 2, 3)), DMA((3, 3)), DMA((3, 3)),
             DMA((4,)), DMA((4,)), DMA((10,)), DMA((10,)), DMA((3, 2)), DMA((4, 2)), DMA((2,)), pltpu.SemaphoreType.REGULAR((2,))],
         compiler_params=pltpu.CompilerParams(collective_id=0, has_side_effects=True, vmem_limit_bytes=63 << 20),
         name="layer",
     )(*operands)
 
 
-def unpack_kernel(fin, fin2, bo, pi, ep, *outs):
+def unpack_kernel(*refs):
+    ins, outs, (fin, fin2, bo, pi, ep, sems) = refs[:5], refs[5:18], refs[18:]
+    copies = [pltpu.make_async_copy(src, dst, sems.at[i]) for i, (src, dst) in enumerate(zip(ins, (fin, fin2, bo, pi, ep)))]
+    for c in copies:
+        c.start()
+    for c in copies:
+        c.wait()
     out, gi, ge, mats, h_in, h_out = outs[0], outs[1], outs[2], outs[3:11], outs[11], outs[12]
     out[...] = bo[...][:, None]
     gi[...] = pi[...].astype(f32)[:, None]
-    ge[...] = ep[:, :375].astype(f32)[:, None]
+    for micro in (0, 1):
+        ge[micro, :, 0, :] = ep[micro, :375].astype(f32)
     for i in range(4):
         mats[i][...] = fin[0, i // 2, 6 * (i % 2):6 * (i % 2) + 6]
         mats[4 + i][...] = fin[1, i // 2, 6 * (i % 2):6 * (i % 2) + 6]
@@ -863,11 +936,15 @@
 
 
 def unpack(fin, fin2, bo, pi, ep):
-    S = jax.ShapeDtypeStruct
+    S, V, hbm = jax.ShapeDtypeStruct, pltpu.VMEM, pl.BlockSpec(memory_space=pl.ANY)
     return pl.pallas_call(
         unpack_kernel,
-        out_shape=[S((2, 1, 112, D), bf), S((2, 1, 112, D), f32), S((2, 1, 375, D), f32)] + [S((6, D), f32)] * 8 + [S((6, 4 * D), f32), S((24, D), f32)],
-        compiler_params=pltpu.CompilerParams(vmem_limit_bytes=32 << 20),
+        out_shape=[S((2, 1, 112, D), bf), S((2, 1, 112, D), f32), S((2, 375, 1, D), f32)] + [S((6, D), f32)] * 8
+        + [S((6, 4 * D), f32), S((24, D), f32)],
+        in_specs=[hbm] * 5,
+        scratch_shapes=[V((3, 2, 16, D), f32), V((24, D), f32), V((2, 112, D), bf), V((2, 112, D), bf), V((2, 384, D), bf),
+                        pltpu.SemaphoreType.DMA((5,))],
+        compiler_params=pltpu.CompilerParams(vmem_limit_bytes=60 << 20),
         name="unpack",
     )(fin, fin2, bo, pi, ep)
 
@@ -892,7 +969,7 @@
         small, tokens[:, 0], frames, out_grad[:, 0], segments[:, 0], clip)
     out, gi, ge, *m = unpack(fin, fin2, bo, pi, ep)
     gv = [gs[0, 6 * i:6 * i + 6] for i in range(13)]
-    return (out, gi, ge,
+    return (out, gi, ge.transpose(0, 2, 1, 3),
             gv[0], gv[1], m[0], gv[2], m[1], m[2], gv[3], m[3], gv[4],
             gv[5], gv[6], m[4], gv[7], m[5], m[6], gv[8], m[7], gv[9],
             gv[10], gv[11], m[8], gs[0, 78:102], m[9], gv[12])

time: 229 us -> 195 us (0.85)
  the two profiles are of different devices: /device:TPU:1 before, /device:TPU:0 now
where the time goes in v4:
time: 195 us; the launch traced here: 191 us
  Pallas kernels  184 us (94%)
  local copies, waits for them, and re-layouts  5.69 us (3%)
    pallas_call x1, Pallas kernels, layer(): pl.pallas_call(layer_kernel, out_shape=[S((3, 2, 16, D), f32), S((24, D),...  181 us

profile of v4, /device:TPU:0, one launch (start us, length us, event | category | flops | bytes accessed | tf_op | source)
XLA Modules:
  0.0 191.1 jit_solution(12733809777856376630)
XLA Ops:
  0.7 1.4 copy.56
  2.0 0.0 copy-start
  2.1 0.0 copy-start.3
  2.1 0.0 copy-start.4
  2.1 0.0 copy-start.5
  2.1 0.0 copy-start.6
  2.1 0.0 copy-start.7
  2.1 0.0 copy-start.8
  2.1 0.0 copy-start.9
  2.1 0.0 copy-start.10
  2.2 0.0 copy-start.11
  2.2 0.0 copy-start.14
  2.2 0.0 copy-start.15
  2.2 0.0 copy-start.2
  2.2 1.1 pad_bitcast_fusion.enc_in
  3.4 0.1 reshape.65
  3.5 0.6 copy.58
  4.2 0.1 convert_add_fusion
  4.3 0.6 broadcast_in_dim.2.small
  4.9 0.6 copy.60
  5.5 180.5 %layer.1 = (f32[3,2,16,768]{3,2,1,0:T(8,128)}, f32[24,768]{1,0:T(8,128)}, f32[8,128]{1,0:T(8,128)}, bf16[2,112,768]{2,1,0:T(8,128)(2,1)}, bf16[2,112,768]{2,1,0:T(8,128)(2,1)}, /*index=5*/bf16[2,384,768]{2,1,0:T(8,128)(2,1)}) custom-call(bf16[6,768]{1,0:T(8,128)(2,1)} %m0.1, bf16[6,768]{1,0:T(8,128)(2,1)} %m1.1, bf16[6,768]{1,0:T(8,128)(2,1)} %m2.1, ...), custom_call_target="tpu_custom_call" | custom-call | tf_op jit(solution)/shard_map/layer/pallas_call | solution.py:893
  186.0 3.6 %unpack.1 = (bf16[2,1,112,768]{3,2,1,0:T(8,128)(2,1)}, f32[2,1,112,768]{3,2,1,0:T(8,128)}, f32[2,375,1,768]{3,2,1,0:T(1,128)}, f32[6,768]{1,0:T(8,128)}, f32[6,7...) custom-call(f32[3,2,16,768]{3,2,1,0:T(8,128)} %get-tuple-element.46., ...), custom_call_target="tpu_custom_call" | custom-call | tf_op jit(solution)/shard_map/unpack/pallas_call | solution.py:940
  189.7 0.6 slice_bitcast_fusion
  190.3 0.6 slice_bitcast_fusion.1
  (23 shorter events, 0.1 us)
Async XLA Ops:
  2.0 1.3 copy-start
  2.1 2.0 %copy-start.3 = (bf16[6]{0:T(256)(128)(2,1)S(1)}, bf16[6]{0:T(256)(128)(2,1)}, u32[]{:S(2)}) copy-start(bf16[6]{0:T(256)(128)(2,1)} %param.57) | copy-start | bytes 40
  2.1 2.0 %copy-start.4 = (bf16[6]{0:T(256)(128)(2,1)S(1)}, bf16[6]{0:T(256)(128)(2,1)}, u32[]{:S(2)}) copy-start(bf16[6]{0:T(256)(128)(2,1)} %param.53) | copy-start | bytes 40
  2.1 2.0 %copy-start.5 = (bf16[6]{0:T(256)(128)(2,1)S(1)}, bf16[6]{0:T(256)(128)(2,1)}, u32[]{:S(2)}) copy-start(bf16[6]{0:T(256)(128)(2,1)} %param.52) | copy-start | bytes 40
  2.1 2.0 %copy-start.6 = (bf16[6]{0:T(256)(128)(2,1)S(1)}, bf16[6]{0:T(256)(128)(2,1)}, u32[]{:S(2)}) copy-start(bf16[6]{0:T(256)(128)(2,1)} %param.51) | copy-start | bytes 40
  2.1 2.0 %copy-start.7 = (bf16[6]{0:T(256)(128)(2,1)S(1)}, bf16[6]{0:T(256)(128)(2,1)}, u32[]{:S(2)}) copy-start(bf16[6]{0:T(256)(128)(2,1)} %param.49) | copy-start | bytes 40
  2.1 2.0 %copy-start.8 = (bf16[6]{0:T(256)(128)(2,1)S(1)}, bf16[6]{0:T(256)(128)(2,1)}, u32[]{:S(2)}) copy-start(bf16[6]{0:T(256)(128)(2,1)} %param.46) | copy-start | bytes 40
  2.1 2.0 %copy-start.9 = (bf16[6]{0:T(256)(128)(2,1)S(1)}, bf16[6]{0:T(256)(128)(2,1)}, u32[]{:S(2)}) copy-start(bf16[6]{0:T(256)(128)(2,1)} %param.44) | copy-start | bytes 40
  2.1 2.0 %copy-start.10 = (bf16[6]{0:T(256)(128)(2,1)S(1)}, bf16[6]{0:T(256)(128)(2,1)}, u32[]{:S(2)}) copy-start(bf16[6]{0:T(256)(128)(2,1)} %param.43) | copy-start | bytes 40
  2.2 2.0 %copy-start.11 = (bf16[6]{0:T(256)(128)(2,1)S(1)}, bf16[6]{0:T(256)(128)(2,1)}, u32[]{:S(2)}) copy-start(bf16[6]{0:T(256)(128)(2,1)} %param.42) | copy-start | bytes 40
  2.2 2.0 %copy-start.12 = (bf16[6]{0:T(256)(128)(2,1)S(1)}, bf16[6]{0:T(256)(128)(2,1)}, u32[]{:S(2)}) copy-start(bf16[6]{0:T(256)(128)(2,1)} %param.40) | copy-start | bytes 40
  2.2 2.0 %copy-start.13 = (bf16[6]{0:T(256)(128)(2,1)S(1)}, bf16[6]{0:T(256)(128)(2,1)}, u32[]{:S(2)}) copy-start(bf16[6]{0:T(256)(128)(2,1)} %param.37) | copy-start | bytes 40
  2.2 2.0 %copy-start.14 = (bf16[6]{0:T(256)(128)(2,1)S(1)}, bf16[6]{0:T(256)(128)(2,1)}, u32[]{:S(2)}) copy-start(bf16[6]{0:T(256)(128)(2,1)} %param.35) | copy-start | bytes 40
  2.2 2.0 %copy-start.15 = (bf16[6]{0:T(256)(128)(2,1)S(1)}, bf16[6]{0:T(256)(128)(2,1)}, u32[]{:S(2)}) copy-start(bf16[6]{0:T(256)(128)(2,1)} %param.34) | copy-start | bytes 40
  2.2 2.0 %copy-start.16 = (bf16[24]{0:T(256)(128)(2,1)S(1)}, bf16[24]{0:T(256)(128)(2,1)}, u32[]{:S(2)}) copy-start(bf16[24]{0:T(256)(128)(2,1)} %param.55) | copy-start | bytes 148
  2.2 2.7 %copy-start.2 = (s32[2,1,448]{2,1,0:T(1,128)S(1)}, s32[2,1,448]{2,1,0:T(1,128)}, u32[]{:S(2)}) copy-start(s32[2,1,448]{2,1,0:T(1,128)} %param.31) | copy-start | bytes 10756
  186.0 3.7 %copy-start.1 = (f32[8,128]{1,0:T(8,128)S(1)}, f32[8,128]{1,0:T(8,128)}, u32[]{:S(2)}) copy-start(f32[8,128]{1,0:T(8,128)} %get-tuple-element.54) | copy-start | bytes 12292
